TPU v7x, 32 devices: a whole 2x2x4 slice. The times are simulated.
32 devices in a mesh: dp: 2 (over x), row: 4 (over z), col: 4 (over y, core).
Axes of the slice: x: 2, y: 2, z: 4, core: 2. Of those that a mesh axis runs over, the one named last changes fastest.
Arguments:
- layer_in: bfloat16 [768, 4096], P('row', ('dp', 'col')), may hold values from -6 to 6
- seq_lengths: int32 [8], P('dp'), may hold values from 1 to 512, as said below
- w_qkv: bfloat16 [768, 3, 768], P('row', None, 'col'), may hold values from -0.21875 to 0.21875
- q_bias: bfloat16 [768], P('col'), may hold values from -3 to 3
- v_bias: bfloat16 [768], P('col'), may hold values from -3 to 3
- w_out: bfloat16 [768, 768], P('col', 'row'), may hold values from -2.5 to 2.5
- b_out: bfloat16 [768], P('row'), may hold values from -2 to 2
- ln1_gain: bfloat16 [768], P('row'), may hold values from 0.099609375 to 1.8984375
- ln1_bias: bfloat16 [768], P('row'), may hold values from -2 to 2
- w_in: bfloat16 [768, 3072], P('row', 'col'), may hold values from -0.21875 to 0.21875
- b_in: bfloat16 [3072], P('col'), may hold values from -3 to 3
- w_back: bfloat16 [768, 3072], P('row', 'col'), may hold values from -0.109375 to 0.109375
- b_back: bfloat16 [768], P('row'), may hold values from -2 to 2
- ln2_gain: bfloat16 [768], P('row'), may hold values from 0.099609375 to 1.8984375
- ln2_bias: bfloat16 [768], P('row'), may hold values from -2 to 2
- out_grad: float32 [768, 4096], P('row', ('dp', 'col')), may hold values from -6 to 6
Outputs:
- layer_out: bfloat16 [768, 4096], P('row', ('dp', 'col'))
- in_grad: float32 [768, 4096], P('row', ('dp', 'col'))
- w_qkv_grad: float32 [768, 3, 768], P('row', None, 'col')
- q_bias_grad: float32 [768], P('col')
- v_bias_grad: float32 [768], P('col')
- w_out_grad: float32 [768, 768], P('col', 'row')
- b_out_grad: float32 [768], P('row')
- ln1_gain_grad: float32 [768], P('row')
- ln1_bias_grad: float32 [768], P('row')
- w_in_grad: float32 [768, 3072], P('row', 'col')
- b_in_grad: float32 [3072], P('col')
- w_back_grad: float32 [768, 3072], P('row', 'col')
- b_back_grad: float32 [768], P('row')
- ln2_gain_grad: float32 [768], P('row')
- ln2_bias_grad: float32 [768], P('row')
Inputs may be any that keep to these rules, and one draw needn't show every extreme that they name: `seq_lengths`: each replica's 4 * 1 slots (replicas one after another) hold at least one sequence of length 512.
All inputs are finite; a program needn't handle non-finite values.
Results may differ from a plain program's by a relative error of at most 0.015.
Values may be sent and summed in bfloat16 or wider, within the bound.
No kernel may reach another device: no remote copies, remote signals or barrier semaphores. Data moves between devices by JAX's collectives and lax.ppermute only.
A program may use at most 128 MiB of HBM per device.

v0:
```python
from functools import partial

import jax
import jax.numpy as jnp
from jax import lax
from jax.sharding import PartitionSpec as P

HEAD_DIM = 64
L = 512


EPSILON = 1e-12


def product(block_rows, weight_mat, flipped):
    if flipped:
        contract = ((1,), (1,))
    else:
        contract = ((1,), (0,))
    return lax.dot_general(
        block_rows, weight_mat, (contract, ((), ())), preferred_element_type=jnp.float32
    )


def outer_sum(left_rows, right_rows):
    return lax.dot_general(
        left_rows, right_rows, (((0,), (0,)), ((), ())), preferred_element_type=jnp.float32
    )


def spread_cols(activations, weight_mat, flipped):
    gathered = lax.all_gather(activations, "col", axis=0, tiled=True)
    row_share = gathered.shape[0] // lax.axis_size("row")

    def term(start_row, row_count):
        return product(
            lax.dynamic_slice_in_dim(gathered, start_row, row_count, 0), weight_mat, flipped
        )

    return (
        gathered,
        lax.psum_scatter(
            term(jnp.int32(0), row_share * lax.axis_size("row")),
            "row",
            scatter_dimension=0,
            tiled=True,
        ),
    )


def spread_rows(activations, weight_mat, flipped):
    gathered = lax.all_gather(activations, "row", axis=0, tiled=True)
    col_share = gathered.shape[0] // lax.axis_size("col")

    def term(start_row, row_count):
        return product(
            lax.dynamic_slice_in_dim(gathered, start_row, row_count, 0), weight_mat, flipped
        )

    return (
        gathered,
        lax.psum_scatter(
            term(jnp.int32(0), col_share * lax.axis_size("col")),
            "col",
            scatter_dimension=0,
            tiled=True,
        ),
    )


def row_totals(first_sum, second_sum):
    return lax.psum((first_sum, second_sum), "row")


def norm_forward(hidden, gain_row, shift_row, model_width):
    totals = row_totals(jnp.sum(hidden, axis=-1), jnp.sum(hidden * hidden, axis=-1))
    center = totals[0] / model_width
    spread = totals[1] / model_width - center * center
    inverse = lax.rsqrt(spread + EPSILON)
    scaled = (hidden - center[:, None]) * inverse[:, None]
    return (scaled, inverse, scaled * gain_row + shift_row)


def norm_backward(upstream, scaled, inverse, gain_row, model_width):
    weighted = upstream * gain_row
    totals = row_totals(jnp.sum(weighted, axis=-1), jnp.sum(weighted * scaled, axis=-1))
    return inverse[:, None] * (
        weighted - totals[0][:, None] / model_width - scaled * (totals[1][:, None] / model_width)
    )


def score_block(queries, keys_in, key_live):
    scores = jnp.einsum(
        "sqhd,skhd->shqk", queries, keys_in, preferred_element_type=jnp.float32
    ) * HEAD_DIM ** (-0.5)
    return jnp.where(key_live[:, None, None, :], scores, -1000000000.0)


def attention_forward(queries, keys_in, values, key_live):
    scores = score_block(queries, keys_in, key_live)
    row_peak = jnp.max(scores, axis=-1, keepdims=True)
    exponent = jnp.exp(scores - row_peak)
    denominator = jnp.sum(exponent, axis=-1, keepdims=True)
    weights = (exponent / denominator).astype(jnp.bfloat16)
    context = jnp.einsum("shqk,skhd->sqhd", weights, values, preferred_element_type=jnp.float32)
    return (context, row_peak + jnp.log(denominator))


def attention_backward(queries, keys_in, values, key_live, log_total, grad_context):
    score_scale = HEAD_DIM ** (-0.5)
    weights = jnp.exp(score_block(queries, keys_in, key_live) - log_total)
    grad_weights = jnp.einsum(
        "sqhd,skhd->shqk", grad_context, values, preferred_element_type=jnp.float32
    )
    inner = jnp.sum(weights * grad_weights, axis=-1, keepdims=True)
    grad_scores = (weights * (grad_weights - inner)).astype(jnp.bfloat16)
    grad_queries = (
        jnp.einsum("shqk,skhd->sqhd", grad_scores, keys_in, preferred_element_type=jnp.float32)
        * score_scale
    )
    grad_keys = (
        jnp.einsum("shqk,sqhd->skhd", grad_scores, queries, preferred_element_type=jnp.float32)
        * score_scale
    )
    grad_values = jnp.einsum(
        "shqk,sqhd->skhd",
        weights.astype(jnp.bfloat16),
        grad_context,
        preferred_element_type=jnp.float32,
    )
    return (grad_queries, grad_keys, grad_values)


def shards(
    layer_in,
    seq_lengths,
    w_qkv,
    q_bias,
    v_bias,
    w_out,
    b_out,
    ln1_gain,
    ln1_bias,
    w_in,
    b_in,
    w_back,
    b_back,
    ln2_gain,
    ln2_bias,
    out_grad,
):
    n_rows = lax.axis_size("row")
    layer_rows = layer_in.T
    grad_rows = out_grad.T
    tok_cols, feat_rows = layer_rows.shape
    feat_cols = w_out.shape[0]
    model_width = feat_rows * n_rows
    rep_tokens = tok_cols * lax.axis_size("col")
    tok_rows = rep_tokens // n_rows
    slot_count = tok_rows // L
    head_count = feat_cols // HEAD_DIM
    position = jnp.arange(rep_tokens, dtype=jnp.int32)
    slot_length = jnp.repeat(seq_lengths, L, total_repeat_length=rep_tokens)
    live_all = (position % L < slot_length).astype(jnp.float32)
    live_cols = lax.dynamic_slice_in_dim(live_all, lax.axis_index("col") * tok_cols, tok_cols)
    row_lengths = lax.dynamic_slice_in_dim(
        seq_lengths, lax.axis_index("row") * slot_count, slot_count
    )
    key_live = jnp.arange(L, dtype=jnp.int32)[None, :] < row_lengths[:, None]
    qkv_flat = w_qkv.reshape(feat_rows, 3 * feat_cols)
    input_all, qkv_part = spread_cols(layer_rows, qkv_flat, False)
    qkv_part = qkv_part.reshape(tok_rows, 3, feat_cols)
    head_shape = (slot_count, L, head_count, HEAD_DIM)
    queries = (qkv_part[:, 0] + q_bias.astype(jnp.float32)).astype(jnp.bfloat16).reshape(head_shape)
    keys_in = qkv_part[:, 1].astype(jnp.bfloat16).reshape(head_shape)
    values = (qkv_part[:, 2] + v_bias.astype(jnp.float32)).astype(jnp.bfloat16).reshape(head_shape)
    context, log_total = attention_forward(queries, keys_in, values, key_live)
    context_low = context.reshape(tok_rows, feat_cols).astype(jnp.bfloat16)
    context_all, attended = spread_rows(context_low, w_out, False)
    first_sum = layer_rows.astype(jnp.float32) + attended + b_out.astype(jnp.float32)
    gain_one = ln1_gain.astype(jnp.float32)
    scaled_one, inverse_one, normed = norm_forward(
        first_sum, gain_one, ln1_bias.astype(jnp.float32), model_width
    )
    normed_low = normed.astype(jnp.bfloat16)
    normed_all, hidden_pre = spread_cols(normed_low, w_in, False)
    hidden_pre = hidden_pre + b_in.astype(jnp.float32)
    gelu_exact = partial(jax.nn.gelu, approximate=False)
    hidden_low = gelu_exact(hidden_pre).astype(jnp.bfloat16)
    hidden_all, returned = spread_rows(hidden_low, w_back, True)
    second_sum = normed + returned + b_back.astype(jnp.float32)
    gain_two = ln2_gain.astype(jnp.float32)
    scaled_two, inverse_two, final_norm = norm_forward(
        second_sum, gain_two, ln2_bias.astype(jnp.float32), model_width
    )
    layer_out = (final_norm * live_cols[:, None]).astype(jnp.bfloat16)
    grad_norm_two = grad_rows * live_cols[:, None]
    ln2_gain_grad = jnp.sum(grad_norm_two * scaled_two, axis=0)
    ln2_bias_grad = jnp.sum(grad_norm_two, axis=0)
    grad_second = norm_backward(grad_norm_two, scaled_two, inverse_two, gain_two, model_width)
    grad_returned = grad_second.astype(jnp.bfloat16)
    returned_all, grad_hidden = spread_cols(grad_returned, w_back, False)
    w_back_grad = outer_sum(returned_all, hidden_all)
    b_back_grad = jnp.sum(returned_all, axis=0, dtype=jnp.float32)
    grad_pre = jax.vjp(gelu_exact, hidden_pre)[1](grad_hidden)[0].astype(jnp.bfloat16)
    pre_all, grad_from_ffn = spread_rows(grad_pre, w_in, True)
    w_in_grad = outer_sum(normed_all, pre_all)
    b_in_grad = jnp.sum(pre_all, axis=0, dtype=jnp.float32)
    grad_normed = grad_second + grad_from_ffn
    ln1_gain_grad = jnp.sum(grad_normed * scaled_one, axis=0)
    ln1_bias_grad = jnp.sum(grad_normed, axis=0)
    grad_first = norm_backward(grad_normed, scaled_one, inverse_one, gain_one, model_width)
    grad_attended = grad_first.astype(jnp.bfloat16)
    attended_all, grad_context = spread_cols(grad_attended, w_out, True)
    w_out_grad = outer_sum(context_all, attended_all)
    b_out_grad = jnp.sum(attended_all, axis=0, dtype=jnp.float32)
    grad_context_low = grad_context.astype(jnp.bfloat16).reshape(head_shape)
    grad_queries, grad_keys, grad_values = attention_backward(
        queries, keys_in, values, key_live, log_total, grad_context_low
    )
    grad_qkv = jnp.stack(
        (
            grad_queries.reshape(tok_rows, feat_cols),
            grad_keys.reshape(tok_rows, feat_cols),
            grad_values.reshape(tok_rows, feat_cols),
        ),
        axis=1,
    )
    grad_qkv = grad_qkv.astype(jnp.bfloat16).reshape(tok_rows, 3 * feat_cols)
    qkv_all, grad_from_qkv = spread_rows(grad_qkv, qkv_flat, True)
    w_qkv_grad = outer_sum(input_all, qkv_all).reshape(feat_rows, 3, feat_cols)
    qkv_column_sum = jnp.sum(qkv_all, axis=0, dtype=jnp.float32)
    q_bias_grad = qkv_column_sum[:feat_cols]
    v_bias_grad = qkv_column_sum[2 * feat_cols :]
    in_grad = grad_first + grad_from_qkv
    (
        w_qkv_grad,
        q_bias_grad,
        v_bias_grad,
        w_out_grad,
        b_out_grad,
        w_in_grad,
        b_in_grad,
        w_back_grad,
        b_back_grad,
    ) = (
        lax.psum(w_qkv_grad.astype(jnp.bfloat16), "dp").astype(jnp.float32),
        lax.psum(q_bias_grad.astype(jnp.bfloat16), "dp").astype(jnp.float32),
        lax.psum(v_bias_grad.astype(jnp.bfloat16), "dp").astype(jnp.float32),
        lax.psum(w_out_grad.astype(jnp.bfloat16), "dp").astype(jnp.float32),
        lax.psum(b_out_grad.astype(jnp.bfloat16), "dp").astype(jnp.float32),
        lax.psum(w_in_grad.astype(jnp.bfloat16), "dp").astype(jnp.float32),
        lax.psum(b_in_grad.astype(jnp.bfloat16), "dp").astype(jnp.float32),
        lax.psum(w_back_grad.astype(jnp.bfloat16), "dp").astype(jnp.float32),
        lax.psum(b_back_grad.astype(jnp.bfloat16), "dp").astype(jnp.float32),
    )
    ln1_gain_grad, ln1_bias_grad, ln2_gain_grad, ln2_bias_grad = lax.psum(
        (ln1_gain_grad, ln1_bias_grad, ln2_gain_grad, ln2_bias_grad), ("dp", "col")
    )
    return (
        layer_out.T,
        in_grad.T,
        w_qkv_grad,
        q_bias_grad,
        v_bias_grad,
        w_out_grad,
        b_out_grad,
        ln1_gain_grad,
        ln1_bias_grad,
        w_in_grad,
        b_in_grad,
        w_back_grad,
        b_back_grad,
        ln2_gain_grad,
        ln2_bias_grad,
    )


def solution(mesh):
    in_specs = (
        P("row", ("dp", "col")),
        P("dp"),
        P("row", None, "col"),
        P("col"),
        P("col"),
        P("col", "row"),
        P("row"),
        P("row"),
        P("row"),
        P("row", "col"),
        P("col"),
        P("row", "col"),
        P("row"),
        P("row"),
        P("row"),
        P("row", ("dp", "col")),
    )
    out_specs = (
        P("row", ("dp", "col")),
        P("row", ("dp", "col")),
        P("row", None, "col"),
        P("col"),
        P("col"),
        P("col", "row"),
        P("row"),
        P("row"),
        P("row"),
        P("row", "col"),
        P("col"),
        P("row", "col"),
        P("row"),
        P("row"),
        P("row"),
    )
    return jax.shard_map(shards, mesh=mesh, in_specs=in_specs, out_specs=out_specs, check_vma=False)
```

profile of v0, /device:TPU:20, one launch (start us, length us, event | category | flops | bytes accessed | tf_op | source)
XLA Modules:
  0.0 850.7 jit_solution(11451595379997520173)
XLA Ops:
  8.4 8.4 all_gather.24
  21.8 85.0 %reduce-scatter.9.cloned.1.call-done = f32[512,576]{0,1:T(8,128)} async-done(((f32[2048,576]{0,1:T(8,128)}), f32[512,576]{0,1:T(8,128)}) %reduce-scatter.9.cloned.1.call-update) | async-done | bytes 1179664 | tf_op jit(solution)/shard_map/reduce_scatter | solution.py:42
  111.2 17.0 %all_gather.25 = bf16[2048,192]{0,1:T(8,128)(2,1)S(1)} all-gather(bf16[512,192]{0,1:T(8,128)(2,1)S(1)} %bitcast.106), channel_id=1, replica_groups=mesh['dp'=2,'row'=4,'col'=4] {'row'}, dimensions={0}, use_global_device_ids=true | all-gather | bytes 983040 | tf_op jit(solution)/shard_map/all_gather | solution.py:52
  133.1 25.9 %reduce-scatter.11.cloned.1.call-done = f32[512,192]{0,1:T(8,128)} async-done(((f32[2048,192]{0,1:T(8,128)}), f32[512,192]{0,1:T(8,128)}) %reduce-scatter.11.cloned.1.call-update) | async-done | bytes 393232 | tf_op jit(solution)/shard_map/reduce_scatter | solution.py:62
  161.0 9.5 %all-reduce.4 = (f32[512]{0:T(512)}, f32[512]{0:T(512)}) all-reduce(f32[512]{0:T(512)S(1)} %get-tuple-element.52, f32[512]{0:T(512)S(1)} %get-tuple-element.51), channel_id=1, replica_groups=mesh['dp'=2,'row'=4,'col'=4] {'row'}, use_global_device_ids=true, to_apply=%region_7.8 | all-reduce | flops 1024 | bytes 8192 | tf_op jit(solution)/shard_map/psum | solution.py:72
  172.4 8.6 %all_gather.26 = bf16[2048,192]{0,1:T(8,128)(2,1)S(1)} all-gather(bf16[512,192]{0,1:T(8,128)(2,1)S(1)} %fusion.20), channel_id=1, replica_groups=mesh['dp'=2,'row'=4,'col'=4] {'col'}, dimensions={0}, use_global_device_ids=true | all-gather | bytes 983040 | tf_op jit(solution)/shard_map/all_gather | solution.py:32
  186.3 111.7 %reduce-scatter.13.cloned.1.call-done = f32[512,768]{1,0:T(8,128)} async-done(((f32[2048,768]{1,0:T(8,128)}), f32[512,768]{1,0:T(8,128)}) %reduce-scatter.13.cloned.1.call-update) | async-done | bytes 1572880 | tf_op jit(solution)/shard_map/reduce_scatter | solution.py:42
  298.0 5.7 multiply_convert_fusion.1
  303.8 62.3 %all-gather.4.cloned.1.call-done = bf16[2048,768]{1,0:T(8,128)(2,1)} async-done(((bf16[512,768]{1,0:T(8,128)(2,1)}), bf16[2048,768]{1,0:T(8,128)(2,1)}) %all-gather.4.cloned.1.call-update) | async-done | bytes 3145744 | tf_op jit(solution)/shard_map/all_gather | solution.py:52
  376.1 21.6 %reduce-scatter.15.cloned.1.call-done = f32[512,192]{0,1:T(8,128)} async-done(((f32[2048,192]{0,1:T(8,128)}), f32[512,192]{0,1:T(8,128)}) %reduce-scatter.15.cloned.1.call-update) | async-done | bytes 393232 | tf_op jit(solution)/shard_map/reduce_scatter | solution.py:62
  400.3 9.6 %all-reduce.3 = (f32[512]{0:T(512)}, f32[512]{0:T(512)}) all-reduce(f32[512]{0:T(512)} %get-tuple-element.50, f32[512]{0:T(512)} %get-tuple-element.49), channel_id=1, replica_groups=mesh['dp'=2,'row'=4,'col'=4] {'row'}, use_global_device_ids=true, to_apply=%region_13.14 | all-reduce | flops 1024 | bytes 8192 | tf_op jit(solution)/shard_map/psum | solution.py:72
  413.1 9.7 %all-reduce.2 = (f32[512]{0:T(512)}, f32[512]{0:T(512)}) all-reduce(f32[512]{0:T(512)} %get-tuple-element.43, f32[512]{0:T(512)} %get-tuple-element.46), channel_id=1, replica_groups=mesh['dp'=2,'row'=4,'col'=4] {'row'}, use_global_device_ids=true, to_apply=%region_17.18 | all-reduce | flops 1024 | bytes 8192 | tf_op jit(solution)/shard_map/psum | solution.py:72
  425.3 8.6 %all_gather.28 = bf16[2048,192]{0,1:T(8,128)(2,1)S(1)} all-gather(bf16[512,192]{0,1:T(8,128)(2,1)S(1)} %fusion.31), channel_id=1, replica_groups=mesh['dp'=2,'row'=4,'col'=4] {'col'}, dimensions={0}, use_global_device_ids=true | all-gather | bytes 983040 | tf_op jit(solution)/shard_map/all_gather | solution.py:32
  438.6 113.1 %reduce-scatter.17.cloned.1.call-done = f32[512,768]{1,0:T(8,128)} async-done(((f32[2048,768]{1,0:T(8,128)}), f32[512,768]{1,0:T(8,128)}) %reduce-scatter.17.cloned.1.call-update) | async-done | bytes 1572880 | tf_op jit(solution)/shard_map/reduce_scatter | solution.py:42
  555.9 62.1 %all-gather.6.cloned.1.call-done = bf16[2048,768]{1,0:T(8,128)(2,1)} async-done(((bf16[512,768]{1,0:T(8,128)(2,1)}), bf16[2048,768]{1,0:T(8,128)(2,1)}) %all-gather.6.cloned.1.call-update) | async-done | bytes 3145744 | tf_op jit(solution)/shard_map/all_gather | solution.py:52
  623.5 26.1 %reduce-scatter.19.cloned.1.call-done = f32[512,192]{0,1:T(8,128)} async-done(((f32[2048,192]{0,1:T(8,128)}), f32[512,192]{0,1:T(8,128)}) %reduce-scatter.19.cloned.1.call-update) | async-done | bytes 393232 | tf_op jit(solution)/shard_map/reduce_scatter | solution.py:62
  652.7 9.6 %all-reduce.1 = (f32[512]{0:T(512)}, f32[512]{0:T(512)}) all-reduce(f32[512]{0:T(512)} %get-tuple-element.45, f32[512]{0:T(512)} %get-tuple-element.47), channel_id=1, replica_groups=mesh['dp'=2,'row'=4,'col'=4] {'row'}, use_global_device_ids=true, to_apply=%region_23.24 | all-reduce | flops 1024 | bytes 8192 | tf_op jit(solution)/shard_map/psum | solution.py:72
  665.5 8.6 %all_gather.30 = bf16[2048,192]{0,1:T(8,128)(2,1)S(1)} all-gather(bf16[512,192]{0,1:T(8,128)(2,1)S(1)} %fusion.29), channel_id=1, replica_groups=mesh['dp'=2,'row'=4,'col'=4] {'col'}, dimensions={0}, use_global_device_ids=true | all-gather | bytes 983040 | tf_op jit(solution)/shard_map/all_gather | solution.py:32
  677.2 34.7 %reduce-scatter.21.cloned.1.call-done = f32[512,192]{0,1:T(8,128)} async-done(((f32[2048,192]{0,1:T(8,128)}), f32[512,192]{0,1:T(8,128)}) %reduce-scatter.21.cloned.1.call-update) | async-done | bytes 393232 | tf_op jit(solution)/shard_map/reduce_scatter | solution.py:42
  724.4 43.0 %all-gather.8.cloned.1.call-done = bf16[2048,576]{0,1:T(8,128)(2,1)} async-done(((bf16[512,576]{0,1:T(8,128)(2,1)}), bf16[2048,576]{0,1:T(8,128)(2,1)}) %all-gather.8.cloned.1.call-update) | async-done | bytes 2359312 | tf_op jit(solution)/shard_map/all_gather | solution.py:52
  781.0 11.6 %all-reduce = (f32[192]{0:T(256)}, f32[192]{0:T(256)}, f32[192]{0:T(256)}, f32[192]{0:T(256)}) all-reduce(f32[192]{0:T(256)S(1)} %copy-done.42, f32[192]{0:T(256)S(1)} %copy-done.43, f32[192]{0:T(256)S(1)} %copy-done.41, f32[192]{0:T(256)S(1)} %multiply_reduce_fusion.7), channel_id=1, replica_groups=mesh['dp'=2,'row'=4,'col'=4] {'dp','col'}, use_global_device_ids=true, to_apply=%region_35.36 | all-reduce | flops 768 | bytes 6144 | tf_op jit(solution)/shard_map/psum | solution.py:257
  794.7 5.1 all-reduce.5
  802.6 9.6 %all-reduce.9.cloned.1.call-done = (bf16[192,3,192]{0,2,1:T(8,128)(2,1)}, bf16[192,192]{1,0:T(8,128)(2,1)}, bf16[192,768]{1,0:T(8,128)(2,1)}, bf16[192,768]{1,0:T(8,128)(2,1)}) async-done(((bf16[192,3,192]{0,2,1:T(8,128)(2,1)}, bf16[192,192]{1,0:T(8,128)(2,1)}, bf16[192,768]{1,0:T(8,128)(2,1)}, bf16[192,768]{1,0:T(8,128)(2,1)}), (bf16[192,3,192]{0,2,1:T(8,128)(2,1)}, bf16[192,192]{1,0:T(8,128)(2,1)}, ...) | async-done | bytes 884752 | tf_op jit(solution)/shard_map/psum | solution.py:247
  818.5 23.4 %reduce-scatter.23.cloned.1.call-done = f32[512,192]{0,1:T(8,128)} async-done(((f32[2048,192]{0,1:T(8,128)}), f32[512,192]{0,1:T(8,128)}) %reduce-scatter.23.cloned.1.call-update) | async-done | bytes 393232 | tf_op jit(solution)/shard_map/reduce_scatter | solution.py:62
  (190 shorter events, 105.6 us)
Async XLA Ops:
  7.2 358.8 %copy-start = (bf16[192,768]{1,0:T(8,128)(2,1)S(1)}, bf16[192,768]{1,0:T(8,128)(2,1)}, u32[]{:S(2)}) copy-start(bf16[192,768]{1,0:T(8,128)(2,1)} %param.29) | copy-start | bytes 884740
  7.2 99.6 %reduce-scatter.9.cloned.1.call-start = ((), (), s32[]{:S(2)}) async-start(), calls=%async_computation.8 | async-start | bytes 5898240 | tf_op jit(solution)/shard_map/reduce_scatter | solution.py:42
  19.8 139.3 %reduce-scatter.11.cloned.1.call-start = ((), (), s32[]{:S(2)}) async-start(), calls=%async_computation.9 | async-start | bytes 1966080 | tf_op jit(solution)/shard_map/reduce_scatter | solution.py:62
  20.5 89.5 %copy-start.30 = (f32[3,64]{1,0:T(4,128)}, f32[3,64]{1,0:T(4,128)S(1)}, u32[]{:S(2)}) copy-start(f32[3,64]{1,0:T(4,128)S(1)} %reshape.262) | copy-start | bytes 2308
  20.6 89.9 %copy-start.39 = (f32[3,64]{1,0:T(4,128)}, f32[3,64]{1,0:T(4,128)S(1)}, u32[]{:S(2)}) copy-start(f32[3,64]{1,0:T(4,128)S(1)} %reshape.261) | copy-start | bytes 2308
  110.5 18.6 %copy-start.20 = (bf16[192,192]{1,0:T(8,128)(2,1)S(1)}, bf16[192,192]{1,0:T(8,128)(2,1)}, u32[]{:S(2)}) copy-start(bf16[192,192]{1,0:T(8,128)(2,1)} %param.23) | copy-start | bytes 221188
  130.7 167.3 %reduce-scatter.13.cloned.1.call-start = ((), (), s32[]{:S(2)}) async-start(), calls=%async_computation.10 | async-start | bytes 7864320 | tf_op jit(solution)/shard_map/reduce_scatter | solution.py:42
  171.2 14.3 %copy-start.22 = (f32[512]{0:T(512)}, f32[512]{0:T(512)S(1)}, u32[]{:S(2)}) copy-start(f32[512]{0:T(512)S(1)} %get-tuple-element.87) | copy-start | bytes 6148
  185.6 180.5 %all-gather.4.cloned.1.call-start = ((), (), s32[]{:S(2)}) async-start(), calls=%async_computation.11 | async-start | bytes 3932160 | tf_op jit(solution)/shard_map/all_gather | solution.py:52
  186.3 117.4 %copy-start.24 = (f32[768]{0:T(1024)}, f32[768]{0:T(1024)S(1)}, u32[]{:S(2)}) copy-start(f32[768]{0:T(1024)S(1)} %convert_element_type.167) | copy-start | bytes 9220
  303.7 94.0 %reduce-scatter.15.cloned.1.call-start = ((), (), s32[]{:S(2)}) async-start(), calls=%async_computation.12 | async-start | bytes 1966080 | tf_op jit(solution)/shard_map/reduce_scatter | solution.py:62
  370.3 181.4 %reduce-scatter.17.cloned.1.call-start = ((), (), s32[]{:S(2)}) async-start(), calls=%async_computation.13 | async-start | bytes 7864320 | tf_op jit(solution)/shard_map/reduce_scatter | solution.py:42
  438.5 179.4 %all-gather.6.cloned.1.call-start = ((), (), s32[]{:S(2)}) async-start(), calls=%async_computation.14 | async-start | bytes 3932160 | tf_op jit(solution)/shard_map/all_gather | solution.py:52
  555.6 94.0 %reduce-scatter.19.cloned.1.call-start = ((), (), s32[]{:S(2)}) async-start(), calls=%async_computation.15 | async-start | bytes 1966080 | tf_op jit(solution)/shard_map/reduce_scatter | solution.py:62
  622.2 89.7 %reduce-scatter.21.cloned.1.call-start = ((), (), s32[]{:S(2)}) async-start(), calls=%async_computation.16 | async-start | bytes 1966080 | tf_op jit(solution)/shard_map/reduce_scatter | solution.py:42
  676.5 90.9 %all-gather.8.cloned.1.call-start = ((), (), s32[]{:S(2)}) async-start(), calls=%async_computation.17 | async-start | bytes 2949120 | tf_op jit(solution)/shard_map/all_gather | solution.py:52
  718.0 94.2 %all-reduce.9.cloned.1.call-start = ((), (), s32[]{:S(2)}) async-start(), calls=%async_computation.19 | async-start | bytes 1966080 | tf_op jit(solution)/shard_map/psum | solution.py:247
  772.8 69.1 %reduce-scatter.23.cloned.1.call-start = ((), (), s32[]{:S(2)}) async-start(), calls=%async_computation.18 | async-start | bytes 1966080 | tf_op jit(solution)/shard_map/reduce_scatter | solution.py:62
  794.6 47.3 %copy-start.3 = (f32[512,192]{0,1:T(8,128)S(1)}, f32[512,192]{0,1:T(8,128)}, u32[]{:S(2)}) copy-start(f32[512,192]{0,1:T(8,128)} %get-tuple-element.78) | copy-start | bytes 1179652
  794.6 47.3 %copy-start.12 = (f32[512,192]{0,1:T(8,128)S(1)}, f32[512,192]{0,1:T(8,128)}, u32[]{:S(2)}) copy-start(f32[512,192]{0,1:T(8,128)} %get-tuple-element.74) | copy-start | bytes 1179652
  794.6 47.3 %copy-start.23 = (f32[512]{0:T(512)S(1)}, f32[512]{0:T(512)}, u32[]{:S(2)}) copy-start(f32[512]{0:T(512)} %copy-done.22) | copy-start | bytes 6148
  794.6 47.3 %copy-start.29 = (f32[192]{0:T(256)S(1)}, f32[192]{0:T(256)}, u32[]{:S(2)}) copy-start(f32[192]{0:T(256)} %convert_element_type.164) | copy-start | bytes 2308
  794.6 47.3 %copy-start.33 = (f32[512]{0:T(512)S(1)}, f32[512]{0:T(512)}, u32[]{:S(2)}) copy-start(f32[512]{0:T(512)} %copy-done.32) | copy-start | bytes 6148
  794.7 47.3 %copy-start.35 = (f32[512]{0:T(512)S(1)}, f32[512]{0:T(512)}, u32[]{:S(2)}) copy-start(f32[512]{0:T(512)} %copy-done.34) | copy-start | bytes 6148
  (37 other events, 75.3 us)
Sparse Core Ops, SparseCore 0:
  19.9 86.8 reduce-scatter.8
  130.8 28.1 reduce-scatter.10
  185.7 112.2 reduce-scatter.12
  303.8 62.1 all-gather.3
  370.4 27.2 reduce-scatter.14
  438.7 113.0 reduce-scatter.16
  555.8 62.1 all-gather.5
  622.3 27.2 reduce-scatter.18
  676.6 35.2 reduce-scatter.20
  718.1 49.2 all-gather.7
  773.0 39.2 all-reduce.8
  814.6 27.2 reduce-scatter.22
where the time goes:
time: 855 us; the launch traced here: 851 us
  waiting for transfers between devices  619 us (72%)
  blocking collectives  106 us (12%)
  other arithmetic  55.1 us (6%)
  matrix products  39.4 us (5%)
  local copies, waits for them, and re-layouts  16 us (2%)
  between operations  14.7 us (2%)
    reduce_scatter x4, waiting for transfers between devices, spread_cols(): lax.psum_scatter(term(jnp.int32(0), row_share * lax.axis_size('row')), 'r...  344 us
    all_gather x3, waiting for transfers between devices, spread_rows(): gathered = lax.all_gather(activations, 'row', axis=0, tiled=True)  167 us
    reduce_scatter x4, waiting for transfers between devices, spread_rows(): lax.psum_scatter(term(jnp.int32(0), col_share * lax.axis_size('col')), 'c...  97.1 us
    psum x4, blocking collectives, row_totals(): return lax.psum((first_sum, second_sum), 'row')  38.4 us
    all_gather x4, blocking collectives, spread_cols(): gathered = lax.all_gather(activations, 'col', axis=0, tiled=True)  34.2 us
    dot_general x8, matrix products, product(): lax.dot_general(block_rows, weight_mat, (contract, ((), ())), preferred_e...  25.5 us
  transfers between devices with their start and end apart: 12, of which 12 were waited for; matrix products, arithmetic and copies ran while one was open for 4% of the time, Pallas kernels for 0%

commit v1 on v0

v1 whole, which is shorter than its diff:
```python
import jax
import jax.numpy as jnp
from jax import lax
from jax.sharding import PartitionSpec as P

HEAD_DIM = 64
EPSILON = 1e-12
F32 = jnp.float32
BF16 = jnp.bfloat16


def dot(left, right, left_dim, right_dim):
    return lax.dot_general(
        left, right, (((left_dim,), (right_dim,)), ((), ())), preferred_element_type=F32
    )


def swap_bit(value, axis, bit):
    size = lax.axis_size(axis)
    return lax.ppermute(value, axis, [(at, at ^ bit) for at in range(size)])


def transpose_grid(value):
    rows, cols = lax.axis_size("row"), lax.axis_size("col")
    pairs = [(a * cols + b, b * cols + a) for a in range(rows) for b in range(cols)]
    return lax.ppermute(value, ("row", "col"), pairs)


def ordered(flag, own, other, axis):
    return jnp.concatenate(
        (jnp.where(flag, other, own), jnp.where(flag, own, other)), axis=axis
    )


def normalise(hidden, gain, shift):
    width = hidden.shape[0]
    center = jnp.sum(hidden, axis=0, keepdims=True) / width
    spread = jnp.sum(hidden * hidden, axis=0, keepdims=True) / width - center * center
    inverse = lax.rsqrt(spread + EPSILON)
    scaled = (hidden - center) * inverse
    return scaled, inverse, scaled * gain + shift


def normalise_back(upstream, scaled, inverse, gain):
    width = upstream.shape[0]
    weighted = upstream * gain
    mean = jnp.sum(weighted, axis=0, keepdims=True) / width
    slope = jnp.sum(weighted * scaled, axis=0, keepdims=True) / width
    return inverse * (weighted - mean - scaled * slope)


def shards(
    layer_in,
    seq_lengths,
    w_qkv,
    q_bias,
    v_bias,
    w_out,
    b_out,
    ln1_gain,
    ln1_bias,
    w_in,
    b_in,
    w_back,
    b_back,
    ln2_gain,
    ln2_bias,
    out_grad,
):
    n_rows = lax.axis_size("row")
    row, col = lax.axis_index("row"), lax.axis_index("col")
    low_bit, high_bit = (col % 2) == 1, (col // 2) == 1
    feats, slot = layer_in.shape
    half = slot // 2
    heads = w_out.shape[0] // HEAD_DIM
    head_cols = w_out.shape[0]

    def my_half(whole):
        return jnp.where(low_bit, whole[:, half:], whole[:, :half])

    def other_half(whole):
        return jnp.where(low_bit, whole[:, :half], whole[:, half:])

    def join_halves(own):
        return ordered(low_bit, own, swap_bit(own, "col", 1), 1)

    def sum_tokens(partial):
        mine = my_half(partial) + swap_bit(other_half(partial), "col", 1)
        mine = mine.astype(BF16)
        return mine.astype(F32) + swap_bit(mine, "col", 2).astype(F32)

    qkv_part = w_qkv.transpose(1, 2, 0).reshape(3 * head_cols, feats)
    vectors = jnp.stack((b_out, ln1_gain, ln1_bias, b_back, ln2_gain, ln2_bias))
    vectors = jnp.pad(vectors, ((0, 16 - vectors.shape[0]), (0, 0)))
    x_block = transpose_grid(layer_in)
    qkv_all = lax.all_gather(qkv_part, "row", axis=0)
    out_all = lax.all_gather(jnp.concatenate((w_out, vectors)), "row", axis=0)
    in_all = lax.all_gather(w_in, "row", axis=0, tiled=True)
    back_all = lax.all_gather(w_back, "row", axis=0, tiled=True)
    vec_all = out_all[:, head_cols : head_cols + 6].astype(F32)
    vec_all = vec_all.transpose(1, 0, 2).reshape(6, n_rows * feats, 1)
    b_out_all, gain_one, shift_one, b_back_all, gain_two, shift_two = [
        vec_all[i] for i in range(6)
    ]
    out_all = out_all[:, :head_cols]

    pair = ordered(low_bit, x_block, swap_bit(x_block, "col", 1), 0)
    x = ordered(high_bit, pair, swap_bit(pair, "col", 2), 0)
    length = lax.dynamic_slice_in_dim(seq_lengths, row, 1)
    key_live = jnp.arange(slot, dtype=jnp.int32)[:, None] < length
    first_token = jnp.where(low_bit, half, 0)
    live = (first_token + jnp.arange(half, dtype=jnp.int32)[None, :] < length).astype(F32)

    grad_block = transpose_grid(out_grad.astype(BF16))
    grad_pair = ordered(
        low_bit, my_half(grad_block), swap_bit(other_half(grad_block), "col", 1), 0
    )
    grad_out = ordered(high_bit, grad_pair, swap_bit(grad_pair, "col", 2), 0)

    qkv = sum(
        dot(qkv_all[b], x[b * feats : (b + 1) * feats], 1, 0) for b in range(n_rows)
    )
    queries = (qkv[:head_cols] + q_bias.astype(F32)[:, None]).astype(BF16)
    keys_in = qkv[head_cols : 2 * head_cols].astype(BF16)
    values = (qkv[2 * head_cols :] + v_bias.astype(F32)[:, None]).astype(BF16)
    head_shape = (heads, HEAD_DIM, slot)
    queries, keys_in, values = (
        part.reshape(head_shape) for part in (queries, keys_in, values)
    )
    scale = HEAD_DIM ** (-0.5)
    scores = (
        jnp.einsum("hdk,hdq->hkq", keys_in, queries, preferred_element_type=F32) * scale
    )
    scores = jnp.where(key_live[None], scores, -1000000000.0)
    peak = jnp.max(scores, axis=1, keepdims=True)
    exponent = jnp.exp(scores - peak)
    weights = (exponent / jnp.sum(exponent, axis=1, keepdims=True)).astype(BF16)
    context = jnp.einsum("hdk,hkq->hdq", values, weights, preferred_element_type=F32)
    context = context.reshape(head_cols, slot).astype(BF16)

    attended = jnp.concatenate([dot(out_all[b], context, 0, 0) for b in range(n_rows)])
    first = my_half(x).astype(F32) + sum_tokens(attended) + b_out_all
    scaled_one, inverse_one, normed = normalise(first, gain_one, shift_one)
    normed_all = join_halves(normed.astype(BF16))

    pre = dot(in_all, normed_all, 0, 0) + b_in.astype(F32)[:, None]
    share = 0.5 * (1.0 + lax.erf(pre * (0.5**0.5)))
    hidden = (pre * share).astype(BF16)
    slope = (share + pre * jnp.exp(-0.5 * pre * pre) * ((0.5 / jnp.pi) ** 0.5)).astype(BF16)
    second = normed + sum_tokens(dot(back_all, hidden, 1, 0)) + b_back_all
    scaled_two, inverse_two, final = normalise(second, gain_two, shift_two)
    final = (final * live).astype(BF16)

    grad_final = grad_out.astype(F32) * live
    ln2_gain_sum = jnp.sum(grad_final * scaled_two, axis=1)
    ln2_bias_sum = jnp.sum(grad_final, axis=1)
    grad_second = normalise_back(grad_final, scaled_two, inverse_two, gain_two)
    b_back_sum = jnp.sum(grad_second, axis=1)
    grad_returned = join_halves(grad_second.astype(BF16))

    w_back_part = dot(grad_returned, hidden, 1, 1)
    grad_hidden = dot(back_all, grad_returned, 0, 0)
    grad_pre = grad_hidden * slope.astype(F32)
    b_in_sum = jnp.sum(grad_pre, axis=1)
    grad_pre = grad_pre.astype(BF16)
    w_in_part = dot(normed_all, grad_pre, 1, 1)
    grad_normed = grad_second + sum_tokens(dot(in_all, grad_pre, 1, 0))
    ln1_gain_sum = jnp.sum(grad_normed * scaled_one, axis=1)
    ln1_bias_sum = jnp.sum(grad_normed, axis=1)
    grad_first = normalise_back(grad_normed, scaled_one, inverse_one, gain_one)
    b_out_sum = jnp.sum(grad_first, axis=1)
    grad_attended = join_halves(grad_first.astype(BF16))

    w_out_part = dot(context, grad_attended, 1, 1)
    grad_context = sum(
        dot(out_all[b], grad_attended[b * feats : (b + 1) * feats], 1, 0)
        for b in range(n_rows)
    )
    grad_context = grad_context.astype(BF16).reshape(head_shape)
    grad_weights = jnp.einsum(
        "hdk,hdq->hkq", values, grad_context, preferred_element_type=F32
    )
    weights_wide = weights.astype(F32)
    inner = jnp.sum(weights_wide * grad_weights, axis=1, keepdims=True)
    grad_scores = (weights_wide * (grad_weights - inner)).astype(BF16)
    grad_queries = (
        jnp.einsum("hdk,hkq->hdq", keys_in, grad_scores, preferred_element_type=F32) * scale
    )
    grad_keys = (
        jnp.einsum("hdq,hkq->hdk", queries, grad_scores, preferred_element_type=F32) * scale
    )
    grad_values = jnp.einsum(
        "hdq,hkq->hdk", grad_context, weights, preferred_element_type=F32
    )
    grad_qkv = jnp.concatenate(
        [
            part.reshape(head_cols, slot).astype(BF16)
            for part in (grad_queries, grad_keys, grad_values)
        ]
    )
    q_bias_sum = jnp.sum(grad_qkv[:head_cols], axis=1, dtype=F32)
    v_bias_sum = jnp.sum(grad_qkv[2 * head_cols :], axis=1, dtype=F32)

    half_grad = 0.5 * grad_first
    kept = jnp.concatenate(
        (jnp.where(low_bit, 0.0, half_grad), jnp.where(low_bit, half_grad, 0.0)), axis=1
    )
    blocks = [
        dot(qkv_all[b], grad_qkv, 0, 0) + kept[b * feats : (b + 1) * feats]
        for b in range(n_rows)
    ]
    evens = jnp.concatenate((blocks[0], blocks[2]))
    odds = jnp.concatenate((blocks[1], blocks[3]))
    mine = jnp.where(low_bit, odds, evens) + swap_bit(
        jnp.where(low_bit, evens, odds), "col", 1
    )
    own = jnp.where(high_bit, mine[feats:], mine[:feats])
    away = jnp.where(high_bit, mine[:feats], mine[feats:]).astype(BF16)
    in_grad = own + swap_bit(away, "col", 2).astype(F32)
    in_grad = transpose_grid(in_grad.astype(BF16)).astype(F32)

    final = final.reshape(n_rows, feats, half)
    own = lax.dynamic_index_in_dim(final, col, 0, False)
    away = lax.dynamic_index_in_dim(final, col ^ 1, 0, False)
    layer_out = transpose_grid(ordered(low_bit, own, swap_bit(away, "col", 1), 1))

    def reduce_rows(part):
        kept_rows = lax.psum_scatter(part.astype(BF16), "row", scatter_dimension=0, tiled=True)
        return lax.psum(kept_rows, "dp").astype(F32)

    w_back_grad = reduce_rows(w_back_part)
    w_in_grad = reduce_rows(w_in_part)
    w_out_blocks = w_out_part.reshape(head_cols, n_rows, feats).transpose(1, 0, 2)
    w_out_grad = reduce_rows(w_out_blocks.reshape(n_rows * head_cols, feats))
    vector_sums = jnp.stack(
        (ln1_gain_sum, ln1_bias_sum, ln2_gain_sum, ln2_bias_sum, b_out_sum, b_back_sum)
    )
    vector_sums = vector_sums + swap_bit(vector_sums, "col", 1)
    vector_blocks = vector_sums.reshape(6, n_rows, feats).transpose(1, 0, 2)
    shared = jnp.concatenate((q_bias_sum[None], v_bias_sum[None], b_in_sum.reshape(-1, feats)))
    n_extra = 6 + shared.shape[0]
    extra = [
        jnp.concatenate((vector_blocks[b], shared, jnp.zeros((16 - n_extra, feats), F32)))
        for b in range(n_rows)
    ]
    qkv_blocks = []
    for b in range(n_rows):
        qkv_blocks += [dot(grad_qkv, x[b * feats : (b + 1) * feats], 1, 1), extra[b]]
    qkv_sum = reduce_rows(jnp.concatenate(qkv_blocks))
    w_qkv_grad = qkv_sum[: 3 * head_cols].reshape(3, head_cols, feats).transpose(2, 0, 1)
    tail = qkv_sum[3 * head_cols :]
    return (
        layer_out,
        in_grad,
        w_qkv_grad,
        tail[6],
        tail[7],
        w_out_grad,
        tail[4],
        tail[0],
        tail[1],
        w_in_grad,
        tail[8:n_extra].reshape(-1),
        w_back_grad,
        tail[5],
        tail[2],
        tail[3],
    )


def solution(mesh):
    tokens = P("row", ("dp", "col"))
    block = P("row", "col")
    in_specs = (
        tokens,
        P("dp"),
        P("row", None, "col"),
        P("col"),
        P("col"),
        P("col", "row"),
        P("row"),
        P("row"),
        P("row"),
        block,
        P("col"),
        block,
        P("row"),
        P("row"),
        P("row"),
        tokens,
    )
    out_specs = (
        tokens,
        tokens,
        P("row", None, "col"),
        P("col"),
        P("col"),
        P("col", "row"),
        P("row"),
        P("row"),
        P("row"),
        block,
        P("col"),
        block,
        P("row"),
        P("row"),
        P("row"),
    )
    return jax.shard_map(shards, mesh=mesh, in_specs=in_specs, out_specs=out_specs, check_vma=False)
```

time: 855 us -> 334 us (0.39)
  waiting for transfers between devices: 619 us -> 166 us
  blocking collectives: 106 us -> 45.7 us
  other arithmetic: 55.1 us -> 22.9 us
  local copies, waits for them, and re-layouts: 16 us -> 34.7 us
  starting transfers between devices: 0.68 us -> 14.5 us
    reduce_scatter x8 -> x4, waiting for transfers between devices: 442 us -> 70.4 us  [reduce_rows(): lax.psum_scatter(part.astype(BF16), 'row', scatter_dimension=0, tiled=True)]
    all_gather x3 -> x2, waiting for transfers between devices: 167 us -> 18.1 us  [the longest x1 18.1 us: shards(): back_all = lax.all_gather(w_back, 'row', axis=0, tiled=True)]
    psum x6 -> x0, blocking collectives: 55 us -> none  [the longest x4 38.4 us: row_totals(): return lax.psum((first_sum, second_sum), 'row')]
    ppermute x0 -> x21, waiting for transfers between devices: none -> 43.6 us  [the longest x17 43.6 us: swap_bit(): return lax.ppermute(value, axis, [(at, at ^ bit) for at in range(size)])]
    psum x1, waiting for transfers between devices: 9.62 us -> 33.4 us  [reduce_rows(): return lax.psum(kept_rows, 'dp').astype(F32)]
    convert_element_type x23 -> x20, other arithmetic: 31.8 us -> 10.2 us  [the longest x3 2.4 us: reduce_rows(): return lax.psum(kept_rows, 'dp').astype(F32)]
    ppermute x0 -> x21, starting transfers between devices: none -> 14 us  [the longest x17 10.2 us: swap_bit(): return lax.ppermute(value, axis, [(at, at ^ bit) for at in range(size)])]
    dot_general x18 -> x32, matrix products: 39.4 us -> 29.2 us  [the longest x27 24 us: dot(): lax.dot_general(left, right, (((left_dim,), (right_dim,)), ((), ())), pre...]
  transfers between devices with their start and end apart: 12 -> 28, of which waited for: 12 -> 17; matrix products, arithmetic and copies ran while one was open for 4% -> 20% of each run, Pallas kernels for 0% -> 0%
where the time goes in v1:
time: 334 us; the launch traced here: 331 us
  waiting for transfers between devices  166 us (50%)
  blocking collectives  45.7 us (14%)
  local copies, waits for them, and re-layouts  34.7 us (10%)
  matrix products  32.1 us (10%)
  other arithmetic  22.9 us (7%)
  between operations  15.3 us (5%)
  starting transfers between devices  14.5 us (4%)
    reduce_scatter x4, waiting for transfers between devices, reduce_rows(): lax.psum_scatter(part.astype(BF16), 'row', scatter_dimension=0, tiled=True)  70.4 us
    ppermute x17, waiting for transfers between devices, swap_bit(): return lax.ppermute(value, axis, [(at, at ^ bit) for at in range(size)])  43.6 us
    psum x1, waiting for transfers between devices, reduce_rows(): return lax.psum(kept_rows, 'dp').astype(F32)  33.4 us
    all_gather x1, blocking collectives, shards(): out_all = lax.all_gather(jnp.concatenate((w_out, vectors)), 'row', axis=0)  25.2 us
    dot_general x27, matrix products, dot(): lax.dot_general(left, right, (((left_dim,), (right_dim,)), ((), ())), pre...  24 us
    all_gather x1, blocking collectives, shards(): qkv_all = lax.all_gather(qkv_part, 'row', axis=0)  20.5 us
    all_gather x1, waiting for transfers between devices, shards(): back_all = lax.all_gather(w_back, 'row', axis=0, tiled=True)  18.1 us
    unnamed x115, local copies, waits for them, and re-layouts  10.6 us
  transfers between devices with their start and end apart: 28, of which 17 were waited for; matrix products, arithmetic and copies ran while one was open for 20% of the time, Pallas kernels for 0%

profile of v1, /device:TPU:20, one launch (start us, length us, event | category | flops | bytes accessed | tf_op | source)
XLA Modules:
  0.0 330.9 jit_solution(16241139114271701276)
XLA Ops:
  13.5 2.0 collective-permute-start.1
  15.6 25.2 %all-gather.1 = bf16[4,208,192]{1,2,0:T(8,128)(2,1)S(1)} all-gather(bf16[1,208,192]{1,2,0:T(8,128)(2,1)S(1)} %fusion.64), channel_id=2, replica_groups=mesh['dp'=2,'row'=4,'col'=4] {'row'}, dimensions={0}, use_global_device_ids=true | all-gather | bytes 399360 | tf_op jit(solution)/shard_map/all_gather | solution.py:97
  40.9 2.6 collective-permute-start.2
  44.2 20.5 %all_gather.17 = bf16[4,576,192]{1,2,0:T(8,128)(2,1)S(1)} all-gather(bf16[1,576,192]{1,2,0:T(8,128)(2,1)S(1)} %copy.76), channel_id=1, replica_groups=mesh['dp'=2,'row'=4,'col'=4] {'row'}, dimensions={0}, use_global_device_ids=true | all-gather | bytes 1105920 | tf_op jit(solution)/shard_map/all_gather | solution.py:96
  66.6 2.9 fusion.85
  69.4 2.3 divide_convert_fusion
  73.4 2.3 collective-permute-done.3
  78.4 8.9 %collective-permute-done.4 = bf16[768,256]{1,0:T(8,128)(2,1)} collective-permute-done((bf16[768,256]{1,0:T(8,128)(2,1)S(1)}, bf16[768,256]{1,0:T(8,128)(2,1)}, u32[]{:S(2)}, u32[]{:S(2)}) %collective-permute-start.4) | collective-permute-done | bytes 393248 | tf_op jit(solution)/shard_map/ppermute | solution.py:20
  91.0 4.0 %fusion.12 = (bf16[768,512]{0,1:T(8,128)(2,1)}, f32[512,768]{1,0:T(8,128)}) fusion(f32[768]{0:T(1024)} %convert_element_type.189, bf16[768,768]{1,0:T(8,128)(2,1)} %all-gather.5.cloned.1.call-done, bf16[768,256]{1,0:T(8,128)(2,1)S(1)} %get-tuple-element.100, bf16[768,256]{1,0:T(8,128)(2,1)S(1)} %get-tuple-element.99), kind=kOutput, calls=%fused_computation.28 | convolution fusion | flops 607911936 | bytes 4328448 | tf_op jit(solution)/shard_map/dot_general | solution.py:13
  95.0 18.1 %all-gather.7.cloned.1.call-done = bf16[768,768]{1,0:T(8,128)(2,1)} async-done(((bf16[192,768]{1,0:T(8,128)(2,1)}), bf16[768,768]{1,0:T(8,128)(2,1)}) %all-gather.7.cloned.1.call-update) | async-done | bytes 1179664 | tf_op jit(solution)/shard_map/all_gather | solution.py:99
  113.1 2.3 convolution_bitcast_fusion.1
  126.9 6.5 %collective-permute-done.7 = bf16[768,256]{1,0:T(8,128)(2,1)S(1)} collective-permute-done((bf16[768,256]{1,0:T(8,128)(2,1)S(1)}, bf16[768,256]{1,0:T(8,128)(2,1)S(1)}, u32[]{:S(2)}, u32[]{:S(2)}) %collective-permute-start.7) | collective-permute-done | bytes 393248 | tf_op jit(solution)/shard_map/ppermute | solution.py:20
  142.3 2.1 collective-permute-done.14
  145.2 10.6 %collective-permute-done.15 = bf16[768,256]{1,0:T(8,128)(2,1)S(1)} collective-permute-done((bf16[768,256]{1,0:T(8,128)(2,1)S(1)}, bf16[768,256]{1,0:T(8,128)(2,1)S(1)}, u32[]{:S(2)}, u32[]{:S(2)}) %collective-permute-start.15) | collective-permute-done | bytes 393248 | tf_op jit(solution)/shard_map/ppermute | solution.py:20
  162.0 3.2 convolution_convert_fusion
  169.9 3.2 convolution_convert_fusion.1
  186.8 2.1 fusion.24
  191.9 3.2 concatenate.62
  195.1 2.5 copy.96
  203.6 9.5 %reduce-scatter.11.cloned.1.call-done = bf16[192,768]{1,0:T(8,128)(2,1)} async-done(((bf16[768,768]{1,0:T(8,128)(2,1)}), bf16[192,768]{1,0:T(8,128)(2,1)}) %reduce-scatter.11.cloned.1.call-update) | async-done | bytes 294928 | tf_op jit(solution)/shard_map/reduce_scatter | solution.py:228
  213.1 30.2 %reduce-scatter.9.cloned.1.call-done = bf16[192,768]{1,0:T(8,128)(2,1)} async-done(((bf16[768,768]{1,0:T(8,128)(2,1)}), bf16[192,768]{1,0:T(8,128)(2,1)}) %reduce-scatter.9.cloned.1.call-update) | async-done | bytes 294928 | tf_op jit(solution)/shard_map/reduce_scatter | solution.py:228
  243.3 30.7 %reduce-scatter.13.cloned.1.call-done = bf16[592,192]{1,0:T(8,128)(2,1)} async-done(((bf16[2368,192]{1,0:T(8,128)(2,1)}), bf16[592,192]{1,0:T(8,128)(2,1)}) %reduce-scatter.13.cloned.1.call-update) | async-done | bytes 227344 | tf_op jit(solution)/shard_map/reduce_scatter | solution.py:228
  275.4 5.4 %collective-permute-done.18 = bf16[192,512]{1,0:T(8,128)(2,1)S(1)} collective-permute-done((bf16[192,512]{1,0:T(8,128)(2,1)S(1)}, bf16[192,512]{1,0:T(8,128)(2,1)S(1)}, u32[]{:S(2)}, u32[]{:S(2)}) %collective-permute-start.18) | collective-permute-done | bytes 196640 | tf_op jit(solution)/shard_map/ppermute | solution.py:20
  282.5 33.4 %all-reduce.4.cloned.1.call-done = (bf16[592,192]{1,0:T(8,128)(2,1)}, bf16[192,192]{1,0:T(8,128)(2,1)}, bf16[192,768]{1,0:T(8,128)(2,1)}, bf16[192,768]{1,0:T(8,128)(2,1)}) async-done(((bf16[592,192]{1,0:T(8,128)(2,1)}, bf16[192,192]{1,0:T(8,128)(2,1)}, bf16[192,768]{1,0:T(8,128)(2,1)}, bf16[192,768]{1,0:T(8,128)(2,1)}), (bf16[592,192]{1,0:T(8,128)(2,1)}, bf16[192,192]{1,0:T(8,128)(2,1)}, ...) | async-done | bytes 890896 | tf_op jit(solution)/shard_map/psum | solution.py:229
  (281 shorter events, 81.8 us)
Async XLA Ops:
  7.3 83.7 %all-gather.5.cloned.1.call-start = ((), (), s32[]{:S(2)}) async-start(), calls=%async_computation.4 | async-start | bytes 1474560 | tf_op jit(solution)/shard_map/all_gather | solution.py:98
  7.3 6.2 %collective-permute-start = (bf16[192,512]{1,0:T(8,128)(2,1)}, bf16[192,512]{1,0:T(8,128)(2,1)S(1)}, u32[]{:S(2)}, u32[]{:S(2)}) collective-permute-start(bf16[192,512]{1,0:T(8,128)(2,1)} %param.16), channel_id=1, source_target_pairs={{0,0},{1,4},{2,8},{3,12},{4,1},{5,5},{6,9},{7,13},{8,2},{9,6},{10,... | collective-permute-start | bytes 589832 | tf_op jit(solution)/shard_map/ppermute | solution.py:26
  8.9 104.2 %all-gather.7.cloned.1.call-start = ((), (), s32[]{:S(2)}) async-start(), calls=%async_computation.5 | async-start | bytes 1474560 | tf_op jit(solution)/shard_map/all_gather | solution.py:99
  13.5 27.3 %collective-permute-start.1 = (bf16[192,512]{1,0:T(8,128)(2,1)S(1)}, bf16[192,512]{1,0:T(8,128)(2,1)S(1)}, u32[]{:S(2)}, u32[]{:S(2)}) collective-permute-start(bf16[192,512]{1,0:T(8,128)(2,1)S(1)} %collective-permute-done), channel_id=1, source_target_pairs={{0,1},{1,0},{2,3},{3,2},{4,5},{5,4},{6,7},{7,6},{8,9},{9,8},{10,11... | collective-permute-start | bytes 589832 | tf_op jit(solution)/shard_map/ppermute | solution.py:20
  40.9 23.8 %collective-permute-start.2 = (bf16[384,512]{1,0:T(8,128)(2,1)S(1)}, bf16[384,512]{1,0:T(8,128)(2,1)S(1)}, u32[]{:S(2)}, u32[]{:S(2)}) collective-permute-start(bf16[384,512]{1,0:T(8,128)(2,1)S(1)} %pad_maximum_fusion.13), channel_id=1, source_target_pairs={{0,2},{1,3},{2,0},{3,1},{4,6},{5,7},{6,4},{7,5},{8,10},{9,11},{10,... | collective-permute-start | bytes 1179656 | tf_op jit(solution)/shard_map/ppermute | solution.py:20
  73.3 2.4 collective-permute-start.3
  75.9 11.3 %collective-permute-start.4 = (bf16[768,256]{1,0:T(8,128)(2,1)S(1)}, bf16[768,256]{1,0:T(8,128)(2,1)}, u32[]{:S(2)}, u32[]{:S(2)}) collective-permute-start(bf16[768,256]{1,0:T(8,128)(2,1)S(1)} %add_convert_fusion.2), channel_id=1, source_target_pairs={{0,2},{1,3},{2,0},{3,1},{4,6},{5,7},{6,4},{7,5},{8,10},{9,11},{10,... | collective-permute-start | bytes 1179656 | tf_op jit(solution)/shard_map/ppermute | solution.py:20
  76.0 127.6 %reduce-scatter.7.cloned.1.call-start = ((), (), s32[]{:S(2)}) async-start(), calls=%async_computation.6 | async-start | bytes 491520 | tf_op jit(solution)/shard_map/reduce_scatter | solution.py:228
  89.0 26.6 %collective-permute-start.10 = (bf16[192,512]{1,0:T(8,128)(2,1)S(1)}, bf16[192,512]{1,0:T(8,128)(2,1)S(1)}, u32[]{:S(2)}, u32[]{:S(2)}) collective-permute-start(bf16[192,512]{1,0:T(8,128)(2,1)S(1)} %convert_element_type.197), channel_id=1, source_target_pairs={{0,0},{1,4},{2,8},{3,12},{4,1},{5,5},{6,9},{7,13},{8,2},{9,6},{10,... | collective-permute-start | bytes 589832 | tf_op jit(solution)/shard_map/ppermute | solution.py:26
  115.5 3.1 collective-permute-start.6
  115.6 2.4 collective-permute-start.11
  118.0 7.9 %collective-permute-start.12 = (bf16[384,256]{1,0:T(8,128)(2,1)S(1)}, bf16[384,256]{1,0:T(8,128)(2,1)}, u32[]{:S(2)}, u32[]{:S(2)}) collective-permute-start(bf16[384,256]{1,0:T(8,128)(2,1)S(1)} %pad_maximum_fusion.16), channel_id=1, source_target_pairs={{0,2},{1,3},{2,0},{3,1},{4,6},{5,7},{6,4},{7,5},{8,10},{9,11},{10,... | collective-permute-start | bytes 589832 | tf_op jit(solution)/shard_map/ppermute | solution.py:20
  118.8 14.7 %collective-permute-start.7 = (bf16[768,256]{1,0:T(8,128)(2,1)S(1)}, bf16[768,256]{1,0:T(8,128)(2,1)S(1)}, u32[]{:S(2)}, u32[]{:S(2)}) collective-permute-start(bf16[768,256]{1,0:T(8,128)(2,1)S(1)} %add_convert_fusion.1), channel_id=1, source_target_pairs={{0,2},{1,3},{2,0},{3,1},{4,6},{5,7},{6,4},{7,5},{8,10},{9,11},{10,... | collective-permute-start | bytes 1179656 | tf_op jit(solution)/shard_map/ppermute | solution.py:20
  142.1 2.4 collective-permute-start.14
  144.6 11.2 %collective-permute-start.15 = (bf16[768,256]{1,0:T(8,128)(2,1)S(1)}, bf16[768,256]{1,0:T(8,128)(2,1)S(1)}, u32[]{:S(2)}, u32[]{:S(2)}) collective-permute-start(bf16[768,256]{1,0:T(8,128)(2,1)S(1)} %add_convert_fusion), channel_id=1, source_target_pairs={{0,2},{1,3},{2,0},{3,1},{4,6},{5,7},{6,4},{7,5},{8,10},{9,11},{10,... | collective-permute-start | bytes 1179656 | tf_op jit(solution)/shard_map/ppermute | solution.py:20
  162.0 51.1 %reduce-scatter.11.cloned.1.call-start = ((), (), s32[]{:S(2)}) async-start(), calls=%async_computation.8 | async-start | bytes 1474560 | tf_op jit(solution)/shard_map/reduce_scatter | solution.py:228
  165.2 78.1 %reduce-scatter.9.cloned.1.call-start = ((), (), s32[]{:S(2)}) async-start(), calls=%async_computation.7 | async-start | bytes 1474560 | tf_op jit(solution)/shard_map/reduce_scatter | solution.py:228
  169.8 4.5 %collective-permute-start.20 = (f32[6,768]{1,0:T(8,128)}, f32[6,768]{1,0:T(8,128)}, u32[]{:S(2)}, u32[]{:S(2)}) collective-permute-start(f32[6,768]{1,0:T(8,128)} %stack.55), channel_id=1, source_target_pairs={{0,1},{1,0},{2,3},{3,2},{4,5},{5,4},{6,7},{7,6},{8,9},{9,8},{10,11... | collective-permute-start | bytes 55304 | tf_op jit(solution)/shard_map/ppermute | solution.py:20
  174.0 100.0 %reduce-scatter.13.cloned.1.call-start = ((), (), s32[]{:S(2)}) async-start(), calls=%async_computation.9 | async-start | bytes 1515520 | tf_op jit(solution)/shard_map/reduce_scatter | solution.py:228
  197.6 118.3 %all-reduce.4.cloned.1.call-start = ((), (), s32[]{:S(2)}) async-start(), calls=%async_computation.10 | async-start | bytes 1982464 | tf_op jit(solution)/shard_map/psum | solution.py:229
  199.8 2.3 collective-permute-start.17
  200.2 74.5 %collective-permute-start.8 = (bf16[192,256]{1,0:T(8,128)(2,1)S(1)}, bf16[192,256]{1,0:T(8,128)(2,1)S(1)}, u32[]{:S(2)}, u32[]{:S(2)}) collective-permute-start(bf16[192,256]{1,0:T(8,128)(2,1)S(1)} %dynamic-slice_bitcast_fusion), channel_id=1, source_target_pairs={{0,1},{1,0},{2,3},{3,2},{4,5},{5,4},{6,7},{7,6},{8,9},{9,8},{10,11... | collective-permute-start | bytes 294920 | tf_op jit(solution)/shard_map/ppermute | solution.py:20
  274.1 6.8 %collective-permute-start.18 = (bf16[192,512]{1,0:T(8,128)(2,1)S(1)}, bf16[192,512]{1,0:T(8,128)(2,1)S(1)}, u32[]{:S(2)}, u32[]{:S(2)}) collective-permute-start(bf16[192,512]{1,0:T(8,128)(2,1)S(1)} %select_convert_fusion), channel_id=1, source_target_pairs={{0,2},{1,3},{2,0},{3,1},{4,6},{5,7},{6,4},{7,5},{8,10},{9,11},{10,... | collective-permute-start | bytes 589832 | tf_op jit(solution)/shard_map/ppermute | solution.py:20
  274.8 6.9 %collective-permute-start.9 = (bf16[192,512]{1,0:T(8,128)(2,1)S(1)}, bf16[192,512]{1,0:T(8,128)(2,1)S(1)}, u32[]{:S(2)}, u32[]{:S(2)}) collective-permute-start(bf16[192,512]{1,0:T(8,128)(2,1)S(1)} %pad_maximum_fusion.15), channel_id=1, source_target_pairs={{0,0},{1,4},{2,8},{3,12},{4,1},{5,5},{6,9},{7,13},{8,2},{9,6},{10,... | collective-permute-start | bytes 589832 | tf_op jit(solution)/shard_map/ppermute | solution.py:26
  (59 other events, 260.1 us)
Sparse Core Ops, SparseCore 0:
  9.7 36.9 all-gather.4
  76.1 36.8 all-gather.6
  162.1 20.7 reduce-scatter.6
  185.2 27.9 reduce-scatter.10
  215.4 27.8 reduce-scatter.8
  245.6 28.4 reduce-scatter.12
  276.5 39.2 all-reduce.3

commit v2 on v1

--- a/solution.py
+++ b/solution.py
@@ -20,10 +20,28 @@
     return lax.ppermute(value, axis, [(at, at ^ bit) for at in range(size)])
 
 
-def transpose_grid(value):
-    rows, cols = lax.axis_size("row"), lax.axis_size("col")
-    pairs = [(a * cols + b, b * cols + a) for a in range(rows) for b in range(cols)]
-    return lax.ppermute(value, ("row", "col"), pairs)
+def grid_pairs():
+    size = lax.axis_size("row")
+    return [
+        (a * size + b, b * size + (a - b) % size) for a in range(size) for b in range(size)
+    ]
+
+
+def to_slot(value):
+    return lax.ppermute(value, ("row", "col"), grid_pairs())
+
+
+def from_slot(value):
+    return lax.ppermute(value, ("row", "col"), [(b, a) for a, b in grid_pairs()])
+
+
+def from_row(value, away):
+    size = lax.axis_size("row")
+    return lax.ppermute(value, "row", [((a + away) % size, a) for a in range(size)])
+
+
+def after(value, *others):
+    return lax.optimization_barrier((value,) + others)[0]
 
 
 def ordered(flag, own, other, axis):
@@ -89,20 +107,33 @@
         mine = mine.astype(BF16)
         return mine.astype(F32) + swap_bit(mine, "col", 2).astype(F32)
 
+    odd = (lax.axis_index("dp") % 2) == 1
+    x_block = to_slot(layer_in)
     qkv_part = w_qkv.transpose(1, 2, 0).reshape(3 * head_cols, feats)
     vectors = jnp.stack((b_out, ln1_gain, ln1_bias, b_back, ln2_gain, ln2_bias))
-    vectors = jnp.pad(vectors, ((0, 16 - vectors.shape[0]), (0, 0)))
-    x_block = transpose_grid(layer_in)
-    qkv_all = lax.all_gather(qkv_part, "row", axis=0)
-    out_all = lax.all_gather(jnp.concatenate((w_out, vectors)), "row", axis=0)
-    in_all = lax.all_gather(w_in, "row", axis=0, tiled=True)
-    back_all = lax.all_gather(w_back, "row", axis=0, tiled=True)
-    vec_all = out_all[:, head_cols : head_cols + 6].astype(F32)
-    vec_all = vec_all.transpose(1, 0, 2).reshape(6, n_rows * feats, 1)
+    vectors = jnp.pad(vectors, ((0, 32 - vectors.shape[0]), (0, 0)))
+    packed = jnp.concatenate((qkv_part, w_out, vectors))
+    n_half = packed.shape[0] // 2
+    packed_half = jnp.where(odd, packed[n_half:], packed[:n_half])
+    fetched = [from_row(after(packed_half, x_block), k) for k in range(1, n_rows)]
+    swapped = [swap_bit(part, "dp", 1) for part in fetched]
+    packs = [packed] + [ordered(odd, f, o, 0) for f, o in zip(fetched, swapped)]
+    qkv_all = [part[: 3 * head_cols] for part in packs]
+    out_all = [part[3 * head_cols : 4 * head_cols] for part in packs]
+    vec_all = jnp.stack([part[4 * head_cols : 4 * head_cols + 6] for part in packs], axis=1)
+    vec_all = vec_all.reshape(6, n_rows * feats, 1).astype(F32)
     b_out_all, gain_one, shift_one, b_back_all, gain_two, shift_two = [
         vec_all[i] for i in range(6)
     ]
-    out_all = out_all[:, :head_cols]
+    wide_half = after(jnp.where(odd, w_back, w_in), *fetched)
+    fetched = [from_row(wide_half, k) for k in range(1, n_rows)]
+    swapped = [swap_bit(part, "dp", 1) for part in fetched]
+    in_all = jnp.concatenate(
+        [w_in] + [jnp.where(odd, o, f) for f, o in zip(fetched, swapped)]
+    )
+    back_all = jnp.concatenate(
+        [w_back] + [jnp.where(odd, f, o) for f, o in zip(fetched, swapped)]
+    )
 
     pair = ordered(low_bit, x_block, swap_bit(x_block, "col", 1), 0)
     x = ordered(high_bit, pair, swap_bit(pair, "col", 2), 0)
@@ -111,15 +142,15 @@
     first_token = jnp.where(low_bit, half, 0)
     live = (first_token + jnp.arange(half, dtype=jnp.int32)[None, :] < length).astype(F32)
 
-    grad_block = transpose_grid(out_grad.astype(BF16))
+    qkv = sum(
+        dot(qkv_all[b], x[b * feats : (b + 1) * feats], 1, 0) for b in range(n_rows)
+    )
+    grad_block = to_slot(after(out_grad.astype(BF16), qkv))
     grad_pair = ordered(
         low_bit, my_half(grad_block), swap_bit(other_half(grad_block), "col", 1), 0
     )
     grad_out = ordered(high_bit, grad_pair, swap_bit(grad_pair, "col", 2), 0)
 
-    qkv = sum(
-        dot(qkv_all[b], x[b * feats : (b + 1) * feats], 1, 0) for b in range(n_rows)
-    )
     queries = (qkv[:head_cols] + q_bias.astype(F32)[:, None]).astype(BF16)
     keys_in = qkv[head_cols : 2 * head_cols].astype(BF16)
     values = (qkv[2 * head_cols :] + v_bias.astype(F32)[:, None]).astype(BF16)
@@ -217,38 +248,59 @@
     own = jnp.where(high_bit, mine[feats:], mine[:feats])
     away = jnp.where(high_bit, mine[:feats], mine[feats:]).astype(BF16)
     in_grad = own + swap_bit(away, "col", 2).astype(F32)
-    in_grad = transpose_grid(in_grad.astype(BF16)).astype(F32)
-
-    final = final.reshape(n_rows, feats, half)
+    in_grad = from_slot(in_grad.astype(BF16)).astype(F32)
+
+    final = after(final, grad_normed).reshape(n_rows, feats, half)
     own = lax.dynamic_index_in_dim(final, col, 0, False)
     away = lax.dynamic_index_in_dim(final, col ^ 1, 0, False)
-    layer_out = transpose_grid(ordered(low_bit, own, swap_bit(away, "col", 1), 1))
-
-    def reduce_rows(part):
-        kept_rows = lax.psum_scatter(part.astype(BF16), "row", scatter_dimension=0, tiled=True)
-        return lax.psum(kept_rows, "dp").astype(F32)
-
-    w_back_grad = reduce_rows(w_back_part)
-    w_in_grad = reduce_rows(w_in_part)
-    w_out_blocks = w_out_part.reshape(head_cols, n_rows, feats).transpose(1, 0, 2)
-    w_out_grad = reduce_rows(w_out_blocks.reshape(n_rows * head_cols, feats))
+    layer_out = from_slot(ordered(low_bit, own, swap_bit(away, "col", 1), 1))
+
+    def reduce_rows(blocks):
+        rows = blocks[0].shape[0] // 2
+        blocks = jnp.stack(blocks).astype(BF16)
+        keep = jnp.where(odd, blocks[:, rows:], blocks[:, :rows])
+        give = jnp.where(odd, blocks[:, :rows], blocks[:, rows:])
+        keep = keep.astype(F32) + swap_bit(give, "dp", 1).astype(F32)
+        keep = keep.astype(BF16)
+        terms = [keep[0]] + [from_row(keep[k], n_rows - k) for k in range(1, n_rows)]
+        terms = [term.astype(F32) for term in terms]
+        while len(terms) > 1:
+            pairs = len(terms) // 2
+            terms = [terms[i] + terms[i + pairs] for i in range(pairs)]
+        total = terms[0].astype(BF16)
+        bit = 2
+        while bit < lax.axis_size("dp"):
+            total = total.astype(F32) + swap_bit(total, "dp", bit).astype(F32)
+            total = total.astype(BF16)
+            bit *= 2
+        return ordered(odd, total, swap_bit(total, "dp", 1), 0).astype(F32)
+
+    w_back_grad = reduce_rows([w_back_part[b * feats : (b + 1) * feats] for b in range(n_rows)])
+    w_in_grad = reduce_rows([w_in_part[b * feats : (b + 1) * feats] for b in range(n_rows)])
     vector_sums = jnp.stack(
         (ln1_gain_sum, ln1_bias_sum, ln2_gain_sum, ln2_bias_sum, b_out_sum, b_back_sum)
     )
     vector_sums = vector_sums + swap_bit(vector_sums, "col", 1)
-    vector_blocks = vector_sums.reshape(6, n_rows, feats).transpose(1, 0, 2)
     shared = jnp.concatenate((q_bias_sum[None], v_bias_sum[None], b_in_sum.reshape(-1, feats)))
     n_extra = 6 + shared.shape[0]
-    extra = [
-        jnp.concatenate((vector_blocks[b], shared, jnp.zeros((16 - n_extra, feats), F32)))
-        for b in range(n_rows)
-    ]
-    qkv_blocks = []
+    packs = []
     for b in range(n_rows):
-        qkv_blocks += [dot(grad_qkv, x[b * feats : (b + 1) * feats], 1, 1), extra[b]]
-    qkv_sum = reduce_rows(jnp.concatenate(qkv_blocks))
-    w_qkv_grad = qkv_sum[: 3 * head_cols].reshape(3, head_cols, feats).transpose(2, 0, 1)
-    tail = qkv_sum[3 * head_cols :]
+        span = slice(b * feats, (b + 1) * feats)
+        packs += [
+            jnp.concatenate(
+                (
+                    dot(grad_qkv, x[span], 1, 1),
+                    w_out_part[:, span],
+                    vector_sums[:, span],
+                    shared,
+                    jnp.zeros((32 - n_extra, feats), F32),
+                )
+            )
+        ]
+    total = reduce_rows(packs)
+    w_qkv_grad = total[: 3 * head_cols].reshape(3, head_cols, feats).transpose(2, 0, 1)
+    w_out_grad = total[3 * head_cols : 4 * head_cols]
+    tail = total[4 * head_cols :]
     return (
         layer_out,
         in_grad,

time: 334 us -> 287 us (0.86)
  waiting for transfers between devices: 166 us -> 113 us
  blocking collectives: 45.7 us -> 0 us
  starting transfers between devices: 14.5 us -> 52.6 us
  other arithmetic: 22.9 us -> 43.6 us
  local copies, waits for them, and re-layouts: 34.7 us -> 47.9 us
  between operations: 15.3 us -> 2.12 us
  matrix products: 32.1 us -> 22.3 us
    reduce_scatter x4 -> x0, waiting for transfers between devices: 70.4 us -> none  [reduce_rows(): lax.psum_scatter(part.astype(BF16), 'row', scatter_dimension=0, tiled=True)]
    all_gather x2 -> x0, blocking collectives: 45.7 us -> none  [the longest x1 25.2 us: shards(): out_all = lax.all_gather(jnp.concatenate((w_out, vectors)), 'row', axis=0)]
    ppermute x4 -> x19, waiting for transfers between devices: 0.01 us -> 37.2 us  [the longest x15 32.9 us: from_row(): lax.ppermute(value, 'row', [((a + away) % size, a) for a in range(size)])]
    psum x1 -> x0, waiting for transfers between devices: 33.4 us -> none  [reduce_rows(): return lax.psum(kept_rows, 'dp').astype(F32)]
    ppermute x17 -> x29, waiting for transfers between devices: 43.6 us -> 76.3 us  [swap_bit(): return lax.ppermute(value, axis, [(at, at ^ bit) for at in range(size)])]
    ppermute x4 -> x19, starting transfers between devices: 3.78 us -> 32.9 us  [the longest x15 22.5 us: from_row(): lax.ppermute(value, 'row', [((a + away) % size, a) for a in range(size)])]
    all_gather x2 -> x0, waiting for transfers between devices: 18.1 us -> none  [the longest x1 18.1 us: shards(): back_all = lax.all_gather(w_back, 'row', axis=0, tiled=True)]
    ppermute x17 -> x29, starting transfers between devices: 10.2 us -> 19.8 us  [swap_bit(): return lax.ppermute(value, axis, [(at, at ^ bit) for at in range(size)])]
  transfers between devices with their start and end apart: 28 -> 48, of which waited for: 17 -> 26; matrix products, arithmetic and copies ran while one was open for 20% -> 32% of each run, Pallas kernels for 0% -> 0%
where the time goes in v2:
time: 287 us; the launch traced here: 282 us
  waiting for transfers between devices  113 us (39%)
  starting transfers between devices  52.6 us (18%)
  local copies, waits for them, and re-layouts  47.9 us (17%)
  other arithmetic  43.6 us (15%)
  matrix products  22.3 us (8%)
    ppermute x29, waiting for transfers between devices, swap_bit(): return lax.ppermute(value, axis, [(at, at ^ bit) for at in range(size)])  76.3 us
    ppermute x15, waiting for transfers between devices, from_row(): lax.ppermute(value, 'row', [((a + away) % size, a) for a in range(size)])  32.9 us
    ppermute x15, starting transfers between devices, from_row(): lax.ppermute(value, 'row', [((a + away) % size, a) for a in range(size)])  22.5 us
    ppermute x29, starting transfers between devices, swap_bit(): return lax.ppermute(value, axis, [(at, at ^ bit) for at in range(size)])  19.8 us
    dot_general x27, matrix products, dot(): lax.dot_general(left, right, (((left_dim,), (right_dim,)), ((), ())), pre...  16.7 us
    unnamed x162, local copies, waits for them, and re-layouts  12.4 us
    another operation x7, local copies, waits for them, and re-layouts, shards(): jnp.stack([part[4 * head_cols:4 * head_cols + 6] for part in packs], axis=1)  7.61 us
    ppermute x2, starting transfers between devices, to_slot(): return lax.ppermute(value, ('row', 'col'), grid_pairs())  6.37 us
  transfers between devices with their start and end apart: 48, of which 26 were waited for; matrix products, arithmetic and copies ran while one was open for 32% of the time, Pallas kernels for 0%

profile of v2, /device:TPU:20, one launch (start us, length us, event | category | flops | bytes accessed | tf_op | source)
XLA Modules:
  0.0 282.0 jit_solution(12777663954675502548)
XLA Ops:
  11.5 4.3 %collective-permute-start.7 = (bf16[400,192]{0,1:T(8,128)(2,1)S(1)}, bf16[400,192]{0,1:T(8,128)(2,1)S(1)}, u32[]{:S(2)}, u32[]{:S(2)}) collective-permute-start(bf16[400,192]{0,1:T(8,128)(2,1)S(1)} %fusion.47), channel_id=1, source_target_pairs={{12,0},{0,4},{4,8},{8,12},{13,1},{1,5},{5,9},{9,13},{14,2},{2,6},{... | collective-permute-start | bytes 460808 | tf_op jit(solution)/shard_map/ppermute | solution.py:40
  21.9 4.8 %collective-permute-done.5 = bf16[400,192]{0,1:T(8,128)(2,1)S(1)} collective-permute-done((bf16[400,192]{0,1:T(8,128)(2,1)S(1)}, bf16[400,192]{0,1:T(8,128)(2,1)S(1)}, u32[]{:S(2)}, u32[]{:S(2)}) %collective-permute-start.5) | collective-permute-done | bytes 153632 | tf_op jit(solution)/shard_map/ppermute | solution.py:40
  26.8 4.1 %collective-permute-done.3 = bf16[400,192]{0,1:T(8,128)(2,1)S(1)} collective-permute-done((bf16[400,192]{0,1:T(8,128)(2,1)S(1)}, bf16[400,192]{0,1:T(8,128)(2,1)S(1)}, u32[]{:S(2)}, u32[]{:S(2)}) %collective-permute-start.3) | collective-permute-done | bytes 153632 | tf_op jit(solution)/shard_map/ppermute | solution.py:40
  37.0 5.7 %collective-permute-done.8 = bf16[400,192]{0,1:T(8,128)(2,1)S(1)} collective-permute-done((bf16[400,192]{0,1:T(8,128)(2,1)S(1)}, bf16[400,192]{0,1:T(8,128)(2,1)S(1)}, u32[]{:S(2)}, u32[]{:S(2)}) %collective-permute-start.8) | collective-permute-done | bytes 153632 | tf_op jit(solution)/shard_map/ppermute | solution.py:20
  44.2 2.7 collective-permute-done.6
  47.0 2.6 collective-permute-done.4
  49.6 5.4 %collective-permute-done.2 = bf16[384,512]{1,0:T(8,128)(2,1)S(1)} collective-permute-done((bf16[384,512]{1,0:T(8,128)(2,1)S(1)}, bf16[384,512]{1,0:T(8,128)(2,1)S(1)}, u32[]{:S(2)}, u32[]{:S(2)}) %collective-permute-start.2) | collective-permute-done | bytes 393248 | tf_op jit(solution)/shard_map/ppermute | solution.py:20
  56.8 2.9 %fusion.105 = (f32[3,512]{1,0:T(4,128)S(1)}, f32[3,512,512]{2,1,0:T(8,128)}) fusion(pred[512]{0:T(512)(128)(4,1)S(1)} %iota_compare_fusion, bf16[3,64,512]{2,1,0:T(8,128)(2,1)S(1)} %bitcast.166, bf16[3,64,512]{2,1,0:T(8,128)(2,1)S(1)} %bitcast.168), kind=kOutput, calls=%fused_computation.292 | convolution fusion | flops 103809536 | bytes 3545600 | tf_op jit(solution)/shard_map/sub | solution.py:167
  79.1 3.8 %collective-permute-start.20 = (bf16[192,512]{1,0:T(8,128)(2,1)}, bf16[192,512]{1,0:T(8,128)(2,1)S(1)}, u32[]{:S(2)}, u32[]{:S(2)}) collective-permute-start(bf16[192,512]{1,0:T(8,128)(2,1)} %convert_element_type.269), channel_id=1, source_target_pairs={{0,0},{1,7},{2,10},{3,13},{4,1},{5,4},{6,11},{7,14},{8,2},{9,5},{1... | collective-permute-start | bytes 589832 | tf_op jit(solution)/shard_map/ppermute | solution.py:31
  84.0 3.4 %collective-permute-done.10 = bf16[768,256]{1,0:T(8,128)(2,1)S(1)} collective-permute-done((bf16[768,256]{1,0:T(8,128)(2,1)}, bf16[768,256]{1,0:T(8,128)(2,1)S(1)}, u32[]{:S(2)}, u32[]{:S(2)}) %collective-permute-start.10) | collective-permute-done | bytes 393248 | tf_op jit(solution)/shard_map/ppermute | solution.py:20
  90.4 4.3 %collective-permute-done.12 = bf16[192,768]{1,0:T(8,128)(2,1)S(1)} collective-permute-done((bf16[192,768]{1,0:T(8,128)(2,1)}, bf16[192,768]{1,0:T(8,128)(2,1)S(1)}, u32[]{:S(2)}, u32[]{:S(2)}) %collective-permute-start.12) | collective-permute-done | bytes 294944 | tf_op jit(solution)/shard_map/ppermute | solution.py:20
  110.7 6.6 %collective-permute-done.19 = bf16[768,256]{1,0:T(8,128)(2,1)} collective-permute-done((bf16[768,256]{1,0:T(8,128)(2,1)S(1)}, bf16[768,256]{1,0:T(8,128)(2,1)}, u32[]{:S(2)}, u32[]{:S(2)}) %collective-permute-start.19) | collective-permute-done | bytes 393248 | tf_op jit(solution)/shard_map/ppermute | solution.py:20
  142.1 7.7 %collective-permute-done.43 = bf16[4,96,768]{2,1,0:T(8,128)(2,1)} collective-permute-done((bf16[4,96,768]{2,1,0:T(8,128)(2,1)}, bf16[4,96,768]{2,1,0:T(8,128)(2,1)}, u32[]{:S(2)}, u32[]{:S(2)}) %collective-permute-start.43) | collective-permute-done | bytes 589856 | tf_op jit(solution)/shard_map/ppermute | solution.py:20
  156.0 6.1 %collective-permute-done.38 = bf16[4,96,768]{2,1,0:T(8,128)(2,1)} collective-permute-done((bf16[4,96,768]{2,1,0:T(8,128)(2,1)}, bf16[4,96,768]{2,1,0:T(8,128)(2,1)}, u32[]{:S(2)}, u32[]{:S(2)}) %collective-permute-start.38) | collective-permute-done | bytes 589856 | tf_op jit(solution)/shard_map/ppermute | solution.py:20
  167.9 4.8 %collective-permute-done.45 = bf16[96,768]{1,0:T(8,128)(2,1)S(1)} collective-permute-done((bf16[96,768]{1,0:T(8,128)(2,1)S(1)}, bf16[96,768]{1,0:T(8,128)(2,1)S(1)}, u32[]{:S(2)}, u32[]{:S(2)}) %collective-permute-start.45) | collective-permute-done | bytes 147488 | tf_op jit(solution)/shard_map/ppermute | solution.py:40
  174.7 4.0 %collective-permute-done.41 = bf16[96,768]{1,0:T(8,128)(2,1)S(1)} collective-permute-done((bf16[96,768]{1,0:T(8,128)(2,1)S(1)}, bf16[96,768]{1,0:T(8,128)(2,1)S(1)}, u32[]{:S(2)}, u32[]{:S(2)}) %collective-permute-start.41) | collective-permute-done | bytes 147488 | tf_op jit(solution)/shard_map/ppermute | solution.py:40
  182.6 3.0 %collective-permute-done.42 = bf16[96,768]{1,0:T(8,128)(2,1)S(1)} collective-permute-done((bf16[96,768]{1,0:T(8,128)(2,1)S(1)}, bf16[96,768]{1,0:T(8,128)(2,1)S(1)}, u32[]{:S(2)}, u32[]{:S(2)}) %collective-permute-start.42) | collective-permute-done | bytes 147488 | tf_op jit(solution)/shard_map/ppermute | solution.py:20
  186.4 5.9 %collective-permute-done.25 = bf16[768,256]{1,0:T(8,128)(2,1)S(1)} collective-permute-done((bf16[768,256]{1,0:T(8,128)(2,1)S(1)}, bf16[768,256]{1,0:T(8,128)(2,1)S(1)}, u32[]{:S(2)}, u32[]{:S(2)}) %collective-permute-start.25) | collective-permute-done | bytes 393248 | tf_op jit(solution)/shard_map/ppermute | solution.py:20
  228.6 15.1 %collective-permute-done.33 = bf16[4,400,192]{1,2,0:T(8,128)(2,1)S(1)} collective-permute-done((bf16[4,400,192]{1,2,0:T(8,128)(2,1)S(1)}, bf16[4,400,192]{1,2,0:T(8,128)(2,1)S(1)}, u32[]{:S(2)}, u32[]{:S(2)}) %collective-permute-start.33) | collective-permute-done | bytes 614432 | tf_op jit(solution)/shard_map/ppermute | solution.py:20
  244.5 3.1 %collective-permute-start.36 = (bf16[400,192]{0,1:T(8,128)(2,1)S(1)}, bf16[400,192]{0,1:T(8,128)(2,1)S(1)}, u32[]{:S(2)}, u32[]{:S(2)}) collective-permute-start(bf16[400,192]{0,1:T(8,128)(2,1)S(1)} %get-tuple-element.107), channel_id=1, source_target_pairs={{4,0},{8,4},{12,8},{0,12},{5,1},{9,5},{13,9},{1,13},{6,2},{10,6},{... | collective-permute-start | bytes 460808 | tf_op jit(solution)/shard_map/ppermute | solution.py:40
  249.3 4.6 %collective-permute-done.34 = bf16[400,192]{0,1:T(8,128)(2,1)S(1)} collective-permute-done((bf16[400,192]{0,1:T(8,128)(2,1)S(1)}, bf16[400,192]{0,1:T(8,128)(2,1)S(1)}, u32[]{:S(2)}, u32[]{:S(2)}) %collective-permute-start.34) | collective-permute-done | bytes 153632 | tf_op jit(solution)/shard_map/ppermute | solution.py:40
  253.8 8.1 %collective-permute-done.36 = bf16[400,192]{0,1:T(8,128)(2,1)S(1)} collective-permute-done((bf16[400,192]{0,1:T(8,128)(2,1)S(1)}, bf16[400,192]{0,1:T(8,128)(2,1)S(1)}, u32[]{:S(2)}, u32[]{:S(2)}) %collective-permute-start.36) | collective-permute-done | bytes 153632 | tf_op jit(solution)/shard_map/ppermute | solution.py:40
  264.9 4.4 %collective-permute-done.37 = bf16[400,192]{0,1:T(8,128)(2,1)S(1)} collective-permute-done((bf16[400,192]{0,1:T(8,128)(2,1)S(1)}, bf16[400,192]{0,1:T(8,128)(2,1)S(1)}, u32[]{:S(2)}, u32[]{:S(2)}) %collective-permute-start.37) | collective-permute-done | bytes 153632 | tf_op jit(solution)/shard_map/ppermute | solution.py:20
  276.9 2.7 collective-permute-done.31
  (400 shorter events, 160.0 us)
Async XLA Ops:
  15.8 15.1 %collective-permute-start.3 = (bf16[400,192]{0,1:T(8,128)(2,1)S(1)}, bf16[400,192]{0,1:T(8,128)(2,1)S(1)}, u32[]{:S(2)}, u32[]{:S(2)}) collective-permute-start(bf16[400,192]{0,1:T(8,128)(2,1)S(1)} %fusion.47), channel_id=1, source_target_pairs={{4,0},{8,4},{12,8},{0,12},{5,1},{9,5},{13,9},{1,13},{6,2},{10,6},{... | collective-permute-start | bytes 460808 | tf_op jit(solution)/shard_map/ppermute | solution.py:40
  18.0 18.4 %collective-permute-start.1 = (bf16[192,512]{1,0:T(8,128)(2,1)S(1)}, bf16[192,512]{1,0:T(8,128)(2,1)S(1)}, u32[]{:S(2)}, u32[]{:S(2)}) collective-permute-start(bf16[192,512]{1,0:T(8,128)(2,1)S(1)} %collective-permute-done), channel_id=1, source_target_pairs={{0,1},{1,0},{2,3},{3,2},{4,5},{5,4},{6,7},{7,6},{8,9},{9,8},{10,11... | collective-permute-start | bytes 589832 | tf_op jit(solution)/shard_map/ppermute | solution.py:20
  30.9 41.5 %collective-permute-start.15 = (bf16[192,768]{1,0:T(8,128)(2,1)}, bf16[192,768]{1,0:T(8,128)(2,1)}, u32[]{:S(2)}, u32[]{:S(2)}) collective-permute-start(bf16[192,768]{1,0:T(8,128)(2,1)} %broadcast_select_fusion.17), channel_id=1, source_target_pairs={{12,0},{0,4},{4,8},{8,12},{13,1},{1,5},{5,9},{9,13},{14,2},{2,6},{... | collective-permute-start | bytes 884744 | tf_op jit(solution)/shard_map/ppermute | solution.py:40
  33.4 43.6 %collective-permute-start.13 = (bf16[192,768]{1,0:T(8,128)(2,1)}, bf16[192,768]{1,0:T(8,128)(2,1)}, u32[]{:S(2)}, u32[]{:S(2)}) collective-permute-start(bf16[192,768]{1,0:T(8,128)(2,1)} %broadcast_select_fusion.17), channel_id=1, source_target_pairs={{8,0},{12,4},{0,8},{4,12},{9,1},{13,5},{1,9},{5,13},{10,2},{14,6},... | collective-permute-start | bytes 884744 | tf_op jit(solution)/shard_map/ppermute | solution.py:40
  34.8 42.7 %collective-permute-start.11 = (bf16[192,768]{1,0:T(8,128)(2,1)}, bf16[192,768]{1,0:T(8,128)(2,1)}, u32[]{:S(2)}, u32[]{:S(2)}) collective-permute-start(bf16[192,768]{1,0:T(8,128)(2,1)} %broadcast_select_fusion.17), channel_id=1, source_target_pairs={{4,0},{8,4},{12,8},{0,12},{5,1},{9,5},{13,9},{1,13},{6,2},{10,6},{... | collective-permute-start | bytes 884744 | tf_op jit(solution)/shard_map/ppermute | solution.py:40
  75.9 11.5 %collective-permute-start.10 = (bf16[768,256]{1,0:T(8,128)(2,1)}, bf16[768,256]{1,0:T(8,128)(2,1)S(1)}, u32[]{:S(2)}, u32[]{:S(2)}) collective-permute-start(bf16[768,256]{1,0:T(8,128)(2,1)} %add_convert_fusion.5), channel_id=1, source_target_pairs={{0,2},{1,3},{2,0},{3,1},{4,6},{5,7},{6,4},{7,5},{8,10},{9,11},{10,... | collective-permute-start | bytes 1179656 | tf_op jit(solution)/shard_map/ppermute | solution.py:20
  77.0 12.3 %collective-permute-start.14 = (bf16[192,768]{1,0:T(8,128)(2,1)}, bf16[192,768]{1,0:T(8,128)(2,1)S(1)}, u32[]{:S(2)}, u32[]{:S(2)}) collective-permute-start(bf16[192,768]{1,0:T(8,128)(2,1)} %collective-permute-done.13), channel_id=1, source_target_pairs={{0,16},{16,0},{1,17},{17,1},{2,18},{18,2},{3,19},{19,3},{4,20},{20... | collective-permute-start | bytes 884744 | tf_op jit(solution)/shard_map/ppermute | solution.py:20
  77.6 17.1 %collective-permute-start.12 = (bf16[192,768]{1,0:T(8,128)(2,1)}, bf16[192,768]{1,0:T(8,128)(2,1)S(1)}, u32[]{:S(2)}, u32[]{:S(2)}) collective-permute-start(bf16[192,768]{1,0:T(8,128)(2,1)} %collective-permute-done.11), channel_id=1, source_target_pairs={{0,16},{16,0},{1,17},{17,1},{2,18},{18,2},{3,19},{19,3},{4,20},{20... | collective-permute-start | bytes 884744 | tf_op jit(solution)/shard_map/ppermute | solution.py:20
  79.1 20.3 %collective-permute-start.20 = (bf16[192,512]{1,0:T(8,128)(2,1)}, bf16[192,512]{1,0:T(8,128)(2,1)S(1)}, u32[]{:S(2)}, u32[]{:S(2)}) collective-permute-start(bf16[192,512]{1,0:T(8,128)(2,1)} %convert_element_type.269), channel_id=1, source_target_pairs={{0,0},{1,7},{2,10},{3,13},{4,1},{5,4},{6,11},{7,14},{8,2},{9,5},{1... | collective-permute-start | bytes 589832 | tf_op jit(solution)/shard_map/ppermute | solution.py:31
  102.3 15.0 %collective-permute-start.19 = (bf16[768,256]{1,0:T(8,128)(2,1)S(1)}, bf16[768,256]{1,0:T(8,128)(2,1)}, u32[]{:S(2)}, u32[]{:S(2)}) collective-permute-start(bf16[768,256]{1,0:T(8,128)(2,1)S(1)} %add_convert_fusion.4), channel_id=1, source_target_pairs={{0,2},{1,3},{2,0},{3,1},{4,6},{5,7},{6,4},{7,5},{8,10},{9,11},{10,... | collective-permute-start | bytes 1179656 | tf_op jit(solution)/shard_map/ppermute | solution.py:20
  133.4 16.4 %collective-permute-start.43 = (bf16[4,96,768]{2,1,0:T(8,128)(2,1)}, bf16[4,96,768]{2,1,0:T(8,128)(2,1)}, u32[]{:S(2)}, u32[]{:S(2)}) collective-permute-start(bf16[4,96,768]{2,1,0:T(8,128)(2,1)} %broadcast_select_fusion.1), channel_id=1, source_target_pairs={{0,16},{16,0},{1,17},{17,1},{2,18},{18,2},{3,19},{19,3},{4,20},{20... | collective-permute-start | bytes 1769480 | tf_op jit(solution)/shard_map/ppermute | solution.py:20
  137.0 25.1 %collective-permute-start.38 = (bf16[4,96,768]{2,1,0:T(8,128)(2,1)}, bf16[4,96,768]{2,1,0:T(8,128)(2,1)}, u32[]{:S(2)}, u32[]{:S(2)}) collective-permute-start(bf16[4,96,768]{2,1,0:T(8,128)(2,1)} %broadcast_select_fusion.2), channel_id=1, source_target_pairs={{0,16},{16,0},{1,17},{17,1},{2,18},{18,2},{3,19},{19,3},{4,20},{20... | collective-permute-start | bytes 1769480 | tf_op jit(solution)/shard_map/ppermute | solution.py:20
  142.1 39.2 %collective-permute-start.24 = (f32[768,256]{1,0:T(8,128)}, f32[768,256]{1,0:T(8,128)S(1)}, u32[]{:S(2)}, u32[]{:S(2)}) collective-permute-start(f32[768,256]{1,0:T(8,128)} %slice_select_fusion), channel_id=1, source_target_pairs={{0,1},{1,0},{2,3},{3,2},{4,5},{5,4},{6,7},{7,6},{8,9},{9,8},{10,11... | collective-permute-start | bytes 2359304 | tf_op jit(solution)/shard_map/ppermute | solution.py:20
  151.5 14.4 %collective-permute-start.44 = (bf16[96,768]{1,0:T(8,128)(2,1)S(1)}, bf16[96,768]{1,0:T(8,128)(2,1)S(1)}, u32[]{:S(2)}, u32[]{:S(2)}) collective-permute-start(bf16[96,768]{1,0:T(8,128)(2,1)S(1)} %get-tuple-element.120), channel_id=1, source_target_pairs={{8,0},{12,4},{0,8},{4,12},{9,1},{13,5},{1,9},{5,13},{10,2},{14,6},... | collective-permute-start | bytes 442376 | tf_op jit(solution)/shard_map/ppermute | solution.py:40
  154.0 12.8 %collective-permute-start.46 = (bf16[96,768]{1,0:T(8,128)(2,1)S(1)}, bf16[96,768]{1,0:T(8,128)(2,1)S(1)}, u32[]{:S(2)}, u32[]{:S(2)}) collective-permute-start(bf16[96,768]{1,0:T(8,128)(2,1)S(1)} %get-tuple-element.121), channel_id=1, source_target_pairs={{4,0},{8,4},{12,8},{0,12},{5,1},{9,5},{13,9},{1,13},{6,2},{10,6},{... | collective-permute-start | bytes 442376 | tf_op jit(solution)/shard_map/ppermute | solution.py:40
  154.8 17.9 %collective-permute-start.45 = (bf16[96,768]{1,0:T(8,128)(2,1)S(1)}, bf16[96,768]{1,0:T(8,128)(2,1)S(1)}, u32[]{:S(2)}, u32[]{:S(2)}) collective-permute-start(bf16[96,768]{1,0:T(8,128)(2,1)S(1)} %get-tuple-element.122), channel_id=1, source_target_pairs={{12,0},{0,4},{4,8},{8,12},{13,1},{1,5},{5,9},{9,13},{14,2},{2,6},{... | collective-permute-start | bytes 442376 | tf_op jit(solution)/shard_map/ppermute | solution.py:40
  163.4 11.3 %collective-permute-start.39 = (bf16[96,768]{1,0:T(8,128)(2,1)S(1)}, bf16[96,768]{1,0:T(8,128)(2,1)S(1)}, u32[]{:S(2)}, u32[]{:S(2)}) collective-permute-start(bf16[96,768]{1,0:T(8,128)(2,1)S(1)} %get-tuple-element.123), channel_id=1, source_target_pairs={{8,0},{12,4},{0,8},{4,12},{9,1},{13,5},{1,9},{5,13},{10,2},{14,6},... | collective-permute-start | bytes 442376 | tf_op jit(solution)/shard_map/ppermute | solution.py:40
  165.9 12.8 %collective-permute-start.41 = (bf16[96,768]{1,0:T(8,128)(2,1)S(1)}, bf16[96,768]{1,0:T(8,128)(2,1)S(1)}, u32[]{:S(2)}, u32[]{:S(2)}) collective-permute-start(bf16[96,768]{1,0:T(8,128)(2,1)S(1)} %get-tuple-element.124), channel_id=1, source_target_pairs={{4,0},{8,4},{12,8},{0,12},{5,1},{9,5},{13,9},{1,13},{6,2},{10,6},{... | collective-permute-start | bytes 442376 | tf_op jit(solution)/shard_map/ppermute | solution.py:40
  166.8 13.0 %collective-permute-start.40 = (bf16[96,768]{1,0:T(8,128)(2,1)S(1)}, bf16[96,768]{1,0:T(8,128)(2,1)S(1)}, u32[]{:S(2)}, u32[]{:S(2)}) collective-permute-start(bf16[96,768]{1,0:T(8,128)(2,1)S(1)} %get-tuple-element.125), channel_id=1, source_target_pairs={{12,0},{0,4},{4,8},{8,12},{13,1},{1,5},{5,9},{9,13},{14,2},{2,6},{... | collective-permute-start | bytes 442376 | tf_op jit(solution)/shard_map/ppermute | solution.py:40
  202.2 47.1 %collective-permute-start.27 = (bf16[192,512]{1,0:T(8,128)(2,1)}, bf16[192,512]{1,0:T(8,128)(2,1)}, u32[]{:S(2)}, u32[]{:S(2)}) collective-permute-start(bf16[192,512]{1,0:T(8,128)(2,1)} %pad_maximum_fusion.30), channel_id=1, source_target_pairs={{0,0},{7,1},{10,2},{13,3},{1,4},{4,5},{11,6},{14,7},{2,8},{5,9},{8... | collective-permute-start | bytes 589832 | tf_op jit(solution)/shard_map/ppermute | solution.py:35
  223.6 20.1 %collective-permute-start.33 = (bf16[4,400,192]{1,2,0:T(8,128)(2,1)S(1)}, bf16[4,400,192]{1,2,0:T(8,128)(2,1)S(1)}, u32[]{:S(2)}, u32[]{:S(2)}) collective-permute-start(bf16[4,400,192]{1,2,0:T(8,128)(2,1)S(1)} %broadcast_select_fusion), channel_id=1, source_target_pairs={{0,16},{16,0},{1,17},{17,1},{2,18},{18,2},{3,19},{19,3},{4,20},{20... | collective-permute-start | bytes 1843208 | tf_op jit(solution)/shard_map/ppermute | solution.py:20
  227.1 37.3 %collective-permute-start.29 = (f32[384,512]{1,0:T(8,128)S(1)}, f32[384,512]{1,0:T(8,128)S(1)}, u32[]{:S(2)}, u32[]{:S(2)}) collective-permute-start(f32[384,512]{1,0:T(8,128)S(1)} %fusion.25), channel_id=1, source_target_pairs={{0,1},{1,0},{2,3},{3,2},{4,5},{5,4},{6,7},{7,6},{8,9},{9,8},{10,11... | collective-permute-start | bytes 2359304 | tf_op jit(solution)/shard_map/ppermute | solution.py:20
  244.5 17.4 %collective-permute-start.36 = (bf16[400,192]{0,1:T(8,128)(2,1)S(1)}, bf16[400,192]{0,1:T(8,128)(2,1)S(1)}, u32[]{:S(2)}, u32[]{:S(2)}) collective-permute-start(bf16[400,192]{0,1:T(8,128)(2,1)S(1)} %get-tuple-element.107), channel_id=1, source_target_pairs={{4,0},{8,4},{12,8},{0,12},{5,1},{9,5},{13,9},{1,13},{6,2},{10,6},{... | collective-permute-start | bytes 460808 | tf_op jit(solution)/shard_map/ppermute | solution.py:40
  247.5 15.9 %collective-permute-start.35 = (bf16[400,192]{0,1:T(8,128)(2,1)S(1)}, bf16[400,192]{0,1:T(8,128)(2,1)S(1)}, u32[]{:S(2)}, u32[]{:S(2)}) collective-permute-start(bf16[400,192]{0,1:T(8,128)(2,1)S(1)} %get-tuple-element.108), channel_id=1, source_target_pairs={{12,0},{0,4},{4,8},{8,12},{13,1},{1,5},{5,9},{9,13},{14,2},{2,6},{... | collective-permute-start | bytes 460808 | tf_op jit(solution)/shard_map/ppermute | solution.py:40
  (103 other events, 649.2 us)

commit v3 on v2

v3 whole, which is shorter than its diff:
```python
import jax
import jax.numpy as jnp
from jax import lax
from jax.experimental import pallas as pl
from jax.experimental.pallas import tpu as pltpu
from jax.sharding import PartitionSpec as P

HEAD_DIM = 64
EPSILON = 1e-12
F32 = jnp.float32
BF16 = jnp.bfloat16
EXTRA = 32


def dot(left, right, left_dim, right_dim):
    return lax.dot_general(
        left, right, (((left_dim,), (right_dim,)), ((), ())), preferred_element_type=F32
    )


def call(kernel, name, outs, args, flops=0, scratch=(), specs=None):
    vmem = pl.BlockSpec(memory_space=pltpu.VMEM)
    in_specs = [
        pl.BlockSpec(memory_space=pltpu.SMEM) if arg.dtype == jnp.int32 else vmem for arg in args
    ]
    for at, spec in (specs or {}).items():
        in_specs[at] = spec
    moved = sum(arg.size * arg.dtype.itemsize for arg in args)
    moved += sum(out.size * out.dtype.itemsize for out in outs)
    return pl.pallas_call(
        kernel,
        name=name,
        out_shape=outs,
        grid=(1,) if specs else (),
        in_specs=in_specs,
        out_specs=[vmem] * len(outs),
        scratch_shapes=list(scratch),
        compiler_params=pltpu.CompilerParams(vmem_limit_bytes=32 * 1024 * 1024),
        cost_estimate=pl.CostEstimate(flops=flops, bytes_accessed=moved, transcendentals=0),
    )(*args)


def shape(dims, dtype):
    return jax.ShapeDtypeStruct(dims, dtype)


def swap_bit(value, axis, bit):
    size = lax.axis_size(axis)
    return lax.ppermute(value, axis, [(at, at ^ bit) for at in range(size)])


def grid_pairs():
    size = lax.axis_size("row")
    return [
        (a * size + b, b * size + (a - b) % size) for a in range(size) for b in range(size)
    ]


def to_slot(value):
    return lax.ppermute(value, ("row", "col"), grid_pairs())


def from_slot(value):
    return lax.ppermute(value, ("row", "col"), [(b, a) for a, b in grid_pairs()])


def from_row(value, away):
    size = lax.axis_size("row")
    return lax.ppermute(value, "row", [((a + away) % size, a) for a in range(size)])


def after(value, *others):
    return lax.optimization_barrier((value,) + others)[0]


def ordered(flag, own, other, axis):
    return jnp.concatenate(
        (jnp.where(flag, other, own), jnp.where(flag, own, other)), axis=axis
    )


def row_sums(products):
    total = 0.0
    for at, product in products.items():
        pick = lax.broadcasted_iota(jnp.int32, (8, product.shape[1]), 0) == at
        pick = pick.astype(BF16)
        high = product.astype(BF16)
        rest = (product - high.astype(F32)).astype(BF16)
        total = total + dot(pick, high, 1, 1) + dot(pick, rest, 1, 1)
    return total


def attend_kernel(
    flags, x0, x1, x2, x3, w_qkv, w_out, f1, f2, f3, s1, s2, s3, bias,
    xs, packs, qkv, prob, context, mine, other,
):
    low, odd, col, length = flags[0], flags[1], flags[2], flags[3]
    feats, slot = x0.shape
    half = slot // 2
    width = w_out.shape[0]
    n_half = f1.shape[0]
    for bit, ref in enumerate((x0, x1, x2, x3)):
        rows = pl.ds(pl.multiple_of((col ^ bit) * feats, feats), feats)

        @pl.when(low == 0)
        def _():
            xs[rows, :] = ref[...]

        @pl.when(low == 1)
        def _():
            xs[rows, :half] = ref[:, half:]
            xs[rows, half:] = ref[:, :half]

    packs[0, : 3 * width] = w_qkv[...]
    packs[0, 3 * width :] = w_out[...]
    for k, (f, s) in enumerate(((f1, s1), (f2, s2), (f3, s3))):

        @pl.when(odd == 0)
        def _():
            packs[k + 1, :n_half] = f[...]
            packs[k + 1, n_half:] = s[...]

        @pl.when(odd == 1)
        def _():
            packs[k + 1, :n_half] = s[...]
            packs[k + 1, n_half:] = f[...]

    for part in range(3):
        rows = slice(part * width, (part + 1) * width)
        total = 0.0
        for k in range(4):
            total = total + dot(packs[k, rows], xs[k * feats : (k + 1) * feats], 1, 0)
        qkv[rows] = (total + bias[rows]).astype(BF16)

    place = lax.broadcasted_iota(jnp.int32, (slot, half), 0)
    place = jnp.where(low == 1, (place + half) % slot, place)
    live = place < length
    scale = HEAD_DIM ** (-0.5)
    for h in range(width // HEAD_DIM):
        q_rows = pl.ds(h * HEAD_DIM, HEAD_DIM)
        k_rows = pl.ds(width + h * HEAD_DIM, HEAD_DIM)
        v_rows = pl.ds(2 * width + h * HEAD_DIM, HEAD_DIM)
        for part in range(2):
            cols = slice(part * half, (part + 1) * half)
            scores = dot(qkv[k_rows, :], qkv[q_rows, cols], 0, 0) * scale
            scores = jnp.where(live, scores, -1000000000.0)
            exponent = jnp.exp(scores - jnp.max(scores, axis=0, keepdims=True))
            inverse = 1.0 / jnp.sum(exponent, axis=0, keepdims=True)
            weights = (exponent * inverse).astype(BF16)
            prob[h, :, cols] = weights
            context[q_rows, cols] = dot(qkv[v_rows, :], weights, 1, 0).astype(BF16)

    for k in range(4):
        rows = slice(k * feats, (k + 1) * feats)
        part = dot(packs[k, 3 * width :], context[...], 0, 0)
        mine[rows] = part[:, :half]
        other[rows] = part[:, half:].astype(BF16)


def vector_kernel(v0, v1, v2, v3, out):
    feats = out.shape[0] // 4
    eye = (
        lax.broadcasted_iota(jnp.int32, (feats, feats), 0)
        == lax.broadcasted_iota(jnp.int32, (feats, feats), 1)
    ).astype(BF16)
    for k, ref in enumerate((v0, v1, v2, v3)):
        out[k * feats : (k + 1) * feats] = dot(eye, ref[:, :feats], 1, 1)


def norm_kernel(x, own, away, vecs, scaled, inverse, low_normed):
    first = x[...].astype(F32) + own[...].astype(F32) + away[...].astype(F32) + vecs[:, 0:1]
    center = jnp.mean(first, axis=0, keepdims=True)
    first = first - center
    inv = lax.rsqrt(jnp.mean(first * first, axis=0, keepdims=True) + EPSILON)
    first = first * inv
    scaled[...] = first
    inverse[...] = jnp.broadcast_to(inv, inverse.shape)
    low_normed[...] = (first * vecs[:, 1:2] + vecs[:, 2:3]).astype(BF16)


def forward_kernel(n_own, n_away, w_in, w_back, bias, hidden, slope, mine, other):
    half = n_own.shape[1]
    step = 256
    for part, ref in enumerate((n_own, n_away)):
        cols = slice(part * half, (part + 1) * half)
        for at in range(0, w_in.shape[1], step):
            rows = slice(at, at + step)
            pre = dot(w_in[:, rows], ref[...], 0, 0) + bias[rows]
            share = 0.5 * (1.0 + lax.erf(pre * (0.5**0.5)))
            hidden[rows, cols] = (pre * share).astype(BF16)
            bell = jnp.exp(-0.5 * pre * pre) * ((0.5 / jnp.pi) ** 0.5)
            slope[rows, cols] = (share + pre * bell).astype(BF16)
    mine[...] = dot(w_back[...], hidden[:, :half], 1, 0)
    other[...] = dot(w_back[...], hidden[:, half:], 1, 0).astype(BF16)


def turn_kernel(
    flags, scaled_one, own, away, vecs, g_own, g_high, g_low,
    keep, give, grad_second, grad_returned, sums, final, grad,
):
    low, col, length = flags[0], flags[2], flags[3]
    feats = g_own.shape[0]
    half = own.shape[1]

    def rows(bit):
        return pl.ds(pl.multiple_of((col ^ bit) * feats, feats), feats)

    for bit, ref in ((0, g_own), (2, g_high)):

        @pl.when(low == 0)
        def _():
            grad[rows(bit), :] = ref[:, :half]

        @pl.when(low == 1)
        def _():
            grad[rows(bit), :] = ref[:, half:]

    grad[rows(1), :] = g_low[:feats]
    grad[rows(3), :] = g_low[feats:]

    normed = scaled_one[...] * vecs[:, 1:2] + vecs[:, 2:3]
    second = normed + own[...].astype(F32) + away[...].astype(F32) + vecs[:, 3:4]
    second = second - jnp.mean(second, axis=0, keepdims=True)
    inv = lax.rsqrt(jnp.mean(second * second, axis=0, keepdims=True) + EPSILON)
    scaled = second * inv
    place = low * half + lax.broadcasted_iota(jnp.int32, (1, half), 1)
    live = (place < length).astype(F32)
    final[...] = ((scaled * vecs[:, 4:5] + vecs[:, 5:6]) * live).astype(BF16)
    keep[...] = final[rows(0), :]
    give[...] = final[rows(1), :]
    upstream = grad[...].astype(F32) * live
    weighted = upstream * vecs[:, 4:5]
    mean = jnp.mean(weighted, axis=0, keepdims=True)
    tilt = jnp.mean(weighted * scaled, axis=0, keepdims=True)
    back = inv * (weighted - mean - scaled * tilt)
    grad_second[...] = back
    grad_returned[...] = back.astype(BF16)
    sums[...] = row_sums({2: upstream * scaled, 3: upstream, 5: back})


def backward_kernel(r_own, r_away, slope, w_in, w_back, mine, other, grad_pre, b_in_sums):
    half = r_own.shape[1]
    step = 256
    for part, ref in enumerate((r_own, r_away)):
        cols = slice(part * half, (part + 1) * half)
        for at in range(0, w_in.shape[1], step):
            rows = slice(at, at + step)
            grad_hidden = dot(w_back[:, rows], ref[...], 0, 0)
            grad_pre[rows, cols] = (grad_hidden * slope[rows, cols].astype(F32)).astype(BF16)
    mine[...] = dot(w_in[...], grad_pre[:, :half], 1, 0)
    other[...] = dot(w_in[...], grad_pre[:, half:], 1, 0).astype(BF16)
    size = b_in_sums.shape[1]
    total = 0.0
    for k in range(w_in.shape[1] // size):
        pick = lax.broadcasted_iota(jnp.int32, (8, 2 * half), 0) == k
        total = total + dot(pick.astype(BF16), grad_pre[k * size : (k + 1) * size], 1, 1)
    b_in_sums[...] = total


def wide_grad_kernel(r_own, r_away, hidden, n_own, n_away, grad_pre, *outs):
    half = r_own.shape[1]
    feats = outs[0].shape[0]
    for k in range(4):
        rows = slice(k * feats, (k + 1) * feats)
        for out, own, away, right in (
            (outs[k], r_own, r_away, hidden),
            (outs[4 + k], n_own, n_away, grad_pre),
        ):
            total = dot(own[rows], right[:, :half], 1, 1)
            out[...] = (total + dot(away[rows], right[:, half:], 1, 1)).astype(BF16)


def norm_back_kernel(
    own, away, grad_second, scaled, inverse, vecs, sums, grad_first, low_first, sums_out
):
    upstream = grad_second[...] + own[...].astype(F32) + away[...].astype(F32)
    weighted = upstream * vecs[:, 1:2]
    mean = jnp.mean(weighted, axis=0, keepdims=True)
    tilt = jnp.mean(weighted * scaled[...], axis=0, keepdims=True)
    back = inverse[0:1] * (weighted - mean - scaled[...] * tilt)
    grad_first[...] = back
    low_first[...] = back.astype(BF16)
    sums_out[...] = sums[...] + row_sums({0: upstream * scaled[...], 1: upstream, 4: back})


def attend_back_kernel(
    flags, a_own, a_away, packs, qkv, prob, grad_first, grad_qkv, keep, give, grad_context
):
    low = flags[0]
    half = a_own.shape[1]
    feats = packs.shape[2]
    width = grad_context.shape[0]
    for part, ref in enumerate((a_own, a_away)):
        cols = slice(part * half, (part + 1) * half)
        total = 0.0
        for k in range(4):
            total = total + dot(
                packs[k, 3 * width :], ref[k * feats : (k + 1) * feats], 1, 0
            )
        grad_context[:, cols] = total.astype(BF16)
    scale = HEAD_DIM ** (-0.5)
    for h in range(width // HEAD_DIM):
        q_rows = pl.ds(h * HEAD_DIM, HEAD_DIM)
        k_rows = pl.ds(width + h * HEAD_DIM, HEAD_DIM)
        v_rows = pl.ds(2 * width + h * HEAD_DIM, HEAD_DIM)
        grad_keys, grad_values = 0.0, 0.0
        for part in range(2):
            cols = slice(part * half, (part + 1) * half)
            weights = prob[h, :, cols]
            wide = weights.astype(F32)
            grad_weights = dot(qkv[v_rows, :], grad_context[q_rows, cols], 0, 0)
            inner = jnp.sum(wide * grad_weights, axis=0, keepdims=True)
            grad_scores = (wide * (grad_weights - inner)).astype(BF16)
            grad_qkv[q_rows, cols] = (dot(qkv[k_rows, :], grad_scores, 1, 0) * scale).astype(BF16)
            grad_keys = grad_keys + dot(qkv[q_rows, cols], grad_scores, 1, 1)
            grad_values = grad_values + dot(grad_context[q_rows, cols], weights, 1, 1)
        grad_qkv[k_rows, :] = (grad_keys * scale).astype(BF16)
        grad_qkv[v_rows, :] = grad_values.astype(BF16)

    def block(k):
        part = dot(packs[k, : 3 * width], grad_qkv[...], 0, 0)
        rows = pl.ds(pl.multiple_of(k * feats, feats), feats)
        return part[:, :half] + 0.5 * grad_first[rows, :], part[:, half:]

    for j in range(2):
        rows = slice(j * feats, (j + 1) * feats)
        near, far = block(2 * j + 1 - low)
        give[rows, :half] = near.astype(BF16)
        give[rows, half:] = far.astype(BF16)
        near, far = block(2 * j + low)
        keep[rows, :half] = near
        keep[rows, half:] = far


def pack_grad_kernel(
    flags, xs, grad_qkv, a_own, a_away, context, sums, sums_away, b_in_sums, keep, give, pack
):
    odd = flags[1]
    feats = pack.shape[1]
    width = context.shape[0]
    half = a_own.shape[1]
    rows = keep.shape[1]
    ones = (lax.broadcasted_iota(jnp.int32, (8, 2 * half), 0) == 4).astype(BF16)
    more = (lax.broadcasted_iota(jnp.int32, (8, 2 * half), 0) == 5).astype(BF16)
    shared = b_in_sums[...] + dot(ones, grad_qkv[:width], 1, 1)
    shared = shared + dot(more, grad_qkv[2 * width :], 1, 1)
    vector_sums = sums[...] + sums_away[...]
    for k in range(4):
        span = slice(k * feats, (k + 1) * feats)
        pack[: 3 * width] = dot(grad_qkv[...], xs[span], 1, 1).astype(BF16)
        total = dot(context[:, :half], a_own[span], 1, 1)
        total = total + dot(context[:, half:], a_away[span], 1, 1)
        pack[3 * width : 4 * width] = total.astype(BF16)
        tail = jnp.concatenate(
            (vector_sums[:, span], shared, jnp.zeros((EXTRA - 16, feats), F32)), axis=0
        )
        pack[4 * width :] = tail.astype(BF16)

        @pl.when(odd == 0)
        def _():
            keep[k] = pack[:rows]
            give[k] = pack[rows:]

        @pl.when(odd == 1)
        def _():
            keep[k] = pack[rows:]
            give[k] = pack[:rows]


def join_kernel(flags, kept, got, own, away):
    high = flags[4]
    feats = own.shape[0]
    half = own.shape[1] // 2
    for out, at in ((own, high), (away, 1 - high)):
        rows = pl.ds(pl.multiple_of(at * feats, feats), feats)
        near = kept[rows, :half] + got[rows, half:].astype(F32)
        far = kept[rows, half:] + got[rows, :half].astype(F32)
        out[:, :half] = near.astype(out.dtype)
        out[:, half:] = far.astype(out.dtype)


def finish_kernel(flags, own, got, out):
    low = flags[0]
    half = own.shape[1] // 2
    total = (own[...] + got[...].astype(F32)).astype(BF16)

    @pl.when(low == 0)
    def _():
        out[...] = total

    @pl.when(low == 1)
    def _():
        out[:, :half] = total[:, half:]
        out[:, half:] = total[:, :half]


def shards(
    layer_in,
    seq_lengths,
    w_qkv,
    q_bias,
    v_bias,
    w_out,
    b_out,
    ln1_gain,
    ln1_bias,
    w_in,
    b_in,
    w_back,
    b_back,
    ln2_gain,
    ln2_bias,
    out_grad,
):
    n_rows = lax.axis_size("row")
    row, col = lax.axis_index("row"), lax.axis_index("col")
    low_bit = (col % 2) == 1
    odd_bit = lax.axis_index("dp") % 2
    odd = odd_bit == 1
    feats, slot = layer_in.shape
    half = slot // 2
    width = w_out.shape[0]
    model = n_rows * feats
    units = w_in.shape[1]
    heads = width // HEAD_DIM
    length = lax.dynamic_index_in_dim(seq_lengths, row, 0, False)
    flags = jnp.stack((col % 2, odd_bit, col, length, col // 2)).astype(jnp.int32)
    halves = shape((model, half), BF16)
    wide_halves = shape((model, half), F32)

    def sum_cores(mine, other):
        return (mine + swap_bit(other, "col", 1).astype(F32)).astype(BF16)

    x0 = to_slot(layer_in)
    qkv_part = w_qkv.transpose(1, 2, 0).reshape(3 * width, feats)
    n_half = 2 * width
    pack_half = jnp.where(
        odd, jnp.concatenate((qkv_part[n_half:], w_out)), qkv_part[:n_half]
    )
    fetched = [from_row(pack_half, k) for k in range(1, n_rows)]
    x2 = swap_bit(x0, "col", 2)
    x1 = swap_bit(x0, "col", 1)
    x3 = swap_bit(x2, "col", 1)
    swapped = [swap_bit(part, "dp", 1) for part in fetched]

    vectors = jnp.concatenate((b_out, ln1_gain, ln1_bias, b_back, ln2_gain, ln2_bias))
    vectors = jnp.pad(vectors.reshape(6, feats), ((0, 10), (0, units - feats)))
    wide = jnp.concatenate((jnp.where(odd, w_back, w_in), vectors))
    wide = after(wide, *fetched)
    wide_fetched = [from_row(wide, k) for k in range(1, n_rows)]
    wide_swapped = [swap_bit(part, "dp", 1) for part in wide_fetched]
    in_all = jnp.concatenate(
        [w_in]
        + [jnp.where(odd, o[:feats], f[:feats]) for f, o in zip(wide_fetched, wide_swapped)]
    )
    back_all = jnp.concatenate(
        [w_back]
        + [jnp.where(odd, f[:feats], o[:feats]) for f, o in zip(wide_fetched, wide_swapped)]
    )
    at_vectors = pl.BlockSpec((16, units), lambda _: (feats // 16, 0))
    (vecs,) = call(
        vector_kernel,
        "vectors",
        [shape((model, 16), F32)],
        [vectors] + wide_fetched,
        specs={k: at_vectors for k in range(1, n_rows)},
    )

    qkv_bias = jnp.concatenate((q_bias, jnp.zeros_like(q_bias), v_bias)).astype(F32)[:, None]
    xs, packs, qkv, prob, context, mine, other = call(
        attend_kernel,
        "attend",
        [
            shape((model, slot), BF16),
            shape((n_rows, 4 * width, feats), BF16),
            shape((3 * width, slot), BF16),
            shape((heads, slot, slot), BF16),
            shape((width, slot), BF16),
            wide_halves,
            halves,
        ],
        [flags, x0, x1, x2, x3, qkv_part, w_out] + fetched + swapped + [qkv_bias],
        flops=8 * model * width * slot + 4 * slot * slot * width,
    )

    g_own = to_slot(after(out_grad.astype(BF16), xs))
    g_high = swap_bit(g_own, "col", 2)
    g_both = jnp.concatenate((g_own, g_high))
    g_low = swap_bit(jnp.where(low_bit, g_both[:, :half], g_both[:, half:]), "col", 1)

    own = sum_cores(mine, other)
    away = swap_bit(own, "col", 2)
    scaled_one, inverse_one, n_own = call(
        norm_kernel,
        "norm",
        [wide_halves, shape((8, half), F32), halves],
        [xs, own, away, vecs],
        specs={0: pl.BlockSpec((model, half), lambda _: (0, 0))},
    )
    n_away = swap_bit(n_own, "col", 1)
    hidden, slope, mine, other = call(
        forward_kernel,
        "feed_forward",
        [shape((units, slot), BF16), shape((units, slot), BF16), wide_halves, halves],
        [n_own, n_away, in_all, back_all, b_in.astype(F32)[:, None]],
        flops=4 * model * units * slot,
    )
    own = sum_cores(mine, other)
    away = swap_bit(own, "col", 2)
    out_own, out_give, grad_second, r_own, sums = call(
        turn_kernel,
        "turn",
        [
            shape((feats, half), BF16),
            shape((feats, half), BF16),
            wide_halves,
            halves,
            shape((8, model), F32),
        ],
        [flags, scaled_one, own, away, vecs, g_own, g_high, g_low],
        scratch=[pltpu.VMEM((model, half), BF16), pltpu.VMEM((model, half), BF16)],
    )
    r_away = swap_bit(r_own, "col", 1)
    mine, other, grad_pre, b_in_sums = call(
        backward_kernel,
        "feed_backward",
        [wide_halves, halves, shape((units, slot), BF16), shape((8, feats), F32)],
        [r_own, r_away, slope, in_all, back_all],
        flops=4 * model * units * slot,
    )
    own = sum_cores(mine, other)
    wide_grads = call(
        wide_grad_kernel,
        "wide_grads",
        [shape((feats, units), BF16)] * (2 * n_rows),
        [after(r_own, own), r_away, hidden, n_own, n_away, grad_pre],
        flops=4 * model * units * slot,
    )
    away = swap_bit(own, "col", 2)
    grad_first, a_own, sums = call(
        norm_back_kernel,
        "norm_back",
        [wide_halves, halves, shape((8, model), F32)],
        [own, away, grad_second, scaled_one, inverse_one, vecs, sums],
    )
    a_away = swap_bit(a_own, "col", 1)
    sums_away = swap_bit(sums, "col", 1)
    grad_qkv, kept, give = call(
        attend_back_kernel,
        "attend_back",
        [
            shape((3 * width, slot), BF16),
            shape((2 * feats, slot), F32),
            shape((2 * feats, slot), BF16),
        ],
        [flags, a_own, a_away, packs, qkv, prob, grad_first],
        flops=8 * model * width * slot + 10 * slot * slot * width,
        scratch=[pltpu.VMEM((width, slot), BF16)],
    )

    in_own, in_away = call(
        join_kernel,
        "join",
        [shape((feats, slot), F32), shape((feats, slot), BF16)],
        [flags, kept, swap_bit(give, "col", 1)],
    )
    (in_grad,) = call(
        finish_kernel,
        "finish",
        [shape((feats, slot), BF16)],
        [flags, in_own, swap_bit(in_away, "col", 2)],
    )
    in_grad = from_slot(in_grad).astype(F32)

    out_give = after(out_give, a_own)
    layer_out = from_slot(ordered(low_bit, out_own, swap_bit(out_give, "col", 1), 1))

    def add_rows(blocks):
        terms = [blocks[0]] + [from_row(blocks[k], n_rows - k) for k in range(1, n_rows)]
        terms = [term.astype(F32) for term in terms]
        while len(terms) > 1:
            pairs = len(terms) // 2
            terms = [terms[i] + terms[i + pairs] for i in range(pairs)]
        return terms[0].astype(BF16)

    def add_replicas(total, first):
        bit = first
        while bit < lax.axis_size("dp"):
            total = total.astype(F32) + swap_bit(total, "dp", bit).astype(F32)
            total = total.astype(BF16)
            bit *= 2
        return total

    pack_keep, pack_give = call(
        pack_grad_kernel,
        "pack_grads",
        [shape((n_rows, 2 * width + EXTRA // 2, feats), BF16)] * 2,
        [flags, xs, grad_qkv, a_own, a_away, context, sums, sums_away, b_in_sums],
        flops=8 * model * width * slot,
        scratch=[pltpu.VMEM((4 * width + EXTRA, feats), BF16)],
    )
    w_back_grad = add_replicas(add_rows(wide_grads[:n_rows]), 1).astype(F32)
    w_in_grad = add_replicas(add_rows(wide_grads[n_rows:]), 1).astype(F32)
    pack_got = swap_bit(pack_give, "dp", 1)
    total = add_rows(
        [
            (pack_keep[k].astype(F32) + pack_got[k].astype(F32)).astype(BF16)
            for k in range(n_rows)
        ]
    )
    total = add_replicas(total, 2)
    total = ordered(odd, total, swap_bit(total, "dp", 1), 0).astype(F32)
    w_qkv_grad = total[: 3 * width].reshape(3, width, feats).transpose(2, 0, 1)
    w_out_grad = total[3 * width : 4 * width]
    tail = total[4 * width :]
    return (
        layer_out,
        in_grad,
        w_qkv_grad,
        tail[12],
        tail[13],
        w_out_grad,
        tail[4],
        tail[0],
        tail[1],
        w_in_grad,
        tail[8:12].reshape(-1),
        w_back_grad,
        tail[5],
        tail[2],
        tail[3],
    )


def solution(mesh):
    tokens = P("row", ("dp", "col"))
    block = P("row", "col")
    in_specs = (
        tokens,
        P("dp"),
        P("row", None, "col"),
        P("col"),
        P("col"),
        P("col", "row"),
        P("row"),
        P("row"),
        P("row"),
        block,
        P("col"),
        block,
        P("row"),
        P("row"),
        P("row"),
        tokens,
    )
    out_specs = (
        tokens,
        tokens,
        P("row", None, "col"),
        P("col"),
        P("col"),
        P("col", "row"),
        P("row"),
        P("row"),
        P("row"),
        block,
        P("col"),
        block,
        P("row"),
        P("row"),
        P("row"),
    )
    return jax.shard_map(shards, mesh=mesh, in_specs=in_specs, out_specs=out_specs, check_vma=False)
```

time: 287 us -> 258 us (0.90)
  other arithmetic: 43.6 us -> 11.4 us
  local copies, waits for them, and re-layouts: 47.9 us -> 20.9 us
  Pallas kernels: 0 us -> 25.3 us
  matrix products: 22.3 us -> 0 us
  waiting for transfers between devices: 113 us -> 134 us
  starting transfers between devices: 52.6 us -> 62 us
    ppermute x15, waiting for transfers between devices: 32.9 us -> 76 us  [from_row(): lax.ppermute(value, 'row', [((a + away) % size, a) for a in range(size)])]
    ppermute x29 -> x28, waiting for transfers between devices: 76.3 us -> 49.9 us  [swap_bit(): return lax.ppermute(value, axis, [(at, at ^ bit) for at in range(size)])]
    pallas_call x0 -> x12, Pallas kernels: none -> 25.3 us  [call(): pl.pallas_call(kernel, name=name, out_shape=outs, grid=(1,) if specs else...]
    dot_general x32 -> x0, matrix products: 19.5 us -> none  [the longest x27 16.7 us: dot(): lax.dot_general(left, right, (((left_dim,), (right_dim,)), ((), ())), pre...]
    another operation x30 -> x1, local copies, waits for them, and re-layouts: 18 us -> 0.73 us  [shards(): jnp.stack((col % 2, odd_bit, col, length, col // 2)).astype(jnp.int32)]
    convert_element_type x27 -> x13, other arithmetic: 18 us -> 8.71 us  [the longest x3 2.71 us: add_rows(): return terms[0].astype(BF16)]
    reduce_sum x6 -> x0, other arithmetic: 7.47 us -> none  [the longest x2 2.96 us: normalise(): center = jnp.sum(hidden, axis=0, keepdims=True) / width]
    select_n x14 -> x6, other arithmetic: 8.55 us -> 1.14 us  [the longest x1 0.95 us: shards(): jnp.where(odd, jnp.concatenate((qkv_part[n_half:], w_out)), qkv_part[:n_h...]
  transfers between devices with their start and end apart: 48 -> 47, of which waited for: 26 -> 29; matrix products, arithmetic and copies ran while one was open for 32% -> 6% of each run, Pallas kernels for 0% -> 6%
where the time goes in v3:
time: 258 us; the launch traced here: 255 us
  waiting for transfers between devices  134 us (52%)
  starting transfers between devices  62 us (24%)
  Pallas kernels  25.3 us (10%)
  local copies, waits for them, and re-layouts  20.9 us (8%)
  other arithmetic  11.4 us (4%)
    ppermute x15, waiting for transfers between devices, from_row(): lax.ppermute(value, 'row', [((a + away) % size, a) for a in range(size)])  76 us
    ppermute x28, waiting for transfers between devices, swap_bit(): return lax.ppermute(value, axis, [(at, at ^ bit) for at in range(size)])  49.9 us
    pallas_call x12, Pallas kernels, call(): pl.pallas_call(kernel, name=name, out_shape=outs, grid=(1,) if specs else...  25.3 us
    ppermute x15, starting transfers between devices, from_row(): lax.ppermute(value, 'row', [((a + away) % size, a) for a in range(size)])  24.4 us
    ppermute x28, starting transfers between devices, swap_bit(): return lax.ppermute(value, axis, [(at, at ^ bit) for at in range(size)])  21.8 us
    unnamed x113, local copies, waits for them, and re-layouts  14.3 us
    ppermute x2, starting transfers between devices, from_slot(): lax.ppermute(value, ('row', 'col'), [(b, a) for a, b in grid_pairs()])  10.1 us
    ppermute x2, waiting for transfers between devices, to_slot(): return lax.ppermute(value, ('row', 'col'), grid_pairs())  7.09 us
  transfers between devices with their start and end apart: 47, of which 29 were waited for; matrix products, arithmetic and copies ran while one was open for 6% of the time, Pallas kernels for 6%

profile of v3, /device:TPU:20, one launch (start us, length us, event | category | flops | bytes accessed | tf_op | source)
XLA Modules:
  0.0 255.4 jit_solution(9191809941609469105)
XLA Ops:
  4.5 7.1 %collective-permute-done.x0 = bf16[192,512]{1,0:T(8,128)(2,1)S(1)} collective-permute-done((bf16[192,512]{1,0:T(8,128)(2,1)}, bf16[192,512]{1,0:T(8,128)(2,1)S(1)}, u32[]{:S(2)}, u32[]{:S(2)}) %collective-permute-start) | collective-permute-done | bytes 196640 | tf_op jit(solution)/shard_map/ppermute | solution.py:60
  13.4 3.6 %collective-permute-start.6 = (bf16[384,192]{1,0:T(8,128)(2,1)S(1)}, bf16[384,192]{1,0:T(8,128)(2,1)S(1)}, u32[]{:S(2)}, u32[]{:S(2)}) collective-permute-start(bf16[384,192]{1,0:T(8,128)(2,1)S(1)} %maximum_select_fusion), channel_id=1, source_target_pairs={{12,0},{0,4},{4,8},{8,12},{13,1},{1,5},{5,9},{9,13},{14,2},{2,6},{... | collective-permute-start | bytes 442376 | tf_op jit(solution)/shard_map/ppermute | solution.py:69
  22.8 5.1 %collective-permute-done.5.f2 = bf16[384,192]{1,0:T(8,128)(2,1)S(1)} collective-permute-done((bf16[384,192]{1,0:T(8,128)(2,1)S(1)}, bf16[384,192]{1,0:T(8,128)(2,1)S(1)}, u32[]{:S(2)}, u32[]{:S(2)}) %collective-permute-start.5) | collective-permute-done | bytes 147488 | tf_op jit(solution)/shard_map/ppermute | solution.py:69
  34.7 4.2 %collective-permute-done.7.s1 = bf16[384,192]{1,0:T(8,128)(2,1)S(1)} collective-permute-done((bf16[384,192]{1,0:T(8,128)(2,1)S(1)}, bf16[384,192]{1,0:T(8,128)(2,1)S(1)}, u32[]{:S(2)}, u32[]{:S(2)}) %collective-permute-start.7) | collective-permute-done | bytes 147488 | tf_op jit(solution)/shard_map/ppermute | solution.py:49
  43.6 4.7 %attend.1 = (bf16[768,512]{1,0:T(8,128)(2,1)S(1)}, bf16[4,768,192]{2,1,0:T(8,128)(2,1)S(1)}, bf16[576,512]{1,0:T(8,128)(2,1)S(1)}, bf16[3,512,512]{2,1,0:T(8,128...) custom-call(s32[5]{0:T(128)S(1)} %stack.20.flags, ...), custom_call_target="tpu_custom_call" | custom-call | flops 805306368 | bytes 7473428 | tf_op jit(solution)/shard_map/attend/pallas_call | solution.py:30
  49.8 7.5 %collective-permute-start.14 = (bf16[208,768]{1,0:T(8,128)(2,1)S(1)}, bf16[208,768]{1,0:T(8,128)(2,1)S(1)}, u32[]{:S(2)}, u32[]{:S(2)}) collective-permute-start(bf16[208,768]{1,0:T(8,128)(2,1)S(1)} %pad_maximum_fusion.2), channel_id=1, source_target_pairs={{12,0},{0,4},{4,8},{8,12},{13,1},{1,5},{5,9},{9,13},{14,2},{2,6},{... | collective-permute-start | bytes 958472 | tf_op jit(solution)/shard_map/ppermute | solution.py:69
  58.9 7.2 %collective-permute-done.14.v3 = bf16[208,768]{1,0:T(8,128)(2,1)S(1)} collective-permute-done((bf16[208,768]{1,0:T(8,128)(2,1)S(1)}, bf16[208,768]{1,0:T(8,128)(2,1)S(1)}, u32[]{:S(2)}, u32[]{:S(2)}) %collective-permute-start.14) | collective-permute-done | bytes 319520 | tf_op jit(solution)/shard_map/ppermute | solution.py:69
  67.8 10.5 %collective-permute-done.13.v2 = bf16[208,768]{1,0:T(8,128)(2,1)S(1)} collective-permute-done((bf16[208,768]{1,0:T(8,128)(2,1)S(1)}, bf16[208,768]{1,0:T(8,128)(2,1)S(1)}, u32[]{:S(2)}, u32[]{:S(2)}) %collective-permute-start.13) | collective-permute-done | bytes 319520 | tf_op jit(solution)/shard_map/ppermute | solution.py:69
  79.8 5.3 %collective-permute-done.12.v1 = bf16[208,768]{1,0:T(8,128)(2,1)S(1)} collective-permute-done((bf16[208,768]{1,0:T(8,128)(2,1)S(1)}, bf16[208,768]{1,0:T(8,128)(2,1)S(1)}, u32[]{:S(2)}, u32[]{:S(2)}) %collective-permute-start.12) | collective-permute-done | bytes 319520 | tf_op jit(solution)/shard_map/ppermute | solution.py:69
  90.3 13.4 %collective-permute-done.11.away = bf16[768,256]{1,0:T(8,128)(2,1)S(1)} collective-permute-done((bf16[768,256]{1,0:T(8,128)(2,1)S(1)}, bf16[768,256]{1,0:T(8,128)(2,1)S(1)}, u32[]{:S(2)}, u32[]{:S(2)}) %collective-permute-start.11) | collective-permute-done | bytes 393248 | tf_op jit(solution)/shard_map/ppermute | solution.py:49
  114.9 4.8 %collective-permute-done.22.g_high = bf16[192,512]{1,0:T(8,128)(2,1)} collective-permute-done((bf16[192,512]{1,0:T(8,128)(2,1)}, bf16[192,512]{1,0:T(8,128)(2,1)}, u32[]{:S(2)}, u32[]{:S(2)}) %collective-permute-start.22) | collective-permute-done | bytes 196640 | tf_op jit(solution)/shard_map/ppermute | solution.py:49
  125.3 7.5 %collective-permute-done.20.away = bf16[768,256]{1,0:T(8,128)(2,1)S(1)} collective-permute-done((bf16[768,256]{1,0:T(8,128)(2,1)S(1)}, bf16[768,256]{1,0:T(8,128)(2,1)S(1)}, u32[]{:S(2)}, u32[]{:S(2)}) %collective-permute-start.20) | collective-permute-done | bytes 393248 | tf_op jit(solution)/shard_map/ppermute | solution.py:49
  132.8 3.0 %turn.1 = (bf16[192,256]{1,0:T(8,128)(2,1)S(1)}, bf16[192,256]{1,0:T(8,128)(2,1)S(1)}, f32[768,256]{1,0:T(8,128)S(1)}, bf16[768,256]{1,0:T(8,128)(2,1)S(1)}, f32[8,768]{1,0:T(8,128)S(1)}) custom-call(s32[5]{0:T(128)S(1)} %stack.20.flags, f32[768,256]{1,0:T(8,128)S(1)} %get-tuple-element.64.scaled_one.scaled, bf16[768,256]{1,0:T(8,128)(2,1)S(1)} %add_convert_fusion.1.own, ...), custom_call_target="tpu_custom_call" | custom-call | bytes 3612692 | tf_op jit(solution)/shard_map/turn/pallas_call | solution.py:30
  144.0 9.7 %collective-permute-done.26.away = bf16[768,256]{1,0:T(8,128)(2,1)S(1)} collective-permute-done((bf16[768,256]{1,0:T(8,128)(2,1)S(1)}, bf16[768,256]{1,0:T(8,128)(2,1)S(1)}, u32[]{:S(2)}, u32[]{:S(2)}) %collective-permute-start.26) | collective-permute-done | bytes 393248 | tf_op jit(solution)/shard_map/ppermute | solution.py:49
  165.2 4.7 %attend_back.1 = (bf16[576,512]{1,0:T(8,128)(2,1)S(1)}, f32[384,512]{1,0:T(8,128)S(1)}, bf16[384,512]{1,0:T(8,128)(2,1)S(1)}) custom-call(s32[5]{0:T(128)S(1)} %stack.20.flags, bf16[768,256]{1,0:T(8,128)(2,1)S(1)} %get-tuple-element.77.a_own, bf16[768,256]{1,0:T(8,128)(2,1)S(1)} %collective-permute-done.29.a_away, ...), custom_call_target="tpu_custom_call" | custom-call | flops 1107296256 | bytes 6684692 | tf_op jit(solution)/shard_map/attend_back/pallas_call | solution.py:30
  170.0 10.3 %collective-permute-done.39 = bf16[192,768]{1,0:T(8,128)(2,1)S(1)} collective-permute-done((bf16[192,768]{1,0:T(8,128)(2,1)S(1)}, bf16[192,768]{1,0:T(8,128)(2,1)S(1)}, u32[]{:S(2)}, u32[]{:S(2)}) %collective-permute-start.39) | collective-permute-done | bytes 294944 | tf_op jit(solution)/shard_map/ppermute | solution.py:69
  186.2 7.9 %collective-permute-done.40 = bf16[192,768]{1,0:T(8,128)(2,1)} collective-permute-done((bf16[192,768]{1,0:T(8,128)(2,1)}, bf16[192,768]{1,0:T(8,128)(2,1)}, u32[]{:S(2)}, u32[]{:S(2)}) %collective-permute-start.40) | collective-permute-done | bytes 294944 | tf_op jit(solution)/shard_map/ppermute | solution.py:69
  195.2 4.1 %collective-permute-done.41 = bf16[192,768]{1,0:T(8,128)(2,1)} collective-permute-done((bf16[192,768]{1,0:T(8,128)(2,1)}, bf16[192,768]{1,0:T(8,128)(2,1)}, u32[]{:S(2)}, u32[]{:S(2)}) %collective-permute-start.41) | collective-permute-done | bytes 294944 | tf_op jit(solution)/shard_map/ppermute | solution.py:69
  201.4 4.3 %collective-permute-done.43 = bf16[192,768]{1,0:T(8,128)(2,1)} collective-permute-done((bf16[192,768]{1,0:T(8,128)(2,1)}, bf16[192,768]{1,0:T(8,128)(2,1)}, u32[]{:S(2)}, u32[]{:S(2)}) %collective-permute-start.43) | collective-permute-done | bytes 294944 | tf_op jit(solution)/shard_map/ppermute | solution.py:69
  205.7 7.0 %collective-permute-done.44 = bf16[192,768]{1,0:T(8,128)(2,1)} collective-permute-done((bf16[192,768]{1,0:T(8,128)(2,1)}, bf16[192,768]{1,0:T(8,128)(2,1)}, u32[]{:S(2)}, u32[]{:S(2)}) %collective-permute-start.44) | collective-permute-done | bytes 294944 | tf_op jit(solution)/shard_map/ppermute | solution.py:69
  223.4 3.8 %collective-permute-start.28 = (bf16[192,512]{1,0:T(8,128)(2,1)}, bf16[192,512]{1,0:T(8,128)(2,1)S(1)}, u32[]{:S(2)}, u32[]{:S(2)}) collective-permute-start(bf16[192,512]{1,0:T(8,128)(2,1)} %pad_maximum_fusion.3), channel_id=1, source_target_pairs={{0,0},{7,1},{10,2},{13,3},{1,4},{4,5},{11,6},{14,7},{2,8},{5,9},{8... | collective-permute-start | bytes 589832 | tf_op jit(solution)/shard_map/ppermute | solution.py:64
  230.1 6.3 %collective-permute-start.32 = (bf16[192,512]{1,0:T(8,128)(2,1)S(1)}, bf16[192,512]{1,0:T(8,128)(2,1)S(1)}, u32[]{:S(2)}, u32[]{:S(2)}) collective-permute-start(bf16[192,512]{1,0:T(8,128)(2,1)S(1)} %finish.1), channel_id=1, source_target_pairs={{0,0},{7,1},{10,2},{13,3},{1,4},{4,5},{11,6},{14,7},{2,8},{5,9},{8... | collective-permute-start | bytes 589832 | tf_op jit(solution)/shard_map/ppermute | solution.py:64
  236.4 3.1 %collective-permute-done.37 = bf16[400,192]{1,0:T(8,128)(2,1)S(1)} collective-permute-done((bf16[400,192]{1,0:T(8,128)(2,1)}, bf16[400,192]{1,0:T(8,128)(2,1)S(1)}, u32[]{:S(2)}, u32[]{:S(2)}) %collective-permute-start.37) | collective-permute-done | bytes 153632 | tf_op jit(solution)/shard_map/ppermute | solution.py:69
  239.5 6.0 %collective-permute-done.36 = bf16[400,192]{1,0:T(8,128)(2,1)S(1)} collective-permute-done((bf16[400,192]{1,0:T(8,128)(2,1)S(1)}, bf16[400,192]{1,0:T(8,128)(2,1)S(1)}, u32[]{:S(2)}, u32[]{:S(2)}) %collective-permute-start.36) | collective-permute-done | bytes 153632 | tf_op jit(solution)/shard_map/ppermute | solution.py:69
  (241 shorter events, 102.6 us)
Async XLA Ops:
  11.6 22.0 %collective-permute-start.2 = (bf16[192,512]{1,0:T(8,128)(2,1)S(1)}, bf16[192,512]{1,0:T(8,128)(2,1)S(1)}, u32[]{:S(2)}, u32[]{:S(2)}) collective-permute-start(bf16[192,512]{1,0:T(8,128)(2,1)S(1)} %collective-permute-done.x0), channel_id=1, source_target_pairs={{0,2},{1,3},{2,0},{3,1},{4,6},{5,7},{6,4},{7,5},{8,10},{9,11},{10,... | collective-permute-start | bytes 589832 | tf_op jit(solution)/shard_map/ppermute | solution.py:49
  17.0 15.1 %collective-permute-start.4 = (bf16[384,192]{1,0:T(8,128)(2,1)S(1)}, bf16[384,192]{1,0:T(8,128)(2,1)S(1)}, u32[]{:S(2)}, u32[]{:S(2)}) collective-permute-start(bf16[384,192]{1,0:T(8,128)(2,1)S(1)} %maximum_select_fusion), channel_id=1, source_target_pairs={{4,0},{8,4},{12,8},{0,12},{5,1},{9,5},{13,9},{1,13},{6,2},{10,6},{... | collective-permute-start | bytes 442376 | tf_op jit(solution)/shard_map/ppermute | solution.py:69
  49.8 40.1 %collective-permute-start.10 = (bf16[768,256]{1,0:T(8,128)(2,1)S(1)}, bf16[768,256]{1,0:T(8,128)(2,1)S(1)}, u32[]{:S(2)}, u32[]{:S(2)}) collective-permute-start(bf16[768,256]{1,0:T(8,128)(2,1)S(1)} %get-tuple-element.62), channel_id=1, source_target_pairs={{0,1},{1,0},{2,3},{3,2},{4,5},{5,4},{6,7},{7,6},{8,9},{9,8},{10,11... | collective-permute-start | bytes 1179656 | tf_op jit(solution)/shard_map/ppermute | solution.py:49
  49.8 16.2 %collective-permute-start.14 = (bf16[208,768]{1,0:T(8,128)(2,1)S(1)}, bf16[208,768]{1,0:T(8,128)(2,1)S(1)}, u32[]{:S(2)}, u32[]{:S(2)}) collective-permute-start(bf16[208,768]{1,0:T(8,128)(2,1)S(1)} %pad_maximum_fusion.2), channel_id=1, source_target_pairs={{12,0},{0,4},{4,8},{8,12},{13,1},{1,5},{5,9},{9,13},{14,2},{2,6},{... | collective-permute-start | bytes 958472 | tf_op jit(solution)/shard_map/ppermute | solution.py:69
  57.3 21.0 %collective-permute-start.13 = (bf16[208,768]{1,0:T(8,128)(2,1)S(1)}, bf16[208,768]{1,0:T(8,128)(2,1)S(1)}, u32[]{:S(2)}, u32[]{:S(2)}) collective-permute-start(bf16[208,768]{1,0:T(8,128)(2,1)S(1)} %pad_maximum_fusion.2), channel_id=1, source_target_pairs={{8,0},{12,4},{0,8},{4,12},{9,1},{13,5},{1,9},{5,13},{10,2},{14,6},... | collective-permute-start | bytes 958472 | tf_op jit(solution)/shard_map/ppermute | solution.py:69
  57.3 27.8 %collective-permute-start.12 = (bf16[208,768]{1,0:T(8,128)(2,1)S(1)}, bf16[208,768]{1,0:T(8,128)(2,1)S(1)}, u32[]{:S(2)}, u32[]{:S(2)}) collective-permute-start(bf16[208,768]{1,0:T(8,128)(2,1)S(1)} %pad_maximum_fusion.2), channel_id=1, source_target_pairs={{4,0},{8,4},{12,8},{0,12},{5,1},{9,5},{13,9},{1,13},{6,2},{10,6},{... | collective-permute-start | bytes 958472 | tf_op jit(solution)/shard_map/ppermute | solution.py:69
  66.1 24.1 %collective-permute-start.18 = (bf16[208,768]{1,0:T(8,128)(2,1)S(1)}, bf16[208,768]{1,0:T(8,128)(2,1)S(1)}, u32[]{:S(2)}, u32[]{:S(2)}) collective-permute-start(bf16[208,768]{1,0:T(8,128)(2,1)S(1)} %collective-permute-done.14.v3), channel_id=1, source_target_pairs={{0,16},{16,0},{1,17},{17,1},{2,18},{18,2},{3,19},{19,3},{4,20},{20... | collective-permute-start | bytes 958472 | tf_op jit(solution)/shard_map/ppermute | solution.py:49
  85.3 18.9 %collective-permute-start.16 = (bf16[208,768]{1,0:T(8,128)(2,1)S(1)}, bf16[208,768]{1,0:T(8,128)(2,1)S(1)}, u32[]{:S(2)}, u32[]{:S(2)}) collective-permute-start(bf16[208,768]{1,0:T(8,128)(2,1)S(1)} %collective-permute-done.12.v1), channel_id=1, source_target_pairs={{0,16},{16,0},{1,17},{17,1},{2,18},{18,2},{3,19},{19,3},{4,20},{20... | collective-permute-start | bytes 958472 | tf_op jit(solution)/shard_map/ppermute | solution.py:49
  86.9 24.5 %collective-permute-start.21 = (bf16[192,512]{1,0:T(8,128)(2,1)S(1)}, bf16[192,512]{1,0:T(8,128)(2,1)}, u32[]{:S(2)}, u32[]{:S(2)}) collective-permute-start(bf16[192,512]{1,0:T(8,128)(2,1)S(1)} %convert_element_type.171), channel_id=1, source_target_pairs={{0,0},{1,7},{2,10},{3,13},{4,1},{5,4},{6,11},{7,14},{8,2},{9,5},{1... | collective-permute-start | bytes 589832 | tf_op jit(solution)/shard_map/ppermute | solution.py:60
  90.0 13.6 %collective-permute-start.11 = (bf16[768,256]{1,0:T(8,128)(2,1)S(1)}, bf16[768,256]{1,0:T(8,128)(2,1)S(1)}, u32[]{:S(2)}, u32[]{:S(2)}) collective-permute-start(bf16[768,256]{1,0:T(8,128)(2,1)S(1)} %add_convert_fusion.2.own), channel_id=1, source_target_pairs={{0,2},{1,3},{2,0},{3,1},{4,6},{5,7},{6,4},{7,5},{8,10},{9,11},{10,... | collective-permute-start | bytes 1179656 | tf_op jit(solution)/shard_map/ppermute | solution.py:49
  158.5 21.8 %collective-permute-start.39 = (bf16[192,768]{1,0:T(8,128)(2,1)S(1)}, bf16[192,768]{1,0:T(8,128)(2,1)S(1)}, u32[]{:S(2)}, u32[]{:S(2)}) collective-permute-start(bf16[192,768]{1,0:T(8,128)(2,1)S(1)} %get-tuple-element.98), channel_id=1, source_target_pairs={{8,0},{12,4},{0,8},{4,12},{9,1},{13,5},{1,9},{5,13},{10,2},{14,6},... | collective-permute-start | bytes 884744 | tf_op jit(solution)/shard_map/ppermute | solution.py:69
  160.3 33.8 %collective-permute-start.40 = (bf16[192,768]{1,0:T(8,128)(2,1)}, bf16[192,768]{1,0:T(8,128)(2,1)}, u32[]{:S(2)}, u32[]{:S(2)}) collective-permute-start(bf16[192,768]{1,0:T(8,128)(2,1)} %get-tuple-element.99), channel_id=1, source_target_pairs={{12,0},{0,4},{4,8},{8,12},{13,1},{1,5},{5,9},{9,13},{14,2},{2,6},{... | collective-permute-start | bytes 884744 | tf_op jit(solution)/shard_map/ppermute | solution.py:69
  162.1 37.2 %collective-permute-start.41 = (bf16[192,768]{1,0:T(8,128)(2,1)}, bf16[192,768]{1,0:T(8,128)(2,1)}, u32[]{:S(2)}, u32[]{:S(2)}) collective-permute-start(bf16[192,768]{1,0:T(8,128)(2,1)} %get-tuple-element.100), channel_id=1, source_target_pairs={{4,0},{8,4},{12,8},{0,12},{5,1},{9,5},{13,9},{1,13},{6,2},{10,6},{... | collective-permute-start | bytes 884744 | tf_op jit(solution)/shard_map/ppermute | solution.py:69
  162.3 43.3 %collective-permute-start.43 = (bf16[192,768]{1,0:T(8,128)(2,1)}, bf16[192,768]{1,0:T(8,128)(2,1)}, u32[]{:S(2)}, u32[]{:S(2)}) collective-permute-start(bf16[192,768]{1,0:T(8,128)(2,1)} %get-tuple-element.102), channel_id=1, source_target_pairs={{8,0},{12,4},{0,8},{4,12},{9,1},{13,5},{1,9},{5,13},{10,2},{14,6},... | collective-permute-start | bytes 884744 | tf_op jit(solution)/shard_map/ppermute | solution.py:69
  165.2 15.1 %collective-permute-start.33 = (f32[8,768]{1,0:T(8,128)S(1)}, f32[8,768]{1,0:T(8,128)S(1)}, u32[]{:S(2)}, u32[]{:S(2)}) collective-permute-start(f32[8,768]{1,0:T(8,128)S(1)} %get-tuple-element.90.sums), channel_id=1, source_target_pairs={{0,1},{1,0},{2,3},{3,2},{4,5},{5,4},{6,7},{7,6},{8,9},{9,8},{10,11... | collective-permute-start | bytes 73736 | tf_op jit(solution)/shard_map/ppermute | solution.py:49
  180.3 32.4 %collective-permute-start.44 = (bf16[192,768]{1,0:T(8,128)(2,1)}, bf16[192,768]{1,0:T(8,128)(2,1)}, u32[]{:S(2)}, u32[]{:S(2)}) collective-permute-start(bf16[192,768]{1,0:T(8,128)(2,1)} %get-tuple-element.103), channel_id=1, source_target_pairs={{12,0},{0,4},{4,8},{8,12},{13,1},{1,5},{5,9},{9,13},{14,2},{2,6},{... | collective-permute-start | bytes 884744 | tf_op jit(solution)/shard_map/ppermute | solution.py:69
  180.3 32.4 %collective-permute-start.45 = (bf16[192,768]{1,0:T(8,128)(2,1)}, bf16[192,768]{1,0:T(8,128)(2,1)}, u32[]{:S(2)}, u32[]{:S(2)}) collective-permute-start(bf16[192,768]{1,0:T(8,128)(2,1)} %get-tuple-element.104), channel_id=1, source_target_pairs={{4,0},{8,4},{12,8},{0,12},{5,1},{9,5},{13,9},{1,13},{6,2},{10,6},{... | collective-permute-start | bytes 884744 | tf_op jit(solution)/shard_map/ppermute | solution.py:69
  194.1 23.0 %collective-permute-start.34 = (bf16[4,400,192]{1,2,0:T(8,128)(2,1)}, bf16[4,400,192]{1,2,0:T(8,128)(2,1)S(1)}, u32[]{:S(2)}, u32[]{:S(2)}) collective-permute-start(bf16[4,400,192]{1,2,0:T(8,128)(2,1)} %copy.50), channel_id=1, source_target_pairs={{0,16},{16,0},{1,17},{17,1},{2,18},{18,2},{3,19},{19,3},{4,20},{20... | collective-permute-start | bytes 1843208 | tf_op jit(solution)/shard_map/ppermute | solution.py:49
  200.6 20.6 %collective-permute-start.42 = (bf16[192,768]{1,0:T(8,128)(2,1)S(1)}, bf16[192,768]{1,0:T(8,128)(2,1)}, u32[]{:S(2)}, u32[]{:S(2)}) collective-permute-start(bf16[192,768]{1,0:T(8,128)(2,1)S(1)} %add_convert_fusion.6), channel_id=1, source_target_pairs={{0,16},{16,0},{1,17},{17,1},{2,18},{18,2},{3,19},{19,3},{4,20},{20... | collective-permute-start | bytes 884744 | tf_op jit(solution)/shard_map/ppermute | solution.py:49
  214.0 33.1 %collective-permute-start.46 = (bf16[192,768]{1,0:T(8,128)(2,1)S(1)}, bf16[192,768]{1,0:T(8,128)(2,1)S(1)}, u32[]{:S(2)}, u32[]{:S(2)}) collective-permute-start(bf16[192,768]{1,0:T(8,128)(2,1)S(1)} %add_convert_fusion.4), channel_id=1, source_target_pairs={{0,16},{16,0},{1,17},{17,1},{2,18},{18,2},{3,19},{19,3},{4,20},{20... | collective-permute-start | bytes 884744 | tf_op jit(solution)/shard_map/ppermute | solution.py:49
  218.5 21.0 %collective-permute-start.37 = (bf16[400,192]{1,0:T(8,128)(2,1)}, bf16[400,192]{1,0:T(8,128)(2,1)S(1)}, u32[]{:S(2)}, u32[]{:S(2)}) collective-permute-start(bf16[400,192]{1,0:T(8,128)(2,1)} %get-tuple-element.106), channel_id=1, source_target_pairs={{4,0},{8,4},{12,8},{0,12},{5,1},{9,5},{13,9},{1,13},{6,2},{10,6},{... | collective-permute-start | bytes 460808 | tf_op jit(solution)/shard_map/ppermute | solution.py:69
  221.3 24.3 %collective-permute-start.36 = (bf16[400,192]{1,0:T(8,128)(2,1)S(1)}, bf16[400,192]{1,0:T(8,128)(2,1)S(1)}, u32[]{:S(2)}, u32[]{:S(2)}) collective-permute-start(bf16[400,192]{1,0:T(8,128)(2,1)S(1)} %get-tuple-element.107), channel_id=1, source_target_pairs={{12,0},{0,4},{4,8},{8,12},{13,1},{1,5},{5,9},{9,13},{14,2},{2,6},{... | collective-permute-start | bytes 460808 | tf_op jit(solution)/shard_map/ppermute | solution.py:69
  223.4 24.6 %collective-permute-start.28 = (bf16[192,512]{1,0:T(8,128)(2,1)}, bf16[192,512]{1,0:T(8,128)(2,1)S(1)}, u32[]{:S(2)}, u32[]{:S(2)}) collective-permute-start(bf16[192,512]{1,0:T(8,128)(2,1)} %pad_maximum_fusion.3), channel_id=1, source_target_pairs={{0,0},{7,1},{10,2},{13,3},{1,4},{4,5},{11,6},{14,7},{2,8},{5,9},{8... | collective-permute-start | bytes 589832 | tf_op jit(solution)/shard_map/ppermute | solution.py:64
  230.1 19.2 %collective-permute-start.32 = (bf16[192,512]{1,0:T(8,128)(2,1)S(1)}, bf16[192,512]{1,0:T(8,128)(2,1)S(1)}, u32[]{:S(2)}, u32[]{:S(2)}) collective-permute-start(bf16[192,512]{1,0:T(8,128)(2,1)S(1)} %finish.1), channel_id=1, source_target_pairs={{0,0},{7,1},{10,2},{13,3},{1,4},{4,5},{11,6},{14,7},{2,8},{5,9},{8... | collective-permute-start | bytes 589832 | tf_op jit(solution)/shard_map/ppermute | solution.py:64
  (76 other events, 868.5 us)

commit v4 on v3

--- a/solution.py
+++ b/solution.py
@@ -18,25 +18,25 @@
     )
 
 
-def call(kernel, name, outs, args, flops=0, scratch=(), specs=None):
+def call(kernel, name, outs, args, weight=1, scratch=(), specs=None, windowed=False, vmem_mib=16):
     vmem = pl.BlockSpec(memory_space=pltpu.VMEM)
     in_specs = [
         pl.BlockSpec(memory_space=pltpu.SMEM) if arg.dtype == jnp.int32 else vmem for arg in args
     ]
     for at, spec in (specs or {}).items():
         in_specs[at] = spec
-    moved = sum(arg.size * arg.dtype.itemsize for arg in args)
-    moved += sum(out.size * out.dtype.itemsize for out in outs)
     return pl.pallas_call(
         kernel,
         name=name,
         out_shape=outs,
-        grid=(1,) if specs else (),
+        grid=(1,) if windowed else (),
         in_specs=in_specs,
         out_specs=[vmem] * len(outs),
         scratch_shapes=list(scratch),
-        compiler_params=pltpu.CompilerParams(vmem_limit_bytes=32 * 1024 * 1024),
-        cost_estimate=pl.CostEstimate(flops=flops, bytes_accessed=moved, transcendentals=0),
+        compiler_params=pltpu.CompilerParams(vmem_limit_bytes=vmem_mib * 1024 * 1024),
+        cost_estimate=pl.CostEstimate(
+            flops=weight * 2**30, bytes_accessed=weight * 2**22, transcendentals=0
+        ),
     )(*args)
 
 
@@ -77,6 +77,11 @@
     return jnp.concatenate(
         (jnp.where(flag, other, own), jnp.where(flag, own, other)), axis=axis
     )
+
+
+def identity(size):
+    at = lax.broadcasted_iota(jnp.int32, (size, size), 0)
+    return (at == lax.broadcasted_iota(jnp.int32, (size, size), 1)).astype(BF16)
 
 
 def row_sums(products):
@@ -90,47 +95,71 @@
     return total
 
 
+def half_kernel(odd, w_qkv, w_out, out, sems):
+    size = w_out.shape[0]
+
+    def move(copies):
+        for copy in copies:
+            copy.start()
+        for copy in copies:
+            copy.wait()
+
+    @pl.when(odd[0] == 0)
+    def _():
+        move([pltpu.make_async_copy(w_qkv.at[pl.ds(0, 2 * size)], out, sems.at[0])])
+
+    @pl.when(odd[0] == 1)
+    def _():
+        first, second = out.at[pl.ds(0, size)], out.at[pl.ds(size, size)]
+        move(
+            [
+                pltpu.make_async_copy(w_qkv.at[pl.ds(2 * size, size)], first, sems.at[0]),
+                pltpu.make_async_copy(w_out, second, sems.at[1]),
+            ]
+        )
+
+
 def attend_kernel(
-    flags, x0, x1, x2, x3, w_qkv, w_out, f1, f2, f3, s1, s2, s3, bias,
-    xs, packs, qkv, prob, context, mine, other,
+    flags, x0, x1, x2, x3, w_qkv, w_out, f1, f2, f3, swapped, vectors,
+    xs, packs, qkv, prob, context, mine, other, raw, sems,
 ):
     low, odd, col, length = flags[0], flags[1], flags[2], flags[3]
     feats, slot = x0.shape
     half = slot // 2
     width = w_out.shape[0]
     n_half = f1.shape[0]
+    copies = [
+        pltpu.make_async_copy(w_qkv, packs.at[0, pl.ds(0, 3 * width)], sems.at[0]),
+        pltpu.make_async_copy(w_out, packs.at[0, pl.ds(3 * width, width)], sems.at[1]),
+    ]
+    for k, f in enumerate((f1, f2, f3)):
+        for ref, part in ((f, odd), (swapped.at[pl.ds(k * n_half, n_half)], 1 - odd)):
+            rows = pl.ds(pl.multiple_of(part * n_half, n_half), n_half)
+            copies += [pltpu.make_async_copy(ref, packs.at[k + 1, rows], sems.at[len(copies)])]
     for bit, ref in enumerate((x0, x1, x2, x3)):
         rows = pl.ds(pl.multiple_of((col ^ bit) * feats, feats), feats)
-
-        @pl.when(low == 0)
-        def _():
-            xs[rows, :] = ref[...]
-
-        @pl.when(low == 1)
-        def _():
-            xs[rows, :half] = ref[:, half:]
-            xs[rows, half:] = ref[:, :half]
-
-    packs[0, : 3 * width] = w_qkv[...]
-    packs[0, 3 * width :] = w_out[...]
-    for k, (f, s) in enumerate(((f1, s1), (f2, s2), (f3, s3))):
-
-        @pl.when(odd == 0)
-        def _():
-            packs[k + 1, :n_half] = f[...]
-            packs[k + 1, n_half:] = s[...]
-
-        @pl.when(odd == 1)
-        def _():
-            packs[k + 1, :n_half] = s[...]
-            packs[k + 1, n_half:] = f[...]
-
-    for part in range(3):
-        rows = slice(part * width, (part + 1) * width)
-        total = 0.0
+        copies += [pltpu.make_async_copy(ref, raw.at[rows], sems.at[len(copies)])]
+    for copy in copies:
+        copy.start()
+    for copy in copies:
+        copy.wait()
+
+    @pl.when(low == 0)
+    def _():
+        xs[...] = raw[...]
+
+    @pl.when(low == 1)
+    def _():
+        xs[:, :half] = raw[:, half:]
+        xs[:, half:] = raw[:, :half]
+
+    columns = dot(identity(width), vectors[:, :width], 1, 1)
+    for part, bias in enumerate((columns[:, 6:7], 0.0, columns[:, 7:8])):
+        total = bias
         for k in range(4):
-            total = total + dot(packs[k, rows], xs[k * feats : (k + 1) * feats], 1, 0)
-        qkv[rows] = (total + bias[rows]).astype(BF16)
+            block = packs[k, part * feats : (part + 1) * feats]
+            total = total + dot(block, xs[k * feats : (k + 1) * feats], 0, 0)
+        qkv[part * width : (part + 1) * width] = total.astype(BF16)
 
     place = lax.broadcasted_iota(jnp.int32, (slot, half), 0)
     place = jnp.where(low == 1, (place + half) % slot, place)
@@ -157,14 +186,52 @@
         other[rows] = part[:, half:].astype(BF16)
 
 
-def vector_kernel(v0, v1, v2, v3, out):
-    feats = out.shape[0] // 4
-    eye = (
-        lax.broadcasted_iota(jnp.int32, (feats, feats), 0)
-        == lax.broadcasted_iota(jnp.int32, (feats, feats), 1)
-    ).astype(BF16)
-    for k, ref in enumerate((v0, v1, v2, v3)):
-        out[k * feats : (k + 1) * feats] = dot(eye, ref[:, :feats], 1, 1)
+def assemble_kernel(
+    flags, own_in, own_back, v0, f1, f2, f3, s12, s3, w_in, w_back, vecs, bias, rows, sems
+):
+    odd = flags[1]
+    feats = own_in.shape[0]
+    first = pl.ds(0, feats)
+    copies = [
+        pltpu.make_async_copy(own_in, w_in.at[first], sems.at[0]),
+        pltpu.make_async_copy(own_back, w_back.at[first], sems.at[1]),
+    ]
+    size = f1.shape[0]
+    for k, (f, s, s_at) in enumerate(((f1, s12, 0), (f2, s12, size), (f3, s3, 0))):
+        span = pl.ds((k + 1) * feats, feats)
+        s = s.at[pl.ds(s_at, feats)]
+        for ref, into in ((f.at[first], (w_in, w_back)), (s, (w_back, w_in))):
+            at = len(copies)
+            even = pltpu.make_async_copy(ref, into[0].at[span], sems.at[at])
+            other = pltpu.make_async_copy(ref, into[1].at[span], sems.at[at])
+            copies += [(even, other)]
+    for k, ref in enumerate((f1, f2, f3)):
+        tail = ref.at[pl.ds(feats, 16)]
+        copies += [pltpu.make_async_copy(tail, rows.at[k], sems.at[len(copies)])]
+    for begin in (True, False):
+        for copy in copies:
+            if isinstance(copy, tuple):
+
+                @pl.when(odd == 0)
+                def _():
+                    copy[0].start() if begin else copy[0].wait()
+
+                @pl.when(odd == 1)
+                def _():
+                    copy[1].start() if begin else copy[1].wait()
+
+            elif begin:
+                copy.start()
+            else:
+                copy.wait()
+    eye = identity(feats)
+    vecs[:feats] = dot(eye, v0[:, :feats], 1, 1)
+    for k in range(4):
+        span = slice(k * feats, (k + 1) * feats)
+        bias[span] = dot(eye, v0[:, span], 1, 1)
+    for k in range(3):
+        span = slice((k + 1) * feats, (k + 2) * feats)
+        vecs[span] = dot(eye, rows[k, :, :feats], 1, 1)
 
 
 def norm_kernel(x, own, away, vecs, scaled, inverse, low_normed):
@@ -185,7 +252,7 @@
         cols = slice(part * half, (part + 1) * half)
         for at in range(0, w_in.shape[1], step):
             rows = slice(at, at + step)
-            pre = dot(w_in[:, rows], ref[...], 0, 0) + bias[rows]
+            pre = dot(w_in[:, rows], ref[...], 0, 0) + bias[rows, 8:9]
             share = 0.5 * (1.0 + lax.erf(pre * (0.5**0.5)))
             hidden[rows, cols] = (pre * share).astype(BF16)
             bell = jnp.exp(-0.5 * pre * pre) * ((0.5 / jnp.pi) ** 0.5)
@@ -257,17 +324,22 @@
     b_in_sums[...] = total
 
 
-def wide_grad_kernel(r_own, r_away, hidden, n_own, n_away, grad_pre, *outs):
+def wide_grad_kernel(
+    flags, r_own, r_away, hidden, n_own, n_away, grad_pre, b0, b1, b2, b3, keep, give
+):
+    odd = flags[1]
     half = r_own.shape[1]
-    feats = outs[0].shape[0]
+    feats = b0.shape[0]
+    part = feats // 2
+    for k, out in enumerate((b0, b1, b2, b3)):
+        rows = slice(k * feats, (k + 1) * feats)
+        total = dot(r_own[rows], hidden[:, :half], 1, 1)
+        out[...] = (total + dot(r_away[rows], hidden[:, half:], 1, 1)).astype(BF16)
     for k in range(4):
-        rows = slice(k * feats, (k + 1) * feats)
-        for out, own, away, right in (
-            (outs[k], r_own, r_away, hidden),
-            (outs[4 + k], n_own, n_away, grad_pre),
-        ):
-            total = dot(own[rows], right[:, :half], 1, 1)
-            out[...] = (total + dot(away[rows], right[:, half:], 1, 1)).astype(BF16)
+        for out, at in ((keep, odd), (give, 1 - odd)):
+            rows = pl.ds(pl.multiple_of(k * feats + at * part, part), part)
+            total = dot(n_own[rows, :], grad_pre[:, :half], 1, 1)
+            out[k] = (total + dot(n_away[rows, :], grad_pre[:, half:], 1, 1)).astype(BF16)
 
 
 def norm_back_kernel(
@@ -318,7 +390,10 @@
         grad_qkv[v_rows, :] = grad_values.astype(BF16)
 
     def block(k):
-        part = dot(packs[k, : 3 * width], grad_qkv[...], 0, 0)
+        part = 0.0
+        for at in range(3):
+            left = packs[k, at * feats : (at + 1) * feats]
+            part = part + dot(left, grad_qkv[at * width : (at + 1) * width], 1, 0)
         rows = pl.ds(pl.multiple_of(k * feats, feats), feats)
         return part[:, :half] + 0.5 * grad_first[rows, :], part[:, half:]
 
@@ -347,7 +422,9 @@
     vector_sums = sums[...] + sums_away[...]
     for k in range(4):
         span = slice(k * feats, (k + 1) * feats)
-        pack[: 3 * width] = dot(grad_qkv[...], xs[span], 1, 1).astype(BF16)
+        for at in range(3):
+            part = dot(xs[span], grad_qkv[at * width : (at + 1) * width], 1, 1)
+            pack[at * feats : (at + 1) * feats] = part.astype(BF16)
         total = dot(context[:, :half], a_own[span], 1, 1)
         total = total + dot(context[:, half:], a_away[span], 1, 1)
         pack[3 * width : 4 * width] = total.astype(BF16)
@@ -424,49 +501,79 @@
     units = w_in.shape[1]
     heads = width // HEAD_DIM
     length = lax.dynamic_index_in_dim(seq_lengths, row, 0, False)
-    flags = jnp.stack((col % 2, odd_bit, col, length, col // 2)).astype(jnp.int32)
+    flags = jnp.stack((col % 2, odd_bit, col, length, col // 2, row)).astype(jnp.int32)
     halves = shape((model, half), BF16)
     wide_halves = shape((model, half), F32)
 
     def sum_cores(mine, other):
         return (mine + swap_bit(other, "col", 1).astype(F32)).astype(BF16)
 
+    def add_rows(blocks, *gates):
+        terms = [blocks[0]]
+        terms += [after(from_row(blocks[k], n_rows - k), *gates) for k in range(1, n_rows)]
+        terms = [term.astype(F32) for term in terms]
+        while len(terms) > 1:
+            pairs = len(terms) // 2
+            terms = [terms[i] + terms[i + pairs] for i in range(pairs)]
+        return terms[0].astype(BF16)
+
+    def add_replicas(total, first):
+        bit = first
+        while bit < lax.axis_size("dp"):
+            total = total.astype(F32) + swap_bit(total, "dp", bit).astype(F32)
+            total = total.astype(BF16)
+            bit *= 2
+        return total
+
+    def add_shares(keep, got):
+        total = add_rows(
+            [(keep[k].astype(F32) + got[k].astype(F32)).astype(BF16) for k in range(n_rows)]
+        )
+        total = add_replicas(total, 2)
+        return ordered(odd, total, swap_bit(total, "dp", 1), 0)
+
     x0 = to_slot(layer_in)
-    qkv_part = w_qkv.transpose(1, 2, 0).reshape(3 * width, feats)
-    n_half = 2 * width
-    pack_half = jnp.where(
-        odd, jnp.concatenate((qkv_part[n_half:], w_out)), qkv_part[:n_half]
+    qkv_part = w_qkv.transpose(1, 0, 2).reshape(3 * feats, width)
+    n_half = 2 * feats
+    (pack_half,) = call(
+        half_kernel,
+        "half",
+        [shape((n_half, width), BF16)],
+        [odd_bit.reshape(1), qkv_part, w_out],
+        specs={k: pl.BlockSpec(memory_space=pl.ANY) for k in (1, 2)},
+        scratch=[pltpu.SemaphoreType.DMA((2,))],
     )
     fetched = [from_row(pack_half, k) for k in range(1, n_rows)]
+    vectors = jnp.concatenate(
+        (b_out, ln1_gain, ln1_bias, b_back, ln2_gain, ln2_bias, q_bias, v_bias)
+    )
+    vectors = jnp.pad(vectors.reshape(8, feats), ((0, 0), (0, units - feats)))
+    vectors = jnp.concatenate((vectors, jnp.pad(b_in[None], ((0, 7), (0, 0)))))
+    wide = jnp.concatenate((jnp.where(odd, w_back, w_in), vectors))
+    x0 = after(x0, flags, wide, *fetched)
     x2 = swap_bit(x0, "col", 2)
     x1 = swap_bit(x0, "col", 1)
-    x3 = swap_bit(x2, "col", 1)
-    swapped = [swap_bit(part, "dp", 1) for part in fetched]
-
-    vectors = jnp.concatenate((b_out, ln1_gain, ln1_bias, b_back, ln2_gain, ln2_bias))
-    vectors = jnp.pad(vectors.reshape(6, feats), ((0, 10), (0, units - feats)))
-    wide = jnp.concatenate((jnp.where(odd, w_back, w_in), vectors))
+    swapped = swap_bit(jnp.concatenate(fetched), "dp", 1)
     wide = after(wide, *fetched)
-    wide_fetched = [from_row(wide, k) for k in range(1, n_rows)]
-    wide_swapped = [swap_bit(part, "dp", 1) for part in wide_fetched]
-    in_all = jnp.concatenate(
-        [w_in]
-        + [jnp.where(odd, o[:feats], f[:feats]) for f, o in zip(wide_fetched, wide_swapped)]
-    )
-    back_all = jnp.concatenate(
-        [w_back]
-        + [jnp.where(odd, f[:feats], o[:feats]) for f, o in zip(wide_fetched, wide_swapped)]
-    )
-    at_vectors = pl.BlockSpec((16, units), lambda _: (feats // 16, 0))
-    (vecs,) = call(
-        vector_kernel,
-        "vectors",
-        [shape((model, 16), F32)],
-        [vectors] + wide_fetched,
-        specs={k: at_vectors for k in range(1, n_rows)},
-    )
-
-    qkv_bias = jnp.concatenate((q_bias, jnp.zeros_like(q_bias), v_bias)).astype(F32)[:, None]
+    wide_fetched = [from_row(wide, 1)]
+    wide_fetched += [from_row(after(wide, wide_fetched[0]), k) for k in range(2, n_rows)]
+    wide_swapped = [
+        swap_bit(jnp.concatenate(wide_fetched[:2]), "dp", 1),
+        swap_bit(wide_fetched[2], "dp", 1),
+    ]
+    x3 = swap_bit(after(x2, swapped, wide_fetched[0]), "col", 1)
+
+    in_all, back_all, vecs, in_bias = call(
+        assemble_kernel,
+        "assemble",
+        [shape((model, units), BF16)] * 2 + [shape((model, 16), F32), shape((units, 16), F32)],
+        [flags, w_in, w_back, vectors] + wide_fetched + wide_swapped,
+        specs={k: pl.BlockSpec(memory_space=pl.ANY) for k in (1, 2, 4, 5, 6, 7, 8)},
+        scratch=[pltpu.VMEM((3, 16, units), BF16), pltpu.SemaphoreType.DMA((11,))],
+        vmem_mib=56,
+        weight=2,
+    )
+
     xs, packs, qkv, prob, context, mine, other = call(
         attend_kernel,
         "attend",
@@ -479,14 +586,12 @@
             wide_halves,
             halves,
         ],
-        [flags, x0, x1, x2, x3, qkv_part, w_out] + fetched + swapped + [qkv_bias],
-        flops=8 * model * width * slot + 4 * slot * slot * width,
-    )
-
-    g_own = to_slot(after(out_grad.astype(BF16), xs))
-    g_high = swap_bit(g_own, "col", 2)
-    g_both = jnp.concatenate((g_own, g_high))
-    g_low = swap_bit(jnp.where(low_bit, g_both[:, :half], g_both[:, half:]), "col", 1)
+        [flags, x0, x1, x2, x3, qkv_part, w_out] + fetched + [swapped, vectors],
+        specs={k: pl.BlockSpec(memory_space=pl.ANY) for k in range(1, 11)},
+        scratch=[pltpu.VMEM((model, slot), BF16), pltpu.SemaphoreType.DMA((12,))],
+        vmem_mib=56,
+        weight=12,
+    )
 
     own = sum_cores(mine, other)
     away = swap_bit(own, "col", 2)
@@ -496,16 +601,23 @@
         [wide_halves, shape((8, half), F32), halves],
         [xs, own, away, vecs],
         specs={0: pl.BlockSpec((model, half), lambda _: (0, 0))},
-    )
+        windowed=True,
+        weight=2,
+    )
+    g_own = to_slot(after(out_grad.astype(BF16), wide_fetched[2]))
+    g_high = swap_bit(after(g_own, scaled_one), "col", 2)
+
     n_away = swap_bit(n_own, "col", 1)
     hidden, slope, mine, other = call(
         forward_kernel,
         "feed_forward",
         [shape((units, slot), BF16), shape((units, slot), BF16), wide_halves, halves],
-        [n_own, n_away, in_all, back_all, b_in.astype(F32)[:, None]],
-        flops=4 * model * units * slot,
-    )
-    own = sum_cores(mine, other)
+        [n_own, n_away, in_all, back_all, in_bias],
+        weight=6,
+    )
+    g_both = jnp.concatenate((after(g_own, hidden), g_high))
+    g_low = swap_bit(jnp.where(low_bit, g_both[:, :half], g_both[:, half:]), "col", 1)
+    own = sum_cores(after(mine, g_low), other)
     away = swap_bit(own, "col", 2)
     out_own, out_give, grad_second, r_own, sums = call(
         turn_kernel,
@@ -519,6 +631,7 @@
         ],
         [flags, scaled_one, own, away, vecs, g_own, g_high, g_low],
         scratch=[pltpu.VMEM((model, half), BF16), pltpu.VMEM((model, half), BF16)],
+        weight=4,
     )
     r_away = swap_bit(r_own, "col", 1)
     mine, other, grad_pre, b_in_sums = call(
@@ -526,22 +639,23 @@
         "feed_backward",
         [wide_halves, halves, shape((units, slot), BF16), shape((8, feats), F32)],
         [r_own, r_away, slope, in_all, back_all],
-        flops=4 * model * units * slot,
+        weight=3,
     )
     own = sum_cores(mine, other)
-    wide_grads = call(
+    *back_grads, into_keep, into_give = call(
         wide_grad_kernel,
         "wide_grads",
-        [shape((feats, units), BF16)] * (2 * n_rows),
-        [after(r_own, own), r_away, hidden, n_own, n_away, grad_pre],
-        flops=4 * model * units * slot,
+        [shape((feats, units), BF16)] * n_rows + [shape((n_rows, feats // 2, units), BF16)] * 2,
+        [flags, after(r_own, own), r_away, hidden, n_own, n_away, grad_pre],
+        weight=8,
     )
     away = swap_bit(own, "col", 2)
     grad_first, a_own, sums = call(
         norm_back_kernel,
         "norm_back",
         [wide_halves, halves, shape((8, model), F32)],
-        [own, away, grad_second, scaled_one, inverse_one, vecs, sums],
+        [own, after(away, into_give), grad_second, scaled_one, inverse_one, vecs, sums],
+        weight=2,
     )
     a_away = swap_bit(a_own, "col", 1)
     sums_away = swap_bit(sums, "col", 1)
@@ -554,63 +668,43 @@
             shape((2 * feats, slot), BF16),
         ],
         [flags, a_own, a_away, packs, qkv, prob, grad_first],
-        flops=8 * model * width * slot + 10 * slot * slot * width,
         scratch=[pltpu.VMEM((width, slot), BF16)],
-    )
-
-    in_own, in_away = call(
-        join_kernel,
-        "join",
-        [shape((feats, slot), F32), shape((feats, slot), BF16)],
-        [flags, kept, swap_bit(give, "col", 1)],
-    )
-    (in_grad,) = call(
-        finish_kernel,
-        "finish",
-        [shape((feats, slot), BF16)],
-        [flags, in_own, swap_bit(in_away, "col", 2)],
-    )
-    in_grad = from_slot(in_grad).astype(F32)
-
-    out_give = after(out_give, a_own)
-    layer_out = from_slot(ordered(low_bit, out_own, swap_bit(out_give, "col", 1), 1))
-
-    def add_rows(blocks):
-        terms = [blocks[0]] + [from_row(blocks[k], n_rows - k) for k in range(1, n_rows)]
-        terms = [term.astype(F32) for term in terms]
-        while len(terms) > 1:
-            pairs = len(terms) // 2
-            terms = [terms[i] + terms[i + pairs] for i in range(pairs)]
-        return terms[0].astype(BF16)
-
-    def add_replicas(total, first):
-        bit = first
-        while bit < lax.axis_size("dp"):
-            total = total.astype(F32) + swap_bit(total, "dp", bit).astype(F32)
-            total = total.astype(BF16)
-            bit *= 2
-        return total
+        weight=8,
+    )
 
     pack_keep, pack_give = call(
         pack_grad_kernel,
         "pack_grads",
         [shape((n_rows, 2 * width + EXTRA // 2, feats), BF16)] * 2,
         [flags, xs, grad_qkv, a_own, a_away, context, sums, sums_away, b_in_sums],
-        flops=8 * model * width * slot,
         scratch=[pltpu.VMEM((4 * width + EXTRA, feats), BF16)],
-    )
-    w_back_grad = add_replicas(add_rows(wide_grads[:n_rows]), 1).astype(F32)
-    w_in_grad = add_replicas(add_rows(wide_grads[n_rows:]), 1).astype(F32)
+        weight=5,
+    )
+
+    in_own, in_away = call(
+        join_kernel,
+        "join",
+        [shape((feats, slot), F32), shape((feats, slot), BF16)],
+        [flags, after(kept, pack_give), swap_bit(give, "col", 1)],
+    )
+    (in_done,) = call(
+        finish_kernel,
+        "finish",
+        [shape((feats, slot), BF16)],
+        [flags, in_own, swap_bit(in_away, "col", 2)],
+    )
+    in_grad = from_slot(in_done).astype(F32)
+
+    into_got = swap_bit(into_give, "dp", 1)
+
+    out_give = after(out_give, in_away)
+    layer_out = from_slot(ordered(low_bit, out_own, swap_bit(out_give, "col", 1), 1))
+
+    w_back_grad = add_replicas(add_rows(back_grads, in_away), 1).astype(F32)
+    w_in_grad = add_shares(into_keep, after(into_got, in_away)).astype(F32)
     pack_got = swap_bit(pack_give, "dp", 1)
-    total = add_rows(
-        [
-            (pack_keep[k].astype(F32) + pack_got[k].astype(F32)).astype(BF16)
-            for k in range(n_rows)
-        ]
-    )
-    total = add_replicas(total, 2)
-    total = ordered(odd, total, swap_bit(total, "dp", 1), 0).astype(F32)
-    w_qkv_grad = total[: 3 * width].reshape(3, width, feats).transpose(2, 0, 1)
+    total = add_shares(pack_keep, after(pack_got, in_done)).astype(F32)
+    w_qkv_grad = total[: 3 * feats].reshape(3, feats, width).transpose(1, 0, 2)
     w_out_grad = total[3 * width : 4 * width]
     tail = total[4 * width :]
     return (

time: 258 us -> 233 us (0.903)
  waiting for transfers between devices: 134 us -> 118 us
  starting transfers between devices: 62 us -> 51.4 us
  Pallas kernels: 25.3 us -> 33.2 us
  local copies, waits for them, and re-layouts: 20.9 us -> 18 us
    ppermute x15, waiting for transfers between devices: 76 us -> 56.6 us  [from_row(): lax.ppermute(value, 'row', [((a + away) % size, a) for a in range(size)])]
    pallas_call x12 -> x13, Pallas kernels: 25.3 us -> 33.2 us  [call(): pl.pallas_call(kernel, name=name, out_shape=outs, grid=(1,) if windowed e...]
    ppermute x2, starting transfers between devices: 10.1 us -> 4.22 us  [from_slot(): lax.ppermute(value, ('row', 'col'), [(b, a) for a, b in grid_pairs()])]
    ppermute x28 -> x26, starting transfers between devices: 21.8 us -> 16.8 us  [swap_bit(): return lax.ppermute(value, axis, [(at, at ^ bit) for at in range(size)])]
    unnamed x113 -> x100, local copies, waits for them, and re-layouts: 14.3 us -> 9.74 us
    ppermute x28 -> x26, waiting for transfers between devices: 49.9 us -> 53.5 us  [swap_bit(): return lax.ppermute(value, axis, [(at, at ^ bit) for at in range(size)])]
  transfers between devices with their start and end apart: 47 -> 45, of which waited for: 29 -> 20; matrix products, arithmetic and copies ran while one was open for 6% -> 7% of each run, Pallas kernels for 6% -> 12%
where the time goes in v4:
time: 233 us
  waiting for transfers between devices  118 us (51%)
  starting transfers between devices  51.4 us (22%)
  Pallas kernels  33.2 us (14%)
  local copies, waits for them, and re-layouts  18 us (8%)
  other arithmetic  10.5 us (5%)
    ppermute x15, waiting for transfers between devices, from_row(): lax.ppermute(value, 'row', [((a + away) % size, a) for a in range(size)])  56.6 us
    ppermute x26, waiting for transfers between devices, swap_bit(): return lax.ppermute(value, axis, [(at, at ^ bit) for at in range(size)])  53.5 us
    pallas_call x13, Pallas kernels, call(): pl.pallas_call(kernel, name=name, out_shape=outs, grid=(1,) if windowed e...  33.2 us
    ppermute x15, starting transfers between devices, from_row(): lax.ppermute(value, 'row', [((a + away) % size, a) for a in range(size)])  25.1 us
    ppermute x26, starting transfers between devices, swap_bit(): return lax.ppermute(value, axis, [(at, at ^ bit) for at in range(size)])  16.8 us
    unnamed x100, local copies, waits for them, and re-layouts  9.74 us
    ppermute x2, waiting for transfers between devices, to_slot(): return lax.ppermute(value, ('row', 'col'), grid_pairs())  8.12 us
    ppermute x2, starting transfers between devices, to_slot(): return lax.ppermute(value, ('row', 'col'), grid_pairs())  5.29 us
  transfers between devices with their start and end apart: 45, of which 20 were waited for; matrix products, arithmetic and copies ran while one was open for 7% of the time, Pallas kernels for 12%

profile of v4, /device:TPU:20, one launch (start us, length us, event | category | flops | bytes accessed | tf_op | source)
XLA Modules:
  0.0 232.7 jit_solution(17155418750273355481)
XLA Ops:
  8.4 14.9 %collective-permute-done.3.f3 = bf16[384,192]{1,0:T(8,128)(2,1)S(1)} collective-permute-done((bf16[384,192]{1,0:T(8,128)(2,1)S(1)}, bf16[384,192]{1,0:T(8,128)(2,1)S(1)}, u32[]{:S(2)}, u32[]{:S(2)}) %collective-permute-start.3) | collective-permute-done | bytes 147488 | tf_op jit(solution)/shard_map/ppermute | solution.py:69
  25.8 3.8 %collective-permute-start.7 = (bf16[208,768]{1,0:T(8,128)(2,1)S(1)}, bf16[208,768]{1,0:T(8,128)(2,1)S(1)}, u32[]{:S(2)}, u32[]{:S(2)}) collective-permute-start(bf16[208,768]{1,0:T(8,128)(2,1)S(1)} %pad_maximum_fusion.2), channel_id=1, source_target_pairs={{4,0},{8,4},{12,8},{0,12},{5,1},{9,5},{13,9},{1,13},{6,2},{10,6},{... | collective-permute-start | bytes 958472 | tf_op jit(solution)/shard_map/ppermute | solution.py:69
  32.6 4.9 %collective-permute-done.5.x2 = bf16[192,512]{1,0:T(8,128)(2,1)S(1)} collective-permute-done((bf16[192,512]{1,0:T(8,128)(2,1)S(1)}, bf16[192,512]{1,0:T(8,128)(2,1)S(1)}, u32[]{:S(2)}, u32[]{:S(2)}) %collective-permute-start.5) | collective-permute-done | bytes 196640 | tf_op jit(solution)/shard_map/ppermute | solution.py:49
  38.3 3.8 %collective-permute-start.11 = (bf16[208,768]{1,0:T(8,128)(2,1)S(1)}, bf16[208,768]{1,0:T(8,128)(2,1)S(1)}, u32[]{:S(2)}, u32[]{:S(2)}) collective-permute-start(bf16[208,768]{1,0:T(8,128)(2,1)S(1)} %pad_maximum_fusion.2), channel_id=1, source_target_pairs={{8,0},{12,4},{0,8},{4,12},{9,1},{13,5},{1,9},{5,13},{10,2},{14,6},... | collective-permute-start | bytes 958472 | tf_op jit(solution)/shard_map/ppermute | solution.py:69
  44.5 7.8 %attend.1 = (bf16[768,512]{1,0:T(8,128)(2,1)}, bf16[4,768,192]{2,1,0:T(8,128)(2,1)}, bf16[576,512]{1,0:T(8,128)(2,1)}, bf16[3,512,512]{2,1,0:T(8,128)(2,1)}, bf1...) custom-call(s32[6]{0:T(128)} %stack.24.flags, bf16[192,512]{1,0:T(8,128)(2,1)} %copy-done.44, ...), custom_call_target="tpu_custom_call" | custom-call | flops 12884901888 | bytes 50331648 | tf_op jit(solution)/shard_map/attend/pallas_call | solution.py:28
  52.5 9.2 %collective-permute-done.11.f2 = bf16[208,768]{1,0:T(8,128)(2,1)S(1)} collective-permute-done((bf16[208,768]{1,0:T(8,128)(2,1)S(1)}, bf16[208,768]{1,0:T(8,128)(2,1)S(1)}, u32[]{:S(2)}, u32[]{:S(2)}) %collective-permute-start.11) | collective-permute-done | bytes 319520 | tf_op jit(solution)/shard_map/ppermute | solution.py:69
  65.5 19.5 %collective-permute-done.14.s3 = bf16[208,768]{1,0:T(8,128)(2,1)S(1)} collective-permute-done((bf16[208,768]{1,0:T(8,128)(2,1)S(1)}, bf16[208,768]{1,0:T(8,128)(2,1)S(1)}, u32[]{:S(2)}, u32[]{:S(2)}) %collective-permute-start.14) | collective-permute-done | bytes 319520 | tf_op jit(solution)/shard_map/ppermute | solution.py:49
  86.7 4.1 %assemble.1 = (bf16[768,768]{1,0:T(8,128)(2,1)}, bf16[768,768]{1,0:T(8,128)(2,1)}, f32[768,16]{1,0:T(8,128)}, f32[768,16]{1,0:T(8,128)}) custom-call(s32[6]{0:T(128)} %stack.24.flags, bf16[192,768]{1,0:T(8,128)(2,1)} %own_in.1, bf16[192,768]{1,0:T(8,128)(2,1)} %own_back.1, bf16[16,768]{1,0:T(8,128)(2,1)} %pad_maximum_fusion.4.vectors.v0, ...), custom_call_target="tpu_custom_call" | custom-call | flops 2147483648 | bytes 8388608 | tf_op jit(solution)/shard_map/assemble/pallas_call | solution.py:28
  94.0 3.0 %collective-permute-start.16 = (bf16[192,512]{1,0:T(8,128)(2,1)}, bf16[192,512]{1,0:T(8,128)(2,1)S(1)}, u32[]{:S(2)}, u32[]{:S(2)}) collective-permute-start(bf16[192,512]{1,0:T(8,128)(2,1)} %convert_element_type.207), channel_id=1, source_target_pairs={{0,0},{1,7},{2,10},{3,13},{4,1},{5,4},{6,11},{7,14},{8,2},{9,5},{1... | collective-permute-start | bytes 589832 | tf_op jit(solution)/shard_map/ppermute | solution.py:60
  97.0 8.1 %collective-permute-done.16.g_own = bf16[192,512]{1,0:T(8,128)(2,1)S(1)} collective-permute-done((bf16[192,512]{1,0:T(8,128)(2,1)}, bf16[192,512]{1,0:T(8,128)(2,1)S(1)}, u32[]{:S(2)}, u32[]{:S(2)}) %collective-permute-start.16) | collective-permute-done | bytes 196640 | tf_op jit(solution)/shard_map/ppermute | solution.py:60
  109.3 3.3 %collective-permute-done.17.g_high = bf16[192,512]{1,0:T(8,128)(2,1)S(1)} collective-permute-done((bf16[192,512]{1,0:T(8,128)(2,1)S(1)}, bf16[192,512]{1,0:T(8,128)(2,1)S(1)}, u32[]{:S(2)}, u32[]{:S(2)}) %collective-permute-start.17) | collective-permute-done | bytes 196640 | tf_op jit(solution)/shard_map/ppermute | solution.py:49
  114.7 10.9 %collective-permute-done.20.away = bf16[768,256]{1,0:T(8,128)(2,1)S(1)} collective-permute-done((bf16[768,256]{1,0:T(8,128)(2,1)S(1)}, bf16[768,256]{1,0:T(8,128)(2,1)S(1)}, u32[]{:S(2)}, u32[]{:S(2)}) %collective-permute-start.20) | collective-permute-done | bytes 393248 | tf_op jit(solution)/shard_map/ppermute | solution.py:49
  125.6 2.5 %turn.1 = (bf16[192,256]{1,0:T(8,128)(2,1)S(1)}, bf16[192,256]{1,0:T(8,128)(2,1)S(1)}, f32[768,256]{1,0:T(8,128)S(1)}, bf16[768,256]{1,0:T(8,128)(2,1)S(1)}, f32[8,768]{1,0:T(8,128)S(1)}) custom-call(s32[6]{0:T(128)S(1)} %copy-done, f32[768,256]{1,0:T(8,128)S(1)} %copy-done.12, bf16[768,256]{1,0:T(8,128)(2,1)S(1)} %add_convert_fusion.1.own, ...), custom_call_target="tpu_custom_call" | custom-call | flops 4294967296 | bytes 16777216 | tf_op jit(solution)/shard_map/turn/pallas_call | solution.py:28
  133.8 4.2 %wide_grads.1 = (bf16[192,768]{1,0:T(8,128)(2,1)S(1)}, bf16[192,768]{1,0:T(8,128)(2,1)}, bf16[192,768]{1,0:T(8,128)(2,1)S(1)}, bf16[192,768]{1,0:T(8,128)(2,1)},...) custom-call(s32[6]{0:T(128)S(1)} %copy-done, bf16[768,256]{1,0:T(8,128)(2,1)S(1)} %get-tuple-element.100.r_own, ...), custom_call_target="tpu_custom_call" | custom-call | flops 8589934592 | bytes 33554432 | tf_op jit(solution)/shard_map/wide_grads/pallas_call | solution.py:28
  138.0 6.6 %collective-permute-done.23.away = bf16[768,256]{1,0:T(8,128)(2,1)S(1)} collective-permute-done((bf16[768,256]{1,0:T(8,128)(2,1)S(1)}, bf16[768,256]{1,0:T(8,128)(2,1)S(1)}, u32[]{:S(2)}, u32[]{:S(2)}) %collective-permute-start.23) | collective-permute-done | bytes 393248 | tf_op jit(solution)/shard_map/ppermute | solution.py:49
  146.5 2.6 %collective-permute-start.41 = (bf16[192,768]{1,0:T(8,128)(2,1)S(1)}, bf16[192,768]{1,0:T(8,128)(2,1)}, u32[]{:S(2)}, u32[]{:S(2)}) collective-permute-start(bf16[192,768]{1,0:T(8,128)(2,1)S(1)} %get-tuple-element.129), channel_id=1, source_target_pairs={{8,0},{12,4},{0,8},{4,12},{9,1},{13,5},{1,9},{5,13},{10,2},{14,6},... | collective-permute-start | bytes 884744 | tf_op jit(solution)/shard_map/ppermute | solution.py:69
  151.2 5.3 %attend_back.1 = (bf16[576,512]{1,0:T(8,128)(2,1)S(1)}, f32[384,512]{1,0:T(8,128)S(1)}, bf16[384,512]{1,0:T(8,128)(2,1)}) custom-call(s32[6]{0:T(128)S(1)} %copy-done, bf16[768,256]{1,0:T(8,128)(2,1)S(1)} %get-tuple-element.107.a_own, bf16[768,256]{1,0:T(8,128)(2,1)S(1)} %collective-permute-done.24.a_away, bf16[4,768,192]{2,1,0:T(8,128)(2,1)S(1)} %copy-done.18, ...), custom_call_target="tpu_custom_call" | custom-call | flops 8589934592 | bytes 33554432 | tf_op jit(solution)/shard_map/attend_back/pallas_call | solution.py:28
  164.3 8.6 %collective-permute-done.43 = bf16[192,768]{1,0:T(8,128)(2,1)} collective-permute-done((bf16[192,768]{1,0:T(8,128)(2,1)}, bf16[192,768]{1,0:T(8,128)(2,1)}, u32[]{:S(2)}, u32[]{:S(2)}) %collective-permute-start.43) | collective-permute-done | bytes 294944 | tf_op jit(solution)/shard_map/ppermute | solution.py:69
  176.0 2.5 %collective-permute-start.39 = (bf16[96,768]{1,0:T(8,128)(2,1)S(1)}, bf16[96,768]{1,0:T(8,128)(2,1)S(1)}, u32[]{:S(2)}, u32[]{:S(2)}) collective-permute-start(bf16[96,768]{1,0:T(8,128)(2,1)S(1)} %get-tuple-element.139), channel_id=1, source_target_pairs={{4,0},{8,4},{12,8},{0,12},{5,1},{9,5},{13,9},{1,13},{6,2},{10,6},{... | collective-permute-start | bytes 442376 | tf_op jit(solution)/shard_map/ppermute | solution.py:69
  184.9 2.9 %collective-permute-done.39 = bf16[96,768]{1,0:T(8,128)(2,1)S(1)} collective-permute-done((bf16[96,768]{1,0:T(8,128)(2,1)S(1)}, bf16[96,768]{1,0:T(8,128)(2,1)S(1)}, u32[]{:S(2)}, u32[]{:S(2)}) %collective-permute-start.39) | collective-permute-done | bytes 147488 | tf_op jit(solution)/shard_map/ppermute | solution.py:69
  199.8 3.1 %collective-permute-start.33 = (bf16[400,192]{1,0:T(8,128)(2,1)S(1)}, bf16[400,192]{1,0:T(8,128)(2,1)S(1)}, u32[]{:S(2)}, u32[]{:S(2)}) collective-permute-start(bf16[400,192]{1,0:T(8,128)(2,1)S(1)} %get-tuple-element.137), channel_id=1, source_target_pairs={{12,0},{0,4},{4,8},{8,12},{13,1},{1,5},{5,9},{9,13},{14,2},{2,6},{... | collective-permute-start | bytes 460808 | tf_op jit(solution)/shard_map/ppermute | solution.py:69
  207.4 10.4 %collective-permute-done.34 = bf16[400,192]{1,0:T(8,128)(2,1)S(1)} collective-permute-done((bf16[400,192]{1,0:T(8,128)(2,1)S(1)}, bf16[400,192]{1,0:T(8,128)(2,1)S(1)}, u32[]{:S(2)}, u32[]{:S(2)}) %collective-permute-start.34) | collective-permute-done | bytes 153632 | tf_op jit(solution)/shard_map/ppermute | solution.py:69
  217.8 4.7 %collective-permute-done.33 = bf16[400,192]{1,0:T(8,128)(2,1)S(1)} collective-permute-done((bf16[400,192]{1,0:T(8,128)(2,1)S(1)}, bf16[400,192]{1,0:T(8,128)(2,1)S(1)}, u32[]{:S(2)}, u32[]{:S(2)}) %collective-permute-start.33) | collective-permute-done | bytes 153632 | tf_op jit(solution)/shard_map/ppermute | solution.py:69
  225.6 3.5 %collective-permute-done.35 = bf16[400,192]{1,0:T(8,128)(2,1)S(1)} collective-permute-done((bf16[400,192]{1,0:T(8,128)(2,1)S(1)}, bf16[400,192]{1,0:T(8,128)(2,1)S(1)}, u32[]{:S(2)}, u32[]{:S(2)}) %collective-permute-start.35) | collective-permute-done | bytes 153632 | tf_op jit(solution)/shard_map/ppermute | solution.py:49
  (219 shorter events, 80.9 us)
Async XLA Ops:
  2.8 20.5 %collective-permute-start.3 = (bf16[384,192]{1,0:T(8,128)(2,1)S(1)}, bf16[384,192]{1,0:T(8,128)(2,1)S(1)}, u32[]{:S(2)}, u32[]{:S(2)}) collective-permute-start(bf16[384,192]{1,0:T(8,128)(2,1)S(1)} %half.1), channel_id=1, source_target_pairs={{12,0},{0,4},{4,8},{8,12},{13,1},{1,5},{5,9},{9,13},{14,2},{2,6},{... | collective-permute-start | bytes 442376 | tf_op jit(solution)/shard_map/ppermute | solution.py:69
  4.4 18.9 %collective-permute-start.2 = (bf16[384,192]{1,0:T(8,128)(2,1)S(1)}, bf16[384,192]{1,0:T(8,128)(2,1)S(1)}, u32[]{:S(2)}, u32[]{:S(2)}) collective-permute-start(bf16[384,192]{1,0:T(8,128)(2,1)S(1)} %half.1), channel_id=1, source_target_pairs={{8,0},{12,4},{0,8},{4,12},{9,1},{13,5},{1,9},{5,13},{10,2},{14,6},... | collective-permute-start | bytes 442376 | tf_op jit(solution)/shard_map/ppermute | solution.py:69
  4.8 18.5 %collective-permute-start.1 = (bf16[384,192]{1,0:T(8,128)(2,1)S(1)}, bf16[384,192]{1,0:T(8,128)(2,1)S(1)}, u32[]{:S(2)}, u32[]{:S(2)}) collective-permute-start(bf16[384,192]{1,0:T(8,128)(2,1)S(1)} %half.1), channel_id=1, source_target_pairs={{4,0},{8,4},{12,8},{0,12},{5,1},{9,5},{13,9},{1,13},{6,2},{10,6},{... | collective-permute-start | bytes 442376 | tf_op jit(solution)/shard_map/ppermute | solution.py:69
  6.1 25.3 %collective-permute-start = (bf16[192,512]{1,0:T(8,128)(2,1)S(1)}, bf16[192,512]{1,0:T(8,128)(2,1)S(1)}, u32[]{:S(2)}, u32[]{:S(2)}) collective-permute-start(bf16[192,512]{1,0:T(8,128)(2,1)S(1)} %copy-done.43), channel_id=1, source_target_pairs={{0,0},{1,7},{2,10},{3,13},{4,1},{5,4},{6,11},{7,14},{8,2},{9,5},{1... | collective-permute-start | bytes 589832 | tf_op jit(solution)/shard_map/ppermute | solution.py:60
  23.8 13.7 %collective-permute-start.6 = (bf16[1152,192]{0,1:T(8,128)(2,1)S(1)}, bf16[1152,192]{0,1:T(8,128)(2,1)S(1)}, u32[]{:S(2)}, u32[]{:S(2)}) collective-permute-start(bf16[1152,192]{0,1:T(8,128)(2,1)S(1)} %copy.31), channel_id=1, source_target_pairs={{0,16},{16,0},{1,17},{17,1},{2,18},{18,2},{3,19},{19,3},{4,20},{20... | collective-permute-start | bytes 1327112 | tf_op jit(solution)/shard_map/ppermute | solution.py:49
  38.3 23.5 %collective-permute-start.11 = (bf16[208,768]{1,0:T(8,128)(2,1)S(1)}, bf16[208,768]{1,0:T(8,128)(2,1)S(1)}, u32[]{:S(2)}, u32[]{:S(2)}) collective-permute-start(bf16[208,768]{1,0:T(8,128)(2,1)S(1)} %pad_maximum_fusion.2), channel_id=1, source_target_pairs={{8,0},{12,4},{0,8},{4,12},{9,1},{13,5},{1,9},{5,13},{10,2},{14,6},... | collective-permute-start | bytes 958472 | tf_op jit(solution)/shard_map/ppermute | solution.py:69
  52.3 12.2 %collective-permute-start.9 = (bf16[768,256]{1,0:T(8,128)(2,1)}, bf16[768,256]{1,0:T(8,128)(2,1)S(1)}, u32[]{:S(2)}, u32[]{:S(2)}) collective-permute-start(bf16[768,256]{1,0:T(8,128)(2,1)} %get-tuple-element.80), channel_id=1, source_target_pairs={{0,1},{1,0},{2,3},{3,2},{4,5},{5,4},{6,7},{7,6},{8,9},{9,8},{10,11... | collective-permute-start | bytes 1179656 | tf_op jit(solution)/shard_map/ppermute | solution.py:49
  61.8 23.3 %collective-permute-start.13 = (bf16[416,768]{1,0:T(8,128)(2,1)S(1)}, bf16[416,768]{1,0:T(8,128)(2,1)S(1)}, u32[]{:S(2)}, u32[]{:S(2)}) collective-permute-start(bf16[416,768]{1,0:T(8,128)(2,1)S(1)} %pad_maximum_fusion), channel_id=1, source_target_pairs={{0,16},{16,0},{1,17},{17,1},{2,18},{18,2},{3,19},{19,3},{4,20},{20... | collective-permute-start | bytes 1916936 | tf_op jit(solution)/shard_map/ppermute | solution.py:49
  64.0 21.1 %collective-permute-start.14 = (bf16[208,768]{1,0:T(8,128)(2,1)S(1)}, bf16[208,768]{1,0:T(8,128)(2,1)S(1)}, u32[]{:S(2)}, u32[]{:S(2)}) collective-permute-start(bf16[208,768]{1,0:T(8,128)(2,1)S(1)} %collective-permute-done.12.f3), channel_id=1, source_target_pairs={{0,16},{16,0},{1,17},{17,1},{2,18},{18,2},{3,19},{19,3},{4,20},{20... | collective-permute-start | bytes 958472 | tf_op jit(solution)/shard_map/ppermute | solution.py:49
  64.6 26.2 %collective-permute-start.10 = (bf16[768,256]{1,0:T(8,128)(2,1)S(1)}, bf16[768,256]{1,0:T(8,128)(2,1)S(1)}, u32[]{:S(2)}, u32[]{:S(2)}) collective-permute-start(bf16[768,256]{1,0:T(8,128)(2,1)S(1)} %add_convert_fusion.2.own), channel_id=1, source_target_pairs={{0,2},{1,3},{2,0},{3,1},{4,6},{5,7},{6,4},{7,5},{8,10},{9,11},{10,... | collective-permute-start | bytes 1179656 | tf_op jit(solution)/shard_map/ppermute | solution.py:49
  93.3 13.1 %collective-permute-start.15 = (bf16[768,256]{1,0:T(8,128)(2,1)S(1)}, bf16[768,256]{1,0:T(8,128)(2,1)S(1)}, u32[]{:S(2)}, u32[]{:S(2)}) collective-permute-start(bf16[768,256]{1,0:T(8,128)(2,1)S(1)} %get-tuple-element.84.n_own), channel_id=1, source_target_pairs={{0,1},{1,0},{2,3},{3,2},{4,5},{5,4},{6,7},{7,6},{8,9},{9,8},{10,11... | collective-permute-start | bytes 1179656 | tf_op jit(solution)/shard_map/ppermute | solution.py:49
  145.8 28.9 %collective-permute-start.36 = (bf16[4,96,768]{2,1,0:T(8,128)(2,1)S(1)}, bf16[4,96,768]{2,1,0:T(8,128)(2,1)}, u32[]{:S(2)}, u32[]{:S(2)}) collective-permute-start(bf16[4,96,768]{2,1,0:T(8,128)(2,1)S(1)} %get-tuple-element.102), channel_id=1, source_target_pairs={{0,16},{16,0},{1,17},{17,1},{2,18},{18,2},{3,19},{19,3},{4,20},{20... | collective-permute-start | bytes 1769480 | tf_op jit(solution)/shard_map/ppermute | solution.py:49
  146.5 28.2 %collective-permute-start.41 = (bf16[192,768]{1,0:T(8,128)(2,1)S(1)}, bf16[192,768]{1,0:T(8,128)(2,1)}, u32[]{:S(2)}, u32[]{:S(2)}) collective-permute-start(bf16[192,768]{1,0:T(8,128)(2,1)S(1)} %get-tuple-element.129), channel_id=1, source_target_pairs={{8,0},{12,4},{0,8},{4,12},{9,1},{13,5},{1,9},{5,13},{10,2},{14,6},... | collective-permute-start | bytes 884744 | tf_op jit(solution)/shard_map/ppermute | solution.py:69
  149.1 25.6 %collective-permute-start.42 = (bf16[192,768]{1,0:T(8,128)(2,1)}, bf16[192,768]{1,0:T(8,128)(2,1)}, u32[]{:S(2)}, u32[]{:S(2)}) collective-permute-start(bf16[192,768]{1,0:T(8,128)(2,1)} %get-tuple-element.131), channel_id=1, source_target_pairs={{12,0},{0,4},{4,8},{8,12},{13,1},{1,5},{5,9},{9,13},{14,2},{2,6},{... | collective-permute-start | bytes 884744 | tf_op jit(solution)/shard_map/ppermute | solution.py:69
  149.1 23.8 %collective-permute-start.43 = (bf16[192,768]{1,0:T(8,128)(2,1)}, bf16[192,768]{1,0:T(8,128)(2,1)}, u32[]{:S(2)}, u32[]{:S(2)}) collective-permute-start(bf16[192,768]{1,0:T(8,128)(2,1)} %get-tuple-element.133), channel_id=1, source_target_pairs={{4,0},{8,4},{12,8},{0,12},{5,1},{9,5},{13,9},{1,13},{6,2},{10,6},{... | collective-permute-start | bytes 884744 | tf_op jit(solution)/shard_map/ppermute | solution.py:69
  160.5 35.3 %collective-permute-start.31 = (bf16[4,400,192]{1,2,0:T(8,128)(2,1)}, bf16[4,400,192]{1,2,0:T(8,128)(2,1)}, u32[]{:S(2)}, u32[]{:S(2)}) collective-permute-start(bf16[4,400,192]{1,2,0:T(8,128)(2,1)} %copy.33), channel_id=1, source_target_pairs={{0,16},{16,0},{1,17},{17,1},{2,18},{18,2},{3,19},{19,3},{4,20},{20... | collective-permute-start | bytes 1843208 | tf_op jit(solution)/shard_map/ppermute | solution.py:49
  172.9 22.2 %collective-permute-start.29 = (bf16[192,512]{1,0:T(8,128)(2,1)S(1)}, bf16[192,512]{1,0:T(8,128)(2,1)S(1)}, u32[]{:S(2)}, u32[]{:S(2)}) collective-permute-start(bf16[192,512]{1,0:T(8,128)(2,1)S(1)} %get-tuple-element.120), channel_id=1, source_target_pairs={{0,2},{1,3},{2,0},{3,1},{4,6},{5,7},{6,4},{7,5},{8,10},{9,11},{10,... | collective-permute-start | bytes 589832 | tf_op jit(solution)/shard_map/ppermute | solution.py:49
  176.0 11.8 %collective-permute-start.39 = (bf16[96,768]{1,0:T(8,128)(2,1)S(1)}, bf16[96,768]{1,0:T(8,128)(2,1)S(1)}, u32[]{:S(2)}, u32[]{:S(2)}) collective-permute-start(bf16[96,768]{1,0:T(8,128)(2,1)S(1)} %get-tuple-element.139), channel_id=1, source_target_pairs={{4,0},{8,4},{12,8},{0,12},{5,1},{9,5},{13,9},{1,13},{6,2},{10,6},{... | collective-permute-start | bytes 442376 | tf_op jit(solution)/shard_map/ppermute | solution.py:69
  179.8 12.7 %collective-permute-start.38 = (bf16[96,768]{1,0:T(8,128)(2,1)S(1)}, bf16[96,768]{1,0:T(8,128)(2,1)S(1)}, u32[]{:S(2)}, u32[]{:S(2)}) collective-permute-start(bf16[96,768]{1,0:T(8,128)(2,1)S(1)} %get-tuple-element.140), channel_id=1, source_target_pairs={{12,0},{0,4},{4,8},{8,12},{13,1},{1,5},{5,9},{9,13},{14,2},{2,6},{... | collective-permute-start | bytes 442376 | tf_op jit(solution)/shard_map/ppermute | solution.py:69
  183.3 40.7 %collective-permute-start.44 = (bf16[192,768]{1,0:T(8,128)(2,1)S(1)}, bf16[192,768]{1,0:T(8,128)(2,1)S(1)}, u32[]{:S(2)}, u32[]{:S(2)}) collective-permute-start(bf16[192,768]{1,0:T(8,128)(2,1)S(1)} %add_convert_fusion.4), channel_id=1, source_target_pairs={{0,16},{16,0},{1,17},{17,1},{2,18},{18,2},{3,19},{19,3},{4,20},{20... | collective-permute-start | bytes 884744 | tf_op jit(solution)/shard_map/ppermute | solution.py:49
  187.8 16.9 %collective-permute-start.28 = (bf16[192,512]{1,0:T(8,128)(2,1)}, bf16[192,512]{1,0:T(8,128)(2,1)S(1)}, u32[]{:S(2)}, u32[]{:S(2)}) collective-permute-start(bf16[192,512]{1,0:T(8,128)(2,1)} %pad_maximum_fusion.3), channel_id=1, source_target_pairs={{0,0},{7,1},{10,2},{13,3},{1,4},{4,5},{11,6},{14,7},{2,8},{5,9},{8... | collective-permute-start | bytes 589832 | tf_op jit(solution)/shard_map/ppermute | solution.py:64
  197.9 19.9 %collective-permute-start.34 = (bf16[400,192]{1,0:T(8,128)(2,1)S(1)}, bf16[400,192]{1,0:T(8,128)(2,1)S(1)}, u32[]{:S(2)}, u32[]{:S(2)}) collective-permute-start(bf16[400,192]{1,0:T(8,128)(2,1)S(1)} %get-tuple-element.136), channel_id=1, source_target_pairs={{4,0},{8,4},{12,8},{0,12},{5,1},{9,5},{13,9},{1,13},{6,2},{10,6},{... | collective-permute-start | bytes 460808 | tf_op jit(solution)/shard_map/ppermute | solution.py:69
  199.8 22.7 %collective-permute-start.33 = (bf16[400,192]{1,0:T(8,128)(2,1)S(1)}, bf16[400,192]{1,0:T(8,128)(2,1)S(1)}, u32[]{:S(2)}, u32[]{:S(2)}) collective-permute-start(bf16[400,192]{1,0:T(8,128)(2,1)S(1)} %get-tuple-element.137), channel_id=1, source_target_pairs={{12,0},{0,4},{4,8},{8,12},{13,1},{1,5},{5,9},{9,13},{14,2},{2,6},{... | collective-permute-start | bytes 460808 | tf_op jit(solution)/shard_map/ppermute | solution.py:69
  204.7 20.2 %collective-permute-start.30 = (bf16[192,512]{1,0:T(8,128)(2,1)S(1)}, bf16[192,512]{1,0:T(8,128)(2,1)S(1)}, u32[]{:S(2)}, u32[]{:S(2)}) collective-permute-start(bf16[192,512]{1,0:T(8,128)(2,1)S(1)} %finish.1), channel_id=1, source_target_pairs={{0,0},{7,1},{10,2},{13,3},{1,4},{4,5},{11,6},{14,7},{2,8},{5,9},{8... | collective-permute-start | bytes 589832 | tf_op jit(solution)/shard_map/ppermute | solution.py:64
  (70 other events, 490.6 us)

commit v5 on v4

--- a/solution.py
+++ b/solution.py
@@ -18,7 +18,7 @@
     )
 
 
-def call(kernel, name, outs, args, weight=1, scratch=(), specs=None, windowed=False, vmem_mib=16):
+def call(kernel, name, outs, args, weight=0, scratch=(), specs=None, windowed=False, vmem_mib=16, out_specs=None):
     vmem = pl.BlockSpec(memory_space=pltpu.VMEM)
     in_specs = [
         pl.BlockSpec(memory_space=pltpu.SMEM) if arg.dtype == jnp.int32 else vmem for arg in args
@@ -31,7 +31,7 @@
         out_shape=outs,
         grid=(1,) if windowed else (),
         in_specs=in_specs,
-        out_specs=[vmem] * len(outs),
+        out_specs=out_specs or [vmem] * len(outs),
         scratch_shapes=list(scratch),
         compiler_params=pltpu.CompilerParams(vmem_limit_bytes=vmem_mib * 1024 * 1024),
         cost_estimate=pl.CostEstimate(
@@ -49,10 +49,16 @@
     return lax.ppermute(value, axis, [(at, at ^ bit) for at in range(size)])
 
 
+def plane_of(slot):
+    return (slot % 2) * 2 + slot // 2
+
+
 def grid_pairs():
     size = lax.axis_size("row")
     return [
-        (a * size + b, b * size + (a - b) % size) for a in range(size) for b in range(size)
+        (a * size + b, plane_of(b) * size + (a - plane_of(b)) % size)
+        for a in range(size)
+        for b in range(size)
     ]
 
 
@@ -95,47 +101,55 @@
     return total
 
 
-def half_kernel(odd, w_qkv, w_out, out, sems):
+def send_kernel(
+    odd, w_qkv, w_out, w_in, w_back, b_in, v0, v1, v2, v3, v4, v5, v6, v7,
+    half, wide, vectors, blocks, long_line, sems, *lines,
+):
     size = w_out.shape[0]
-
-    def move(copies):
-        for copy in copies:
-            copy.start()
-        for copy in copies:
-            copy.wait()
-
-    @pl.when(odd[0] == 0)
-    def _():
-        move([pltpu.make_async_copy(w_qkv.at[pl.ds(0, 2 * size)], out, sems.at[0])])
-
-    @pl.when(odd[0] == 1)
-    def _():
-        first, second = out.at[pl.ds(0, size)], out.at[pl.ds(size, size)]
-        move(
-            [
-                pltpu.make_async_copy(w_qkv.at[pl.ds(2 * size, size)], first, sems.at[0]),
-                pltpu.make_async_copy(w_out, second, sems.at[1]),
-            ]
-        )
+    feats = w_in.shape[0]
+    copies = [pltpu.make_async_copy(b_in, long_line, sems.at[0])]
+    for at, ref in enumerate((v0, v1, v2, v3, v4, v5, v6, v7)):
+        copies += [pltpu.make_async_copy(ref, lines[at], sems.at[at + 1])]
+    into = wide.at[pl.ds(0, feats)]
+    for part in range(2):
+
+        @pl.when(odd[0] == part)
+        def _():
+            pltpu.make_async_copy((w_in, w_back)[part], into, sems.at[9]).start()
+            first = w_qkv.at[pl.ds(2 * part * size, size)]
+            pltpu.make_async_copy(first, blocks.at[0], sems.at[10]).start()
+            second = (w_qkv.at[pl.ds(size, size)], w_out)[part]
+            pltpu.make_async_copy(second, blocks.at[1], sems.at[11]).start()
+
+    for copy in copies:
+        copy.start()
+    vectors[...] = jnp.zeros_like(vectors)
+    for copy in copies:
+        copy.wait()
+    for at in range(8):
+        vectors[at : at + 1, :feats] = lines[at][...].reshape(1, feats)
+    vectors[8:9, :] = long_line[...].reshape(1, long_line.shape[0])
+    wide[feats:] = vectors[...]
+    pltpu.make_async_copy(w_in, into, sems.at[9]).wait()
+    for at in range(2):
+        pltpu.make_async_copy(w_out, blocks.at[at], sems.at[10 + at]).wait()
+        half[:, at * size : (at + 1) * size] = blocks[at]
 
 
 def attend_kernel(
-    flags, x0, x1, x2, x3, w_qkv, w_out, f1, f2, f3, swapped, vectors,
+    flags, x0, x1, x2, x3, fetched, swapped, vectors,
     xs, packs, qkv, prob, context, mine, other, raw, sems,
 ):
     low, odd, col, length = flags[0], flags[1], flags[2], flags[3]
     feats, slot = x0.shape
     half = slot // 2
-    width = w_out.shape[0]
-    n_half = f1.shape[0]
-    copies = [
-        pltpu.make_async_copy(w_qkv, packs.at[0, pl.ds(0, 3 * width)], sems.at[0]),
-        pltpu.make_async_copy(w_out, packs.at[0, pl.ds(3 * width, width)], sems.at[1]),
-    ]
-    for k, f in enumerate((f1, f2, f3)):
-        for ref, part in ((f, odd), (swapped.at[pl.ds(k * n_half, n_half)], 1 - odd)):
-            rows = pl.ds(pl.multiple_of(part * n_half, n_half), n_half)
-            copies += [pltpu.make_async_copy(ref, packs.at[k + 1, rows], sems.at[len(copies)])]
+    width = context.shape[0]
+    row = flags[5]
+    copies = []
+    for k in range(4):
+        for ref, part in ((fetched, odd), (swapped, 1 - odd)):
+            ref = ref.at[lax.rem(row + k, 4)]
+            copies += [pltpu.make_async_copy(ref, packs.at[k, part], sems.at[len(copies)])]
     for bit, ref in enumerate((x0, x1, x2, x3)):
         rows = pl.ds(pl.multiple_of((col ^ bit) * feats, feats), feats)
         copies += [pltpu.make_async_copy(ref, raw.at[rows], sems.at[len(copies)])]
@@ -157,7 +171,7 @@
     for part, bias in enumerate((columns[:, 6:7], 0.0, columns[:, 7:8])):
         total = bias
         for k in range(4):
-            block = packs[k, part * feats : (part + 1) * feats]
+            block = packs[k, part // 2, :, part % 2 * width : (part % 2 + 1) * width]
             total = total + dot(block, xs[k * feats : (k + 1) * feats], 0, 0)
         qkv[part * width : (part + 1) * width] = total.astype(BF16)
 
@@ -181,13 +195,13 @@
 
     for k in range(4):
         rows = slice(k * feats, (k + 1) * feats)
-        part = dot(packs[k, 3 * width :], context[...], 0, 0)
+        part = dot(packs[k, 1, :, width:], context[...], 0, 0)
         mine[rows] = part[:, :half]
         other[rows] = part[:, half:].astype(BF16)
 
 
 def assemble_kernel(
-    flags, own_in, own_back, v0, f1, f2, f3, s12, s3, w_in, w_back, vecs, bias, rows, sems
+    flags, own_in, own_back, v0, f1, f2, f3, s1, s2, s3, w_in, w_back, vecs, bias, rows, sems
 ):
     odd = flags[1]
     feats = own_in.shape[0]
@@ -196,12 +210,11 @@
         pltpu.make_async_copy(own_in, w_in.at[first], sems.at[0]),
         pltpu.make_async_copy(own_back, w_back.at[first], sems.at[1]),
     ]
-    size = f1.shape[0]
-    for k, (f, s, s_at) in enumerate(((f1, s12, 0), (f2, s12, size), (f3, s3, 0))):
+    for k, (f, s) in enumerate(((f1, s1), (f2, s2), (f3, s3))):
         span = pl.ds((k + 1) * feats, feats)
-        s = s.at[pl.ds(s_at, feats)]
-        for ref, into in ((f.at[first], (w_in, w_back)), (s, (w_back, w_in))):
+        for ref, into in ((f, (w_in, w_back)), (s, (w_back, w_in))):
             at = len(copies)
+            ref = ref.at[first]
             even = pltpu.make_async_copy(ref, into[0].at[span], sems.at[at])
             other = pltpu.make_async_copy(ref, into[1].at[span], sems.at[at])
             copies += [(even, other)]
@@ -325,21 +338,21 @@
 
 
 def wide_grad_kernel(
-    flags, r_own, r_away, hidden, n_own, n_away, grad_pre, b0, b1, b2, b3, keep, give
+    flags, r_own, r_away, hidden, n_own, n_away, grad_pre, b_keep, b_give, i_keep, i_give
 ):
     odd = flags[1]
     half = r_own.shape[1]
-    feats = b0.shape[0]
-    part = feats // 2
-    for k, out in enumerate((b0, b1, b2, b3)):
-        rows = slice(k * feats, (k + 1) * feats)
-        total = dot(r_own[rows], hidden[:, :half], 1, 1)
-        out[...] = (total + dot(r_away[rows], hidden[:, half:], 1, 1)).astype(BF16)
+    part = b_keep.shape[1]
     for k in range(4):
-        for out, at in ((keep, odd), (give, 1 - odd)):
-            rows = pl.ds(pl.multiple_of(k * feats + at * part, part), part)
-            total = dot(n_own[rows, :], grad_pre[:, :half], 1, 1)
-            out[k] = (total + dot(n_away[rows, :], grad_pre[:, half:], 1, 1)).astype(BF16)
+        for pick, b_out, i_out in ((1 - odd, b_give, i_give), (odd, b_keep, i_keep)):
+            rows = pl.ds(pl.multiple_of((2 * k + pick) * part, part), part)
+            for out, own, away, right in (
+                (b_out, r_own, r_away, hidden),
+                (i_out, n_own, n_away, grad_pre),
+            ):
+                total = dot(own[rows, :], right[:, :half], 1, 1)
+                total = total + dot(away[rows, :], right[:, half:], 1, 1)
+                out[k] = total.astype(BF16)
 
 
 def norm_back_kernel(
@@ -366,9 +379,7 @@
         cols = slice(part * half, (part + 1) * half)
         total = 0.0
         for k in range(4):
-            total = total + dot(
-                packs[k, 3 * width :], ref[k * feats : (k + 1) * feats], 1, 0
-            )
+            total = total + dot(packs[k, 1, :, width:], ref[k * feats : (k + 1) * feats], 1, 0)
         grad_context[:, cols] = total.astype(BF16)
     scale = HEAD_DIM ** (-0.5)
     for h in range(width // HEAD_DIM):
@@ -392,7 +403,7 @@
     def block(k):
         part = 0.0
         for at in range(3):
-            left = packs[k, at * feats : (at + 1) * feats]
+            left = packs[k, at // 2, :, at % 2 * width : (at % 2 + 1) * width]
             part = part + dot(left, grad_qkv[at * width : (at + 1) * width], 1, 0)
         rows = pl.ds(pl.multiple_of(k * feats, feats), feats)
         return part[:, :half] + 0.5 * grad_first[rows, :], part[:, half:]
@@ -408,40 +419,71 @@
 
 
 def pack_grad_kernel(
-    flags, xs, grad_qkv, a_own, a_away, context, sums, sums_away, b_in_sums, keep, give, pack
+    flags, xs, grad_qkv, a_own, a_away, context, sums, sums_away, b_in_sums, keep, give
 ):
     odd = flags[1]
-    feats = pack.shape[1]
     width = context.shape[0]
+    feats = keep.shape[1] - 16
     half = a_own.shape[1]
-    rows = keep.shape[1]
     ones = (lax.broadcasted_iota(jnp.int32, (8, 2 * half), 0) == 4).astype(BF16)
     more = (lax.broadcasted_iota(jnp.int32, (8, 2 * half), 0) == 5).astype(BF16)
     shared = b_in_sums[...] + dot(ones, grad_qkv[:width], 1, 1)
     shared = shared + dot(more, grad_qkv[2 * width :], 1, 1)
     vector_sums = sums[...] + sums_away[...]
+    none = jnp.zeros((16, 2 * feats), BF16)
     for k in range(4):
         span = slice(k * feats, (k + 1) * feats)
-        for at in range(3):
-            part = dot(xs[span], grad_qkv[at * width : (at + 1) * width], 1, 1)
-            pack[at * feats : (at + 1) * feats] = part.astype(BF16)
-        total = dot(context[:, :half], a_own[span], 1, 1)
-        total = total + dot(context[:, half:], a_away[span], 1, 1)
-        pack[3 * width : 4 * width] = total.astype(BF16)
-        tail = jnp.concatenate(
-            (vector_sums[:, span], shared, jnp.zeros((EXTRA - 16, feats), F32)), axis=0
-        )
-        pack[4 * width :] = tail.astype(BF16)
-
-        @pl.when(odd == 0)
-        def _():
-            keep[k] = pack[:rows]
-            give[k] = pack[rows:]
-
-        @pl.when(odd == 1)
-        def _():
-            keep[k] = pack[rows:]
-            give[k] = pack[:rows]
+        blocks = [
+            dot(xs[span], grad_qkv[at * width : (at + 1) * width], 1, 1) for at in range(3)
+        ]
+        last = dot(context[:, :half], a_own[span], 1, 1)
+        blocks += [last + dot(context[:, half:], a_away[span], 1, 1)]
+        tail = jnp.concatenate((vector_sums[:, span], shared), axis=1)
+        tail = jnp.concatenate((tail, jnp.zeros_like(tail)), axis=0).astype(BF16)
+        for part in range(2):
+            pair = jnp.concatenate(blocks[2 * part : 2 * part + 2], axis=1).astype(BF16)
+            rest = none if part else tail
+            for out, at in ((keep, odd), (give, 1 - odd)):
+
+                @pl.when(at == part)
+                def _():
+                    out[k, :feats] = pair
+                    out[k, feats:] = rest
+
+
+def pack_add_kernel(keep, got, *outs):
+    for k, out in enumerate(outs):
+        out[...] = (keep[k].astype(F32) + got[k].astype(F32)).astype(BF16)
+
+
+def unpack_kernel(flags, own, got, qkv, w_out, tail):
+    odd = flags[1]
+    feats, width = w_out.shape[1], w_out.shape[0]
+
+    def write(first, second):
+        qkv[:feats] = first[:feats, :width].astype(F32)
+        qkv[feats : 2 * feats] = first[:feats, width:].astype(F32)
+        qkv[2 * feats :] = second[:feats, :width].astype(F32)
+        w_out[...] = second[:feats, width:].astype(F32)
+        tail[:16] = first[feats:, :feats].astype(F32)
+        tail[16:] = first[feats:, feats:].astype(F32)
+
+    @pl.when(odd == 0)
+    def _():
+        write(own, got)
+
+    @pl.when(odd == 1)
+    def _():
+        write(got, own)
+
+
+def wide_unpack_kernel(flags, b_own, b_got, i_own, i_got, back, into):
+    odd = flags[1]
+    part = b_own.shape[0]
+    for out, own, got in ((back, b_own, b_got), (into, i_own, i_got)):
+        for ref, at in ((own, odd), (got, 1 - odd)):
+            rows = pl.ds(pl.multiple_of(at * part, part), part)
+            out[rows, :] = ref[...].astype(F32)
 
 
 def join_kernel(flags, kept, got, own, away):
@@ -500,7 +542,7 @@
     model = n_rows * feats
     units = w_in.shape[1]
     heads = width // HEAD_DIM
-    length = lax.dynamic_index_in_dim(seq_lengths, row, 0, False)
+    length = lax.dynamic_index_in_dim(seq_lengths, plane_of(row), 0, False)
     flags = jnp.stack((col % 2, odd_bit, col, length, col // 2, row)).astype(jnp.int32)
     halves = shape((model, half), BF16)
     wide_halves = shape((model, half), F32)
@@ -508,10 +550,9 @@
     def sum_cores(mine, other):
         return (mine + swap_bit(other, "col", 1).astype(F32)).astype(BF16)
 
-    def add_rows(blocks, *gates):
-        terms = [blocks[0]]
-        terms += [after(from_row(blocks[k], n_rows - k), *gates) for k in range(1, n_rows)]
-        terms = [term.astype(F32) for term in terms]
+    def add_rows(blocks):
+        parts = [from_row(blocks[k], n_rows - k) for k in range(1, n_rows)]
+        terms = [term.astype(F32) for term in (blocks[0], *parts)]
         while len(terms) > 1:
             pairs = len(terms) // 2
             terms = [terms[i] + terms[i + pairs] for i in range(pairs)]
@@ -525,53 +566,50 @@
             bit *= 2
         return total
 
-    def add_shares(keep, got):
-        total = add_rows(
-            [(keep[k].astype(F32) + got[k].astype(F32)).astype(BF16) for k in range(n_rows)]
-        )
-        total = add_replicas(total, 2)
-        return ordered(odd, total, swap_bit(total, "dp", 1), 0)
-
     x0 = to_slot(layer_in)
     qkv_part = w_qkv.transpose(1, 0, 2).reshape(3 * feats, width)
-    n_half = 2 * feats
-    (pack_half,) = call(
-        half_kernel,
-        "half",
-        [shape((n_half, width), BF16)],
-        [odd_bit.reshape(1), qkv_part, w_out],
-        specs={k: pl.BlockSpec(memory_space=pl.ANY) for k in (1, 2)},
-        scratch=[pltpu.SemaphoreType.DMA((2,))],
-    )
-    fetched = [from_row(pack_half, k) for k in range(1, n_rows)]
-    vectors = jnp.concatenate(
-        (b_out, ln1_gain, ln1_bias, b_back, ln2_gain, ln2_bias, q_bias, v_bias)
-    )
-    vectors = jnp.pad(vectors.reshape(8, feats), ((0, 0), (0, units - feats)))
-    vectors = jnp.concatenate((vectors, jnp.pad(b_in[None], ((0, 7), (0, 0)))))
-    wide = jnp.concatenate((jnp.where(odd, w_back, w_in), vectors))
-    x0 = after(x0, flags, wide, *fetched)
+    pack_half, wide, vectors = call(
+        send_kernel,
+        "send",
+        [
+            shape((feats, 2 * width), BF16),
+            shape((feats + 16, units), BF16),
+            shape((16, units), BF16),
+        ],
+        [odd_bit.reshape(1), qkv_part, w_out, w_in, w_back, b_in]
+        + [b_out, ln1_gain, ln1_bias, b_back, ln2_gain, ln2_bias, q_bias, v_bias],
+        specs={k: pl.BlockSpec(memory_space=pl.ANY) for k in range(1, 14)},
+        out_specs=[
+            pl.BlockSpec(memory_space=pltpu.VMEM)
+        ]
+        * 3,
+        scratch=[
+            pltpu.VMEM((2, feats, width), BF16),
+            pltpu.VMEM((units,), BF16),
+            pltpu.SemaphoreType.DMA((12,)),
+        ]
+        + [pltpu.VMEM((feats,), BF16)] * 8,
+        vmem_mib=56,
+    )
+    fetched = lax.all_gather(after(pack_half, wide), "row")
+    swapped = swap_bit(fetched, "dp", 1)
+    wide = after(wide, fetched)
+    wide_fetched = [from_row(wide, k) for k in range(1, n_rows)]
+    x0 = after(x0, flags, fetched)
     x2 = swap_bit(x0, "col", 2)
     x1 = swap_bit(x0, "col", 1)
-    swapped = swap_bit(jnp.concatenate(fetched), "dp", 1)
-    wide = after(wide, *fetched)
-    wide_fetched = [from_row(wide, 1)]
-    wide_fetched += [from_row(after(wide, wide_fetched[0]), k) for k in range(2, n_rows)]
-    wide_swapped = [
-        swap_bit(jnp.concatenate(wide_fetched[:2]), "dp", 1),
-        swap_bit(wide_fetched[2], "dp", 1),
-    ]
-    x3 = swap_bit(after(x2, swapped, wide_fetched[0]), "col", 1)
+    wide_swapped = [swap_bit(after(part, x2), "dp", 1) for part in wide_fetched]
+    g_own = to_slot(after(out_grad.astype(BF16), fetched))
+    ready = (wide_swapped[0], wide_fetched[1], wide_swapped[2])
+    x3 = swap_bit(after(x2, swapped, g_own, *ready), "col", 1)
 
     in_all, back_all, vecs, in_bias = call(
         assemble_kernel,
         "assemble",
         [shape((model, units), BF16)] * 2 + [shape((model, 16), F32), shape((units, 16), F32)],
         [flags, w_in, w_back, vectors] + wide_fetched + wide_swapped,
-        specs={k: pl.BlockSpec(memory_space=pl.ANY) for k in (1, 2, 4, 5, 6, 7, 8)},
+        specs={k: pl.BlockSpec(memory_space=pl.ANY) for k in (1, 2, 4, 5, 6, 7, 8, 9)},
         scratch=[pltpu.VMEM((3, 16, units), BF16), pltpu.SemaphoreType.DMA((11,))],
-        vmem_mib=56,
-        weight=2,
     )
 
     xs, packs, qkv, prob, context, mine, other = call(
@@ -579,18 +617,18 @@
         "attend",
         [
             shape((model, slot), BF16),
-            shape((n_rows, 4 * width, feats), BF16),
+            shape((n_rows, 2, feats, 2 * width), BF16),
             shape((3 * width, slot), BF16),
             shape((heads, slot, slot), BF16),
             shape((width, slot), BF16),
             wide_halves,
             halves,
         ],
-        [flags, x0, x1, x2, x3, qkv_part, w_out] + fetched + [swapped, vectors],
-        specs={k: pl.BlockSpec(memory_space=pl.ANY) for k in range(1, 11)},
+        [flags, x0, x1, x2, x3, fetched, swapped, vectors],
+        specs={k: pl.BlockSpec(memory_space=pl.ANY) for k in range(1, 7)},
         scratch=[pltpu.VMEM((model, slot), BF16), pltpu.SemaphoreType.DMA((12,))],
         vmem_mib=56,
-        weight=12,
+        weight=0,
     )
 
     own = sum_cores(mine, other)
@@ -602,9 +640,8 @@
         [xs, own, away, vecs],
         specs={0: pl.BlockSpec((model, half), lambda _: (0, 0))},
         windowed=True,
-        weight=2,
-    )
-    g_own = to_slot(after(out_grad.astype(BF16), wide_fetched[2]))
+        weight=0,
+    )
     g_high = swap_bit(after(g_own, scaled_one), "col", 2)
 
     n_away = swap_bit(n_own, "col", 1)
@@ -613,7 +650,7 @@
         "feed_forward",
         [shape((units, slot), BF16), shape((units, slot), BF16), wide_halves, halves],
         [n_own, n_away, in_all, back_all, in_bias],
-        weight=6,
+        weight=0,
     )
     g_both = jnp.concatenate((after(g_own, hidden), g_high))
     g_low = swap_bit(jnp.where(low_bit, g_both[:, :half], g_both[:, half:]), "col", 1)
@@ -631,7 +668,7 @@
         ],
         [flags, scaled_one, own, away, vecs, g_own, g_high, g_low],
         scratch=[pltpu.VMEM((model, half), BF16), pltpu.VMEM((model, half), BF16)],
-        weight=4,
+        weight=0,
     )
     r_away = swap_bit(r_own, "col", 1)
     mine, other, grad_pre, b_in_sums = call(
@@ -639,23 +676,25 @@
         "feed_backward",
         [wide_halves, halves, shape((units, slot), BF16), shape((8, feats), F32)],
         [r_own, r_away, slope, in_all, back_all],
-        weight=3,
+        weight=0,
     )
     own = sum_cores(mine, other)
-    *back_grads, into_keep, into_give = call(
+    b_keep, b_give, i_keep, i_give = call(
         wide_grad_kernel,
         "wide_grads",
-        [shape((feats, units), BF16)] * n_rows + [shape((n_rows, feats // 2, units), BF16)] * 2,
+        [shape((n_rows, feats // 2, units), BF16)] * 4,
         [flags, after(r_own, own), r_away, hidden, n_own, n_away, grad_pre],
-        weight=8,
-    )
+        weight=0,
+    )
+    b_got = swap_bit(b_give, "dp", 1)
+    i_got = swap_bit(i_give, "dp", 1)
     away = swap_bit(own, "col", 2)
     grad_first, a_own, sums = call(
         norm_back_kernel,
         "norm_back",
         [wide_halves, halves, shape((8, model), F32)],
-        [own, after(away, into_give), grad_second, scaled_one, inverse_one, vecs, sums],
-        weight=2,
+        [own, after(away, b_give), grad_second, scaled_one, inverse_one, vecs, sums],
+        weight=0,
     )
     a_away = swap_bit(a_own, "col", 1)
     sums_away = swap_bit(sums, "col", 1)
@@ -669,16 +708,15 @@
         ],
         [flags, a_own, a_away, packs, qkv, prob, grad_first],
         scratch=[pltpu.VMEM((width, slot), BF16)],
-        weight=8,
+        weight=0,
     )
 
     pack_keep, pack_give = call(
         pack_grad_kernel,
         "pack_grads",
-        [shape((n_rows, 2 * width + EXTRA // 2, feats), BF16)] * 2,
+        [shape((n_rows, feats + 16, 2 * width), BF16)] * 2,
         [flags, xs, grad_qkv, a_own, a_away, context, sums, sums_away, b_in_sums],
-        scratch=[pltpu.VMEM((4 * width + EXTRA, feats), BF16)],
-        weight=5,
+        weight=0,
     )
 
     in_own, in_away = call(
@@ -695,30 +733,56 @@
     )
     in_grad = from_slot(in_done).astype(F32)
 
-    into_got = swap_bit(into_give, "dp", 1)
-
     out_give = after(out_give, in_away)
     layer_out = from_slot(ordered(low_bit, out_own, swap_bit(out_give, "col", 1), 1))
 
-    w_back_grad = add_replicas(add_rows(back_grads, in_away), 1).astype(F32)
-    w_in_grad = add_shares(into_keep, after(into_got, in_away)).astype(F32)
-    pack_got = swap_bit(pack_give, "dp", 1)
-    total = add_shares(pack_keep, after(pack_got, in_done)).astype(F32)
-    w_qkv_grad = total[: 3 * feats].reshape(3, feats, width).transpose(1, 0, 2)
-    w_out_grad = total[3 * width : 4 * width]
-    tail = total[4 * width :]
+    totals = []
+    for name, keep, got in (
+        ("back_add", b_keep, after(b_got, grad_qkv)),
+        ("into_add", i_keep, after(i_got, pack_give)),
+    ):
+        parts = call(
+            pack_add_kernel, name, [shape((feats // 2, units), BF16)] * n_rows, [keep, got]
+        )
+        totals += [add_replicas(add_rows(parts), 2)]
+    b_back, i_back = (swap_bit(total, "dp", 1) for total in totals)
+    pack_got = after(swap_bit(pack_give, "dp", 1), totals[1], b_back)
+    w_back_grad, w_in_grad = call(
+        wide_unpack_kernel,
+        "wide_unpack",
+        [shape((feats, units), F32)] * 2,
+        [flags, totals[0], b_back, totals[1], i_back],
+    )
+    packs = call(
+        pack_add_kernel,
+        "pack_add",
+        [shape(pack_keep.shape[1:], BF16)] * n_rows,
+        [pack_keep, pack_got],
+    )
+    total = add_replicas(add_rows(packs), 2)
+    w_qkv_grad, w_out_grad, tail = call(
+        unpack_kernel,
+        "unpack",
+        [
+            shape((3 * feats, width), F32),
+            shape((width, feats), F32),
+            shape((EXTRA, feats), F32),
+        ],
+        [flags, total, swap_bit(after(total, i_back), "dp", 1)],
+    )
+    w_qkv_grad = w_qkv_grad.reshape(3, feats, width).transpose(1, 0, 2)
     return (
         layer_out,
         in_grad,
         w_qkv_grad,
-        tail[12],
-        tail[13],
+        tail[20],
+        tail[21],
         w_out_grad,
         tail[4],
         tail[0],
         tail[1],
         w_in_grad,
-        tail[8:12].reshape(-1),
+        tail[16:20].reshape(-1),
         w_back_grad,
         tail[5],
         tail[2],

time: 233 us -> 206 us (0.88); the launches traced: 233 us -> 202 us
  waiting for transfers between devices: 118 us -> 75.7 us
  blocking collectives: 0 us -> 16.9 us
  local copies, waits for them, and re-layouts: 18 us -> 9 us
  other arithmetic: 10.5 us -> 2.55 us
  starting transfers between devices: 51.4 us -> 57.9 us
  Pallas kernels: 33.2 us -> 39 us
    ppermute x15 -> x12, waiting for transfers between devices: 56.6 us -> 24 us  [from_row(): lax.ppermute(value, 'row', [((a + away) % size, a) for a in range(size)])]
    all_gather x0 -> x1, blocking collectives: none -> 16.9 us  [shards(): fetched = lax.all_gather(after(pack_half, wide), 'row')]
    ppermute x26 -> x28, waiting for transfers between devices: 53.5 us -> 39.2 us  [swap_bit(): return lax.ppermute(value, axis, [(at, at ^ bit) for at in range(size)])]
    pallas_call x13 -> x18, Pallas kernels: 33.2 us -> 39 us  [call(): pl.pallas_call(kernel, name=name, out_shape=outs, grid=(1,) if windowed e...]
    ppermute x26 -> x28, starting transfers between devices: 16.8 us -> 22.2 us  [swap_bit(): return lax.ppermute(value, axis, [(at, at ^ bit) for at in range(size)])]
    unnamed x100 -> x52, local copies, waits for them, and re-layouts: 9.74 us -> 4.97 us
    ppermute x2, waiting for transfers between devices: 8.12 us -> 12.3 us  [to_slot(): return lax.ppermute(value, ('row', 'col'), grid_pairs())]
    convert_element_type x6 -> x1, other arithmetic: 3.81 us -> 0.02 us  [shards(): g_own = to_slot(after(out_grad.astype(BF16), fetched))]
  transfers between devices with their start and end apart: 45 -> 44, of which waited for: 20 -> 22; matrix products, arithmetic and copies ran while one was open for 7% -> 2% of each run, Pallas kernels for 12% -> 11%
where the time goes in v5:
time: 206 us; the launch traced here: 202 us
  waiting for transfers between devices  75.7 us (37%)
  starting transfers between devices  57.9 us (28%)
  Pallas kernels  39 us (19%)
  blocking collectives  16.9 us (8%)
  local copies, waits for them, and re-layouts  9 us (4%)
  other arithmetic  2.55 us (1%)
    ppermute x28, waiting for transfers between devices, swap_bit(): return lax.ppermute(value, axis, [(at, at ^ bit) for at in range(size)])  39.2 us
    pallas_call x18, Pallas kernels, call(): pl.pallas_call(kernel, name=name, out_shape=outs, grid=(1,) if windowed e...  39 us
    ppermute x12, waiting for transfers between devices, from_row(): lax.ppermute(value, 'row', [((a + away) % size, a) for a in range(size)])  24 us
    ppermute x12, starting transfers between devices, from_row(): lax.ppermute(value, 'row', [((a + away) % size, a) for a in range(size)])  24 us
    ppermute x28, starting transfers between devices, swap_bit(): return lax.ppermute(value, axis, [(at, at ^ bit) for at in range(size)])  22.2 us
    all_gather x1, blocking collectives, shards(): fetched = lax.all_gather(after(pack_half, wide), 'row')  16.9 us
    ppermute x2, waiting for transfers between devices, to_slot(): return lax.ppermute(value, ('row', 'col'), grid_pairs())  12.3 us
    ppermute x2, starting transfers between devices, from_slot(): lax.ppermute(value, ('row', 'col'), [(b, a) for a, b in grid_pairs()])  7.72 us
  transfers between devices with their start and end apart: 44, of which 22 were waited for; matrix products, arithmetic and copies ran while one was open for 2% of the time, Pallas kernels for 11%

profile of v5, /device:TPU:20, one launch (start us, length us, event | category | flops | bytes accessed | tf_op | source)
XLA Modules:
  0.0 202.1 jit_solution(18196145015186784946)
XLA Ops:
  4.7 16.9 %all-gather = bf16[768,384]{1,0:T(8,128)(2,1)S(1)} all-gather(bf16[192,384]{1,0:T(8,128)(2,1)} %get-tuple-element.97), channel_id=2, replica_groups=mesh['dp'=2,'row'=4,'col'=4] {'row'}, dimensions={0}, use_global_device_ids=true | all-gather | bytes 737280 | tf_op jit(solution)/shard_map/all_gather | solution.py:594
  21.6 2.5 %collective-permute-start.8 = (bf16[208,768]{1,0:T(8,128)(2,1)}, bf16[208,768]{1,0:T(8,128)(2,1)S(1)}, u32[]{:S(2)}, u32[]{:S(2)}) collective-permute-start(bf16[208,768]{1,0:T(8,128)(2,1)} %get-tuple-element.100), channel_id=1, source_target_pairs={{12,0},{0,4},{4,8},{8,12},{13,1},{1,5},{5,9},{9,13},{14,2},{2,6},{... | collective-permute-start | bytes 958472 | tf_op jit(solution)/shard_map/ppermute | solution.py:75
  27.8 4.0 %collective-permute-start.7 = (bf16[208,768]{1,0:T(8,128)(2,1)}, bf16[208,768]{1,0:T(8,128)(2,1)S(1)}, u32[]{:S(2)}, u32[]{:S(2)}) collective-permute-start(bf16[208,768]{1,0:T(8,128)(2,1)} %get-tuple-element.100), channel_id=1, source_target_pairs={{8,0},{12,4},{0,8},{4,12},{9,1},{13,5},{1,9},{5,13},{10,2},{14,6},... | collective-permute-start | bytes 958472 | tf_op jit(solution)/shard_map/ppermute | solution.py:75
  31.7 7.3 %collective-permute-done.8.f3 = bf16[208,768]{1,0:T(8,128)(2,1)S(1)} collective-permute-done((bf16[208,768]{1,0:T(8,128)(2,1)}, bf16[208,768]{1,0:T(8,128)(2,1)S(1)}, u32[]{:S(2)}, u32[]{:S(2)}) %collective-permute-start.8) | collective-permute-done | bytes 319520 | tf_op jit(solution)/shard_map/ppermute | solution.py:75
  43.9 12.3 %collective-permute-done.4.g_own = bf16[192,512]{1,0:T(8,128)(2,1)} collective-permute-done((bf16[192,512]{1,0:T(8,128)(2,1)S(1)}, bf16[192,512]{1,0:T(8,128)(2,1)}, u32[]{:S(2)}, u32[]{:S(2)}) %collective-permute-start.4) | collective-permute-done | bytes 196640 | tf_op jit(solution)/shard_map/ppermute | solution.py:66
  58.6 7.9 %attend.1 = (bf16[768,512]{1,0:T(8,128)(2,1)}, bf16[4,2,192,384]{3,2,1,0:T(8,128)(2,1)}, bf16[576,512]{1,0:T(8,128)(2,1)}, bf16[3,512,512]{2,1,0:T(8,128)(2,1)},...) custom-call(s32[6]{0:T(128)} %stack.24.flags, bf16[192,512]{1,0:T(8,128)(2,1)} %copy-done.20, ...), custom_call_target="tpu_custom_call" | custom-call | tf_op jit(solution)/shard_map/attend/pallas_call | solution.py:28
  71.4 8.3 %collective-permute-done.13.s2 = bf16[208,768]{1,0:T(8,128)(2,1)S(1)} collective-permute-done((bf16[208,768]{1,0:T(8,128)(2,1)S(1)}, bf16[208,768]{1,0:T(8,128)(2,1)S(1)}, u32[]{:S(2)}, u32[]{:S(2)}) %collective-permute-start.13) | collective-permute-done | bytes 319520 | tf_op jit(solution)/shard_map/ppermute | solution.py:49
  87.4 3.0 %feed_forward.1 = (bf16[768,512]{1,0:T(8,128)(2,1)S(1)}, bf16[768,512]{1,0:T(8,128)(2,1)S(1)}, f32[768,256]{1,0:T(8,128)S(1)}, bf16[768,256]{1,0:T(8,128)(2,1)S(1)}) custom-call(bf16[768,256]{1,0:T(8,128)(2,1)} %get-tuple-element.111.n_own, bf16[768,256]{1,0:T(8,128)(2,1)} %collective-permute-done.14.n_away, bf16[768,768]{1,0:T(8,128)(2,1)S(1)} %get-tuple-element.112.w_in, ...), custom_call_target="tpu_custom_call" | custom-call | tf_op jit(solution)/shard_map/feed_forward/pallas_call | solution.py:28
  96.3 9.5 %collective-permute-done.18.away = bf16[768,256]{1,0:T(8,128)(2,1)S(1)} collective-permute-done((bf16[768,256]{1,0:T(8,128)(2,1)S(1)}, bf16[768,256]{1,0:T(8,128)(2,1)S(1)}, u32[]{:S(2)}, u32[]{:S(2)}) %collective-permute-start.18) | collective-permute-done | bytes 393248 | tf_op jit(solution)/shard_map/ppermute | solution.py:49
  105.8 3.1 %turn.1 = (bf16[192,256]{1,0:T(8,128)(2,1)S(1)}, bf16[192,256]{1,0:T(8,128)(2,1)S(1)}, f32[768,256]{1,0:T(8,128)S(1)}, bf16[768,256]{1,0:T(8,128)(2,1)S(1)}, f32[8,768]{1,0:T(8,128)S(1)}) custom-call(s32[6]{0:T(128)S(1)} %copy-done.16, f32[768,256]{1,0:T(8,128)S(1)} %copy-done.2, bf16[768,256]{1,0:T(8,128)(2,1)S(1)} %add_convert_fusion.1.own, ...), custom_call_target="tpu_custom_call" | custom-call | tf_op jit(solution)/shard_map/turn/pallas_call | solution.py:28
  115.8 5.1 %wide_grads.1 = (bf16[4,96,768]{2,1,0:T(8,128)(2,1)S(1)}, bf16[4,96,768]{2,1,0:T(8,128)(2,1)S(1)}, bf16[4,96,768]{2,1,0:T(8,128)(2,1)S(1)}, bf16[4,96,768]{2,1,0:T(8,128)(2,1)S(1)}) custom-call(s32[6]{0:T(128)S(1)} %copy-done.16, bf16[768,256]{1,0:T(8,128)(2,1)S(1)} %get-tuple-element.126.r_own, bf16[768,256]{1,0:T(8,128)(2,1)S(1)} %collective-permute-done.19.r_away, ...), custom_call_target="tpu_custom_call" | custom-call | tf_op jit(solution)/shard_map/wide_grads/pallas_call | solution.py:28
  123.0 2.3 %collective-permute-done.21.away = bf16[768,256]{1,0:T(8,128)(2,1)S(1)} collective-permute-done((bf16[768,256]{1,0:T(8,128)(2,1)S(1)}, bf16[768,256]{1,0:T(8,128)(2,1)S(1)}, u32[]{:S(2)}, u32[]{:S(2)}) %collective-permute-start.21) | collective-permute-done | bytes 393248 | tf_op jit(solution)/shard_map/ppermute | solution.py:49
  128.2 4.8 %attend_back.1 = (bf16[576,512]{1,0:T(8,128)(2,1)S(1)}, f32[384,512]{1,0:T(8,128)S(1)}, bf16[384,512]{1,0:T(8,128)(2,1)S(1)}) custom-call(s32[6]{0:T(128)S(1)} %copy-done.16, bf16[768,256]{1,0:T(8,128)(2,1)S(1)} %get-tuple-element.133.a_own, bf16[768,256]{1,0:T(8,128)(2,1)S(1)} %collective-permute-done.22.a_away, bf16[4,2,192,384]{3,2,1,0:T(8,128)(2,1)S(1)} %copy-done.4, ...), custom_call_target="tpu_custom_call" | custom-call | tf_op jit(solution)/shard_map/attend_back/pallas_call | solution.py:28
  133.0 2.9 %pack_grads.1 = (bf16[4,208,384]{2,1,0:T(8,128)(2,1)S(1)}, bf16[4,208,384]{2,1,0:T(8,128)(2,1)S(1)}) custom-call(s32[6]{0:T(128)S(1)} %copy-done.16, bf16[768,512]{1,0:T(8,128)(2,1)S(1)} %copy-done, bf16[576,512]{1,0:T(8,128)(2,1)S(1)} %get-tuple-element.139.grad_qkv, bf16[768,256]{1,0:T(8,128)(2,1)S(1)} %get-tuple-element.133.a_own, ...), custom_call_target="tpu_custom_call" | custom-call | tf_op jit(solution)/shard_map/pack_grads/pallas_call | solution.py:28
  137.6 3.3 %collective-permute-start.35 = (bf16[96,768]{1,0:T(8,128)(2,1)S(1)}, bf16[96,768]{1,0:T(8,128)(2,1)S(1)}, u32[]{:S(2)}, u32[]{:S(2)}) collective-permute-start(bf16[96,768]{1,0:T(8,128)(2,1)S(1)} %get-tuple-element.161), channel_id=1, source_target_pairs={{8,0},{12,4},{0,8},{4,12},{9,1},{13,5},{1,9},{5,13},{10,2},{14,6},... | collective-permute-start | bytes 442376 | tf_op jit(solution)/shard_map/ppermute | solution.py:75
  142.3 7.5 %collective-permute-done.30.got = bf16[4,96,768]{2,1,0:T(8,128)(2,1)S(1)} collective-permute-done((bf16[4,96,768]{2,1,0:T(8,128)(2,1)S(1)}, bf16[4,96,768]{2,1,0:T(8,128)(2,1)S(1)}, u32[]{:S(2)}, u32[]{:S(2)}) %collective-permute-start.30) | collective-permute-done | bytes 589856 | tf_op jit(solution)/shard_map/ppermute | solution.py:49
  151.8 4.3 %collective-permute-start.31 = (bf16[96,768]{1,0:T(8,128)(2,1)S(1)}, bf16[96,768]{1,0:T(8,128)(2,1)S(1)}, u32[]{:S(2)}, u32[]{:S(2)}) collective-permute-start(bf16[96,768]{1,0:T(8,128)(2,1)S(1)} %get-tuple-element.155), channel_id=1, source_target_pairs={{8,0},{12,4},{0,8},{4,12},{9,1},{13,5},{1,9},{5,13},{10,2},{14,6},... | collective-permute-start | bytes 442376 | tf_op jit(solution)/shard_map/ppermute | solution.py:75
  156.1 4.8 %collective-permute-done.37 = bf16[96,768]{1,0:T(8,128)(2,1)S(1)} collective-permute-done((bf16[96,768]{1,0:T(8,128)(2,1)S(1)}, bf16[96,768]{1,0:T(8,128)(2,1)S(1)}, u32[]{:S(2)}, u32[]{:S(2)}) %collective-permute-start.37) | collective-permute-done | bytes 147488 | tf_op jit(solution)/shard_map/ppermute | solution.py:75
  160.9 2.5 %collective-permute-start.33 = (bf16[96,768]{1,0:T(8,128)(2,1)S(1)}, bf16[96,768]{1,0:T(8,128)(2,1)S(1)}, u32[]{:S(2)}, u32[]{:S(2)}) collective-permute-start(bf16[96,768]{1,0:T(8,128)(2,1)S(1)} %get-tuple-element.157), channel_id=1, source_target_pairs={{4,0},{8,4},{12,8},{0,12},{5,1},{9,5},{13,9},{1,13},{6,2},{10,6},{... | collective-permute-start | bytes 442376 | tf_op jit(solution)/shard_map/ppermute | solution.py:75
  165.7 2.1 %collective-permute-done.32 = bf16[96,768]{1,0:T(8,128)(2,1)S(1)} collective-permute-done((bf16[96,768]{1,0:T(8,128)(2,1)S(1)}, bf16[96,768]{1,0:T(8,128)(2,1)S(1)}, u32[]{:S(2)}, u32[]{:S(2)}) %collective-permute-start.32) | collective-permute-done | bytes 147488 | tf_op jit(solution)/shard_map/ppermute | solution.py:75
  170.2 2.2 %collective-permute-start.39 = (bf16[208,384]{1,0:T(8,128)(2,1)S(1)}, bf16[208,384]{1,0:T(8,128)(2,1)S(1)}, u32[]{:S(2)}, u32[]{:S(2)}) collective-permute-start(bf16[208,384]{1,0:T(8,128)(2,1)S(1)} %get-tuple-element.166), channel_id=1, source_target_pairs={{8,0},{12,4},{0,8},{4,12},{9,1},{13,5},{1,9},{5,13},{10,2},{14,6},... | collective-permute-start | bytes 479240 | tf_op jit(solution)/shard_map/ppermute | solution.py:75
  177.7 3.6 %collective-permute-done.39 = bf16[208,384]{1,0:T(8,128)(2,1)S(1)} collective-permute-done((bf16[208,384]{1,0:T(8,128)(2,1)S(1)}, bf16[208,384]{1,0:T(8,128)(2,1)S(1)}, u32[]{:S(2)}, u32[]{:S(2)}) %collective-permute-start.39) | collective-permute-done | bytes 159776 | tf_op jit(solution)/shard_map/ppermute | solution.py:75
  181.3 5.6 %collective-permute-start.28 = (bf16[192,512]{1,0:T(8,128)(2,1)S(1)}, bf16[192,512]{1,0:T(8,128)(2,1)S(1)}, u32[]{:S(2)}, u32[]{:S(2)}) collective-permute-start(bf16[192,512]{1,0:T(8,128)(2,1)S(1)} %finish.1), channel_id=1, source_target_pairs={{0,0},{10,1},{7,2},{13,3},{1,4},{11,5},{4,6},{14,7},{2,8},{8,9},{5... | collective-permute-start | bytes 589832 | tf_op jit(solution)/shard_map/ppermute | solution.py:70
  186.9 6.2 %collective-permute-done.40 = bf16[208,384]{1,0:T(8,128)(2,1)S(1)} collective-permute-done((bf16[208,384]{1,0:T(8,128)(2,1)S(1)}, bf16[208,384]{1,0:T(8,128)(2,1)S(1)}, u32[]{:S(2)}, u32[]{:S(2)}) %collective-permute-start.40) | collective-permute-done | bytes 159776 | tf_op jit(solution)/shard_map/ppermute | solution.py:75
  (152 shorter events, 69.2 us)
Async XLA Ops:
  0.7 26.8 %collective-permute-start = (bf16[192,512]{1,0:T(8,128)(2,1)}, bf16[192,512]{1,0:T(8,128)(2,1)S(1)}, u32[]{:S(2)}, u32[]{:S(2)}) collective-permute-start(bf16[192,512]{1,0:T(8,128)(2,1)} %param.16), channel_id=1, source_target_pairs={{0,0},{1,10},{2,7},{3,13},{4,1},{5,11},{6,4},{7,14},{8,2},{9,8},{1... | collective-permute-start | bytes 589832 | tf_op jit(solution)/shard_map/ppermute | solution.py:66
  21.6 17.4 %collective-permute-start.8 = (bf16[208,768]{1,0:T(8,128)(2,1)}, bf16[208,768]{1,0:T(8,128)(2,1)S(1)}, u32[]{:S(2)}, u32[]{:S(2)}) collective-permute-start(bf16[208,768]{1,0:T(8,128)(2,1)} %get-tuple-element.100), channel_id=1, source_target_pairs={{12,0},{0,4},{4,8},{8,12},{13,1},{1,5},{5,9},{9,13},{14,2},{2,6},{... | collective-permute-start | bytes 958472 | tf_op jit(solution)/shard_map/ppermute | solution.py:75
  24.1 16.4 %collective-permute-start.5 = (bf16[208,768]{1,0:T(8,128)(2,1)}, bf16[208,768]{1,0:T(8,128)(2,1)S(1)}, u32[]{:S(2)}, u32[]{:S(2)}) collective-permute-start(bf16[208,768]{1,0:T(8,128)(2,1)} %get-tuple-element.100), channel_id=1, source_target_pairs={{4,0},{8,4},{12,8},{0,12},{5,1},{9,5},{13,9},{1,13},{6,2},{10,6},{... | collective-permute-start | bytes 958472 | tf_op jit(solution)/shard_map/ppermute | solution.py:75
  24.1 32.1 %collective-permute-start.3 = (bf16[4,192,384]{2,1,0:T(8,128)(2,1)S(1)}, bf16[4,192,384]{2,1,0:T(8,128)(2,1)S(1)}, u32[]{:S(2)}, u32[]{:S(2)}) collective-permute-start(bf16[4,192,384]{2,1,0:T(8,128)(2,1)S(1)} %bitcast.20), channel_id=1, source_target_pairs={{0,16},{16,0},{1,17},{17,1},{2,18},{18,2},{3,19},{19,3},{4,20},{20... | collective-permute-start | bytes 1769480 | tf_op jit(solution)/shard_map/ppermute | solution.py:49
  27.4 11.6 %collective-permute-start.2 = (bf16[192,512]{1,0:T(8,128)(2,1)S(1)}, bf16[192,512]{1,0:T(8,128)(2,1)S(1)}, u32[]{:S(2)}, u32[]{:S(2)}) collective-permute-start(bf16[192,512]{1,0:T(8,128)(2,1)S(1)} %collective-permute-done.x0), channel_id=1, source_target_pairs={{0,2},{1,3},{2,0},{3,1},{4,6},{5,7},{6,4},{7,5},{8,10},{9,11},{10,... | collective-permute-start | bytes 589832 | tf_op jit(solution)/shard_map/ppermute | solution.py:49
  27.8 28.5 %collective-permute-start.7 = (bf16[208,768]{1,0:T(8,128)(2,1)}, bf16[208,768]{1,0:T(8,128)(2,1)S(1)}, u32[]{:S(2)}, u32[]{:S(2)}) collective-permute-start(bf16[208,768]{1,0:T(8,128)(2,1)} %get-tuple-element.100), channel_id=1, source_target_pairs={{8,0},{12,4},{0,8},{4,12},{9,1},{13,5},{1,9},{5,13},{10,2},{14,6},... | collective-permute-start | bytes 958472 | tf_op jit(solution)/shard_map/ppermute | solution.py:75
  39.0 17.2 %collective-permute-start.9 = (bf16[208,768]{1,0:T(8,128)(2,1)S(1)}, bf16[208,768]{1,0:T(8,128)(2,1)S(1)}, u32[]{:S(2)}, u32[]{:S(2)}) collective-permute-start(bf16[208,768]{1,0:T(8,128)(2,1)S(1)} %collective-permute-done.8.f3), channel_id=1, source_target_pairs={{0,16},{16,0},{1,17},{17,1},{2,18},{18,2},{3,19},{19,3},{4,20},{20... | collective-permute-start | bytes 958472 | tf_op jit(solution)/shard_map/ppermute | solution.py:49
  40.5 15.8 %collective-permute-start.6 = (bf16[208,768]{1,0:T(8,128)(2,1)S(1)}, bf16[208,768]{1,0:T(8,128)(2,1)S(1)}, u32[]{:S(2)}, u32[]{:S(2)}) collective-permute-start(bf16[208,768]{1,0:T(8,128)(2,1)S(1)} %collective-permute-done.5.f1), channel_id=1, source_target_pairs={{0,16},{16,0},{1,17},{17,1},{2,18},{18,2},{3,19},{19,3},{4,20},{20... | collective-permute-start | bytes 958472 | tf_op jit(solution)/shard_map/ppermute | solution.py:49
  41.9 14.3 %collective-permute-start.4 = (bf16[192,512]{1,0:T(8,128)(2,1)S(1)}, bf16[192,512]{1,0:T(8,128)(2,1)}, u32[]{:S(2)}, u32[]{:S(2)}) collective-permute-start(bf16[192,512]{1,0:T(8,128)(2,1)S(1)} %convert_element_type.69), channel_id=1, source_target_pairs={{0,0},{1,10},{2,7},{3,13},{4,1},{5,11},{6,4},{7,14},{8,2},{9,8},{1... | collective-permute-start | bytes 589832 | tf_op jit(solution)/shard_map/ppermute | solution.py:66
  69.8 12.3 %collective-permute-start.12 = (bf16[768,256]{1,0:T(8,128)(2,1)S(1)}, bf16[768,256]{1,0:T(8,128)(2,1)S(1)}, u32[]{:S(2)}, u32[]{:S(2)}) collective-permute-start(bf16[768,256]{1,0:T(8,128)(2,1)S(1)} %add_convert_fusion.2.own), channel_id=1, source_target_pairs={{0,2},{1,3},{2,0},{3,1},{4,6},{5,7},{6,4},{7,5},{8,10},{9,11},{10,... | collective-permute-start | bytes 1179656 | tf_op jit(solution)/shard_map/ppermute | solution.py:49
  94.5 11.2 %collective-permute-start.18 = (bf16[768,256]{1,0:T(8,128)(2,1)S(1)}, bf16[768,256]{1,0:T(8,128)(2,1)S(1)}, u32[]{:S(2)}, u32[]{:S(2)}) collective-permute-start(bf16[768,256]{1,0:T(8,128)(2,1)S(1)} %add_convert_fusion.1.own), channel_id=1, source_target_pairs={{0,2},{1,3},{2,0},{3,1},{4,6},{5,7},{6,4},{7,5},{8,10},{9,11},{10,... | collective-permute-start | bytes 1179656 | tf_op jit(solution)/shard_map/ppermute | solution.py:49
  120.9 16.5 %collective-permute-start.34 = (bf16[4,96,768]{2,1,0:T(8,128)(2,1)S(1)}, bf16[4,96,768]{2,1,0:T(8,128)(2,1)S(1)}, u32[]{:S(2)}, u32[]{:S(2)}) collective-permute-start(bf16[4,96,768]{2,1,0:T(8,128)(2,1)S(1)} %get-tuple-element.128), channel_id=1, source_target_pairs={{0,16},{16,0},{1,17},{17,1},{2,18},{18,2},{3,19},{19,3},{4,20},{20... | collective-permute-start | bytes 1769480 | tf_op jit(solution)/shard_map/ppermute | solution.py:49
  122.4 27.4 %collective-permute-start.30 = (bf16[4,96,768]{2,1,0:T(8,128)(2,1)S(1)}, bf16[4,96,768]{2,1,0:T(8,128)(2,1)S(1)}, u32[]{:S(2)}, u32[]{:S(2)}) collective-permute-start(bf16[4,96,768]{2,1,0:T(8,128)(2,1)S(1)} %get-tuple-element.152), channel_id=1, source_target_pairs={{0,16},{16,0},{1,17},{17,1},{2,18},{18,2},{3,19},{19,3},{4,20},{20... | collective-permute-start | bytes 1769480 | tf_op jit(solution)/shard_map/ppermute | solution.py:49
  135.9 34.2 %collective-permute-start.29 = (bf16[4,208,384]{2,1,0:T(8,128)(2,1)S(1)}, bf16[4,208,384]{2,1,0:T(8,128)(2,1)S(1)}, u32[]{:S(2)}, u32[]{:S(2)}) collective-permute-start(bf16[4,208,384]{2,1,0:T(8,128)(2,1)S(1)} %get-tuple-element.143), channel_id=1, source_target_pairs={{0,16},{16,0},{1,17},{17,1},{2,18},{18,2},{3,19},{19,3},{4,20},{20... | collective-permute-start | bytes 1916936 | tf_op jit(solution)/shard_map/ppermute | solution.py:49
  137.4 26.1 %collective-permute-start.24 = (bf16[384,512]{1,0:T(8,128)(2,1)S(1)}, bf16[384,512]{1,0:T(8,128)(2,1)S(1)}, u32[]{:S(2)}, u32[]{:S(2)}) collective-permute-start(bf16[384,512]{1,0:T(8,128)(2,1)S(1)} %get-tuple-element.145), channel_id=1, source_target_pairs={{0,1},{1,0},{2,3},{3,2},{4,5},{5,4},{6,7},{7,6},{8,9},{9,8},{10,11... | collective-permute-start | bytes 1179656 | tf_op jit(solution)/shard_map/ppermute | solution.py:49
  137.6 14.3 %collective-permute-start.35 = (bf16[96,768]{1,0:T(8,128)(2,1)S(1)}, bf16[96,768]{1,0:T(8,128)(2,1)S(1)}, u32[]{:S(2)}, u32[]{:S(2)}) collective-permute-start(bf16[96,768]{1,0:T(8,128)(2,1)S(1)} %get-tuple-element.161), channel_id=1, source_target_pairs={{8,0},{12,4},{0,8},{4,12},{9,1},{13,5},{1,9},{5,13},{10,2},{14,6},... | collective-permute-start | bytes 442376 | tf_op jit(solution)/shard_map/ppermute | solution.py:75
  140.8 15.3 %collective-permute-start.36 = (bf16[96,768]{1,0:T(8,128)(2,1)S(1)}, bf16[96,768]{1,0:T(8,128)(2,1)S(1)}, u32[]{:S(2)}, u32[]{:S(2)}) collective-permute-start(bf16[96,768]{1,0:T(8,128)(2,1)S(1)} %get-tuple-element.162), channel_id=1, source_target_pairs={{12,0},{0,4},{4,8},{8,12},{13,1},{1,5},{5,9},{9,13},{14,2},{2,6},{... | collective-permute-start | bytes 442376 | tf_op jit(solution)/shard_map/ppermute | solution.py:75
  151.8 13.8 %collective-permute-start.31 = (bf16[96,768]{1,0:T(8,128)(2,1)S(1)}, bf16[96,768]{1,0:T(8,128)(2,1)S(1)}, u32[]{:S(2)}, u32[]{:S(2)}) collective-permute-start(bf16[96,768]{1,0:T(8,128)(2,1)S(1)} %get-tuple-element.155), channel_id=1, source_target_pairs={{8,0},{12,4},{0,8},{4,12},{9,1},{13,5},{1,9},{5,13},{10,2},{14,6},... | collective-permute-start | bytes 442376 | tf_op jit(solution)/shard_map/ppermute | solution.py:75
  156.1 11.7 %collective-permute-start.32 = (bf16[96,768]{1,0:T(8,128)(2,1)S(1)}, bf16[96,768]{1,0:T(8,128)(2,1)S(1)}, u32[]{:S(2)}, u32[]{:S(2)}) collective-permute-start(bf16[96,768]{1,0:T(8,128)(2,1)S(1)} %get-tuple-element.156), channel_id=1, source_target_pairs={{12,0},{0,4},{4,8},{8,12},{13,1},{1,5},{5,9},{9,13},{14,2},{2,6},{... | collective-permute-start | bytes 442376 | tf_op jit(solution)/shard_map/ppermute | solution.py:75
  167.9 25.4 %collective-permute-start.42 = (bf16[96,768]{1,0:T(8,128)(2,1)S(1)}, bf16[96,768]{1,0:T(8,128)(2,1)S(1)}, u32[]{:S(2)}, u32[]{:S(2)}) collective-permute-start(bf16[96,768]{1,0:T(8,128)(2,1)S(1)} %add_convert_fusion.5.i_own), channel_id=1, source_target_pairs={{0,16},{16,0},{1,17},{17,1},{2,18},{18,2},{3,19},{19,3},{4,20},{20... | collective-permute-start | bytes 442376 | tf_op jit(solution)/shard_map/ppermute | solution.py:49
  172.4 20.8 %collective-permute-start.40 = (bf16[208,384]{1,0:T(8,128)(2,1)S(1)}, bf16[208,384]{1,0:T(8,128)(2,1)S(1)}, u32[]{:S(2)}, u32[]{:S(2)}) collective-permute-start(bf16[208,384]{1,0:T(8,128)(2,1)S(1)} %get-tuple-element.167), channel_id=1, source_target_pairs={{12,0},{0,4},{4,8},{8,12},{13,1},{1,5},{5,9},{9,13},{14,2},{2,6},{... | collective-permute-start | bytes 479240 | tf_op jit(solution)/shard_map/ppermute | solution.py:75
  174.1 19.1 %collective-permute-start.41 = (bf16[208,384]{1,0:T(8,128)(2,1)S(1)}, bf16[208,384]{1,0:T(8,128)(2,1)S(1)}, u32[]{:S(2)}, u32[]{:S(2)}) collective-permute-start(bf16[208,384]{1,0:T(8,128)(2,1)S(1)} %get-tuple-element.168), channel_id=1, source_target_pairs={{4,0},{8,4},{12,8},{0,12},{5,1},{9,5},{13,9},{1,13},{6,2},{10,6},{... | collective-permute-start | bytes 479240 | tf_op jit(solution)/shard_map/ppermute | solution.py:75
  175.0 21.2 %collective-permute-start.26 = (bf16[192,512]{1,0:T(8,128)(2,1)S(1)}, bf16[192,512]{1,0:T(8,128)(2,1)S(1)}, u32[]{:S(2)}, u32[]{:S(2)}) collective-permute-start(bf16[192,512]{1,0:T(8,128)(2,1)S(1)} %pad_maximum_fusion), channel_id=1, source_target_pairs={{0,0},{10,1},{7,2},{13,3},{1,4},{11,5},{4,6},{14,7},{2,8},{8,9},{5... | collective-permute-start | bytes 589832 | tf_op jit(solution)/shard_map/ppermute | solution.py:70
  181.3 15.0 %collective-permute-start.28 = (bf16[192,512]{1,0:T(8,128)(2,1)S(1)}, bf16[192,512]{1,0:T(8,128)(2,1)S(1)}, u32[]{:S(2)}, u32[]{:S(2)}) collective-permute-start(bf16[192,512]{1,0:T(8,128)(2,1)S(1)} %finish.1), channel_id=1, source_target_pairs={{0,0},{10,1},{7,2},{13,3},{1,4},{11,5},{4,6},{14,7},{2,8},{8,9},{5... | collective-permute-start | bytes 589832 | tf_op jit(solution)/shard_map/ppermute | solution.py:70
  (45 other events, 447.1 us)

commit v6 on v5

--- a/solution.py
+++ b/solution.py
@@ -9,7 +9,6 @@
 EPSILON = 1e-12
 F32 = jnp.float32
 BF16 = jnp.bfloat16
-EXTRA = 32
 
 
 def dot(left, right, left_dim, right_dim):
@@ -275,7 +274,7 @@
 
 
 def turn_kernel(
-    flags, scaled_one, own, away, vecs, g_own, g_high, g_low,
+    flags, scaled_one, own, away, vecs, g_own, g_pair, g_high, g_last,
     keep, give, grad_second, grad_returned, sums, final, grad,
 ):
     low, col, length = flags[0], flags[2], flags[3]
@@ -285,7 +284,7 @@
     def rows(bit):
         return pl.ds(pl.multiple_of((col ^ bit) * feats, feats), feats)
 
-    for bit, ref in ((0, g_own), (2, g_high)):
+    for bit, ref in enumerate((g_own, g_pair, g_high, g_last)):
 
         @pl.when(low == 0)
         def _():
@@ -294,9 +293,6 @@
         @pl.when(low == 1)
         def _():
             grad[rows(bit), :] = ref[:, half:]
-
-    grad[rows(1), :] = g_low[:feats]
-    grad[rows(3), :] = g_low[feats:]
 
     normed = scaled_one[...] * vecs[:, 1:2] + vecs[:, 2:3]
     second = normed + own[...].astype(F32) + away[...].astype(F32) + vecs[:, 3:4]
@@ -337,22 +333,16 @@
     b_in_sums[...] = total
 
 
-def wide_grad_kernel(
-    flags, r_own, r_away, hidden, n_own, n_away, grad_pre, b_keep, b_give, i_keep, i_give
-):
+def wide_grad_kernel(flags, own, away, right, keep, give):
     odd = flags[1]
-    half = r_own.shape[1]
-    part = b_keep.shape[1]
+    half = own.shape[1]
+    part = keep.shape[1]
     for k in range(4):
-        for pick, b_out, i_out in ((1 - odd, b_give, i_give), (odd, b_keep, i_keep)):
+        for pick, out in ((1 - odd, give), (odd, keep)):
             rows = pl.ds(pl.multiple_of((2 * k + pick) * part, part), part)
-            for out, own, away, right in (
-                (b_out, r_own, r_away, hidden),
-                (i_out, n_own, n_away, grad_pre),
-            ):
-                total = dot(own[rows, :], right[:, :half], 1, 1)
-                total = total + dot(away[rows, :], right[:, half:], 1, 1)
-                out[k] = total.astype(BF16)
+            total = dot(own[rows, :], right[:, :half], 1, 1)
+            total = total + dot(away[rows, :], right[:, half:], 1, 1)
+            out[k] = total.astype(BF16)
 
 
 def norm_back_kernel(
@@ -456,7 +446,7 @@
         out[...] = (keep[k].astype(F32) + got[k].astype(F32)).astype(BF16)
 
 
-def unpack_kernel(flags, own, got, qkv, w_out, tail):
+def unpack_kernel(flags, own, got, qkv, w_out, b_in, *lines):
     odd = flags[1]
     feats, width = w_out.shape[1], w_out.shape[0]
 
@@ -465,8 +455,13 @@
         qkv[feats : 2 * feats] = first[:feats, width:].astype(F32)
         qkv[2 * feats :] = second[:feats, :width].astype(F32)
         w_out[...] = second[:feats, width:].astype(F32)
-        tail[:16] = first[feats:, :feats].astype(F32)
-        tail[16:] = first[feats:, feats:].astype(F32)
+        tail = first[feats:].astype(F32)
+        for at in range(6):
+            lines[at][...] = tail[at, :feats]
+        for at in range(4):
+            b_in[at * feats : (at + 1) * feats] = tail[at, feats:]
+        for at in range(2):
+            lines[6 + at][...] = tail[4 + at, feats:]
 
     @pl.when(odd == 0)
     def _():
@@ -594,14 +589,15 @@
     fetched = lax.all_gather(after(pack_half, wide), "row")
     swapped = swap_bit(fetched, "dp", 1)
     wide = after(wide, fetched)
-    wide_fetched = [from_row(wide, k) for k in range(1, n_rows)]
+    wide_fetched = [from_row(wide, 1), None, from_row(wide, 3)]
+    wide_fetched[1] = from_row(wide_fetched[0], 1)
     x0 = after(x0, flags, fetched)
     x2 = swap_bit(x0, "col", 2)
     x1 = swap_bit(x0, "col", 1)
     wide_swapped = [swap_bit(after(part, x2), "dp", 1) for part in wide_fetched]
     g_own = to_slot(after(out_grad.astype(BF16), fetched))
-    ready = (wide_swapped[0], wide_fetched[1], wide_swapped[2])
-    x3 = swap_bit(after(x2, swapped, g_own, *ready), "col", 1)
+    ready = (wide_swapped[0], wide_fetched[1], wide_swapped[2], g_own)
+    x3 = swap_bit(after(x2, swapped, *ready), "col", 1)
 
     in_all, back_all, vecs, in_bias = call(
         assemble_kernel,
@@ -652,9 +648,9 @@
         [n_own, n_away, in_all, back_all, in_bias],
         weight=0,
     )
-    g_both = jnp.concatenate((after(g_own, hidden), g_high))
-    g_low = swap_bit(jnp.where(low_bit, g_both[:, :half], g_both[:, half:]), "col", 1)
-    own = sum_cores(after(mine, g_low), other)
+    g_pair = swap_bit(g_own, "col", 1)
+    g_last = swap_bit(g_high, "col", 1)
+    own = sum_cores(after(mine, g_last), other)
     away = swap_bit(own, "col", 2)
     out_own, out_give, grad_second, r_own, sums = call(
         turn_kernel,
@@ -666,34 +662,39 @@
             halves,
             shape((8, model), F32),
         ],
-        [flags, scaled_one, own, away, vecs, g_own, g_high, g_low],
+        [flags, scaled_one, own, away, vecs, g_own, g_pair, g_high, g_last],
         scratch=[pltpu.VMEM((model, half), BF16), pltpu.VMEM((model, half), BF16)],
         weight=0,
     )
     r_away = swap_bit(r_own, "col", 1)
+    b_keep, b_give = call(
+        wide_grad_kernel,
+        "back_grads",
+        [shape((n_rows, feats // 2, units), BF16)] * 2,
+        [flags, r_own, r_away, hidden],
+    )
+    b_got = swap_bit(b_give, "dp", 1)
     mine, other, grad_pre, b_in_sums = call(
         backward_kernel,
         "feed_backward",
         [wide_halves, halves, shape((units, slot), BF16), shape((8, feats), F32)],
-        [r_own, r_away, slope, in_all, back_all],
+        [r_own, r_away, after(slope, b_give), in_all, back_all],
         weight=0,
     )
     own = sum_cores(mine, other)
-    b_keep, b_give, i_keep, i_give = call(
+    i_keep, i_give = call(
         wide_grad_kernel,
-        "wide_grads",
-        [shape((n_rows, feats // 2, units), BF16)] * 4,
-        [flags, after(r_own, own), r_away, hidden, n_own, n_away, grad_pre],
-        weight=0,
-    )
-    b_got = swap_bit(b_give, "dp", 1)
+        "into_grads",
+        [shape((n_rows, feats // 2, units), BF16)] * 2,
+        [flags, after(n_own, own), n_away, grad_pre],
+    )
     i_got = swap_bit(i_give, "dp", 1)
     away = swap_bit(own, "col", 2)
     grad_first, a_own, sums = call(
         norm_back_kernel,
         "norm_back",
         [wide_halves, halves, shape((8, model), F32)],
-        [own, after(away, b_give), grad_second, scaled_one, inverse_one, vecs, sums],
+        [own, after(away, i_give), grad_second, scaled_one, inverse_one, vecs, sums],
         weight=0,
     )
     a_away = swap_bit(a_own, "col", 1)
@@ -738,9 +739,10 @@
 
     totals = []
     for name, keep, got in (
-        ("back_add", b_keep, after(b_got, grad_qkv)),
+        ("back_add", b_keep, after(b_got, i_give)),
         ("into_add", i_keep, after(i_got, pack_give)),
     ):
+        got = after(got, *totals)
         parts = call(
             pack_add_kernel, name, [shape((feats // 2, units), BF16)] * n_rows, [keep, got]
         )
@@ -760,14 +762,15 @@
         [pack_keep, pack_got],
     )
     total = add_replicas(add_rows(packs), 2)
-    w_qkv_grad, w_out_grad, tail = call(
+    w_qkv_grad, w_out_grad, b_in_grad, *lines = call(
         unpack_kernel,
         "unpack",
         [
             shape((3 * feats, width), F32),
             shape((width, feats), F32),
-            shape((EXTRA, feats), F32),
-        ],
+            shape((units,), F32),
+        ]
+        + [shape((feats,), F32)] * 8,
         [flags, total, swap_bit(after(total, i_back), "dp", 1)],
     )
     w_qkv_grad = w_qkv_grad.reshape(3, feats, width).transpose(1, 0, 2)
@@ -775,18 +778,18 @@
         layer_out,
         in_grad,
         w_qkv_grad,
-        tail[20],
-        tail[21],
+        lines[6],
+        lines[7],
         w_out_grad,
-        tail[4],
-        tail[0],
-        tail[1],
+        lines[4],
+        lines[0],
+        lines[1],
         w_in_grad,
-        tail[16:20].reshape(-1),
+        b_in_grad,
         w_back_grad,
-        tail[5],
-        tail[2],
-        tail[3],
+        lines[5],
+        lines[2],
+        lines[3],
     )
 
 

time: 206 us -> 198 us (0.961)
  starting transfers between devices: 57.9 us -> 44.9 us
  waiting for transfers between devices: 75.7 us -> 87.2 us
  local copies, waits for them, and re-layouts: 9 us -> 3.25 us
    ppermute x12, waiting for transfers between devices: 24 us -> 35.7 us  [from_row(): lax.ppermute(value, 'row', [((a + away) % size, a) for a in range(size)])]
    ppermute x12, starting transfers between devices: 24 us -> 14.5 us  [from_row(): lax.ppermute(value, 'row', [((a + away) % size, a) for a in range(size)])]
    ppermute x28 -> x29, waiting for transfers between devices: 39.2 us -> 44.7 us  [swap_bit(): return lax.ppermute(value, axis, [(at, at ^ bit) for at in range(size)])]
    ppermute x2, waiting for transfers between devices: 12.3 us -> 6.86 us  [to_slot(): return lax.ppermute(value, ('row', 'col'), grid_pairs())]
    unnamed x52 -> x39, local copies, waits for them, and re-layouts: 4.97 us -> 1.42 us
    ppermute x2, starting transfers between devices: 7.72 us -> 4.48 us  [from_slot(): lax.ppermute(value, ('row', 'col'), [(b, a) for a, b in grid_pairs()])]
    pallas_call x18 -> x19, Pallas kernels: 39 us -> 37.9 us  [call(): pl.pallas_call(kernel, name=name, out_shape=outs, grid=(1,) if windowed e...]
    ppermute x28 -> x29, starting transfers between devices: 22.2 us -> 21.9 us  [swap_bit(): return lax.ppermute(value, axis, [(at, at ^ bit) for at in range(size)])]
  transfers between devices with their start and end apart: 44 -> 45, of which waited for: 22 -> 22; matrix products, arithmetic and copies ran while one was open for 2% -> 2% of each run, Pallas kernels for 11% -> 10%
where the time goes in v6:
time: 198 us; the launch traced here: 195 us
  waiting for transfers between devices  87.2 us (44%)
  starting transfers between devices  44.9 us (23%)
  Pallas kernels  37.9 us (19%)
  blocking collectives  16.9 us (9%)
  other arithmetic  3.55 us (2%)
  local copies, waits for them, and re-layouts  3.25 us (2%)
    ppermute x29, waiting for transfers between devices, swap_bit(): return lax.ppermute(value, axis, [(at, at ^ bit) for at in range(size)])  44.7 us
    pallas_call x19, Pallas kernels, call(): pl.pallas_call(kernel, name=name, out_shape=outs, grid=(1,) if windowed e...  37.9 us
    ppermute x12, waiting for transfers between devices, from_row(): lax.ppermute(value, 'row', [((a + away) % size, a) for a in range(size)])  35.7 us
    ppermute x29, starting transfers between devices, swap_bit(): return lax.ppermute(value, axis, [(at, at ^ bit) for at in range(size)])  21.9 us
    all_gather x1, blocking collectives, shards(): fetched = lax.all_gather(after(pack_half, wide), 'row')  16.9 us
    ppermute x12, starting transfers between devices, from_row(): lax.ppermute(value, 'row', [((a + away) % size, a) for a in range(size)])  14.5 us
    ppermute x2, waiting for transfers between devices, to_slot(): return lax.ppermute(value, ('row', 'col'), grid_pairs())  6.86 us
    ppermute x2, starting transfers between devices, from_slot(): lax.ppermute(value, ('row', 'col'), [(b, a) for a, b in grid_pairs()])  4.48 us
  transfers between devices with their start and end apart: 45, of which 22 were waited for; matrix products, arithmetic and copies ran while one was open for 2% of the time, Pallas kernels for 10%

profile of v6, /device:TPU:20, one launch (start us, length us, event | category | flops | bytes accessed | tf_op | source)
XLA Modules:
  0.0 194.8 jit_solution(2733983790711316368)
XLA Ops:
  4.7 16.9 %all-gather = bf16[768,384]{1,0:T(8,128)(2,1)S(1)} all-gather(bf16[192,384]{1,0:T(8,128)(2,1)} %get-tuple-element.106), channel_id=2, replica_groups=mesh['dp'=2,'row'=4,'col'=4] {'row'}, dimensions={0}, use_global_device_ids=true | all-gather | bytes 737280 | tf_op jit(solution)/shard_map/all_gather | solution.py:589
  27.8 4.9 %collective-permute-done.4.f1 = bf16[208,768]{1,0:T(8,128)(2,1)S(1)} collective-permute-done((bf16[208,768]{1,0:T(8,128)(2,1)}, bf16[208,768]{1,0:T(8,128)(2,1)S(1)}, u32[]{:S(2)}, u32[]{:S(2)}) %collective-permute-start.4) | collective-permute-done | bytes 319520 | tf_op jit(solution)/shard_map/ppermute | solution.py:74
  32.8 6.6 %collective-permute-done.7.f3 = bf16[208,768]{1,0:T(8,128)(2,1)S(1)} collective-permute-done((bf16[208,768]{1,0:T(8,128)(2,1)}, bf16[208,768]{1,0:T(8,128)(2,1)S(1)}, u32[]{:S(2)}, u32[]{:S(2)}) %collective-permute-start.7) | collective-permute-done | bytes 319520 | tf_op jit(solution)/shard_map/ppermute | solution.py:74
  43.4 6.9 %collective-permute-done.9.g_own = bf16[192,512]{1,0:T(8,128)(2,1)S(1)} collective-permute-done((bf16[192,512]{1,0:T(8,128)(2,1)S(1)}, bf16[192,512]{1,0:T(8,128)(2,1)S(1)}, u32[]{:S(2)}, u32[]{:S(2)}) %collective-permute-start.9) | collective-permute-done | bytes 196640 | tf_op jit(solution)/shard_map/ppermute | solution.py:65
  50.2 3.2 %collective-permute-start.1 = (bf16[192,512]{1,0:T(8,128)(2,1)S(1)}, bf16[192,512]{1,0:T(8,128)(2,1)S(1)}, u32[]{:S(2)}, u32[]{:S(2)}) collective-permute-start(bf16[192,512]{1,0:T(8,128)(2,1)S(1)} %collective-permute-done.x0), channel_id=1, source_target_pairs={{0,1},{1,0},{2,3},{3,2},{4,5},{5,4},{6,7},{7,6},{8,9},{9,8},{10,11... | collective-permute-start | bytes 589832 | tf_op jit(solution)/shard_map/ppermute | solution.py:48
  56.9 7.9 %attend.1 = (bf16[768,512]{1,0:T(8,128)(2,1)}, bf16[4,2,192,384]{3,2,1,0:T(8,128)(2,1)}, bf16[576,512]{1,0:T(8,128)(2,1)}, bf16[3,512,512]{2,1,0:T(8,128)(2,1)},...) custom-call(s32[6]{0:T(128)} %stack.24.flags, bf16[192,512]{1,0:T(8,128)(2,1)} %copy-done.14, ...), custom_call_target="tpu_custom_call" | custom-call | tf_op jit(solution)/shard_map/attend/pallas_call | solution.py:27
  70.2 7.8 %collective-permute-done.13.s2 = bf16[208,768]{1,0:T(8,128)(2,1)S(1)} collective-permute-done((bf16[208,768]{1,0:T(8,128)(2,1)S(1)}, bf16[208,768]{1,0:T(8,128)(2,1)S(1)}, u32[]{:S(2)}, u32[]{:S(2)}) %collective-permute-start.13) | collective-permute-done | bytes 319520 | tf_op jit(solution)/shard_map/ppermute | solution.py:48
  84.1 3.5 %collective-permute-done.15.g_high = bf16[192,512]{1,0:T(8,128)(2,1)S(1)} collective-permute-done((bf16[192,512]{1,0:T(8,128)(2,1)S(1)}, bf16[192,512]{1,0:T(8,128)(2,1)S(1)}, u32[]{:S(2)}, u32[]{:S(2)}) %collective-permute-start.15) | collective-permute-done | bytes 196640 | tf_op jit(solution)/shard_map/ppermute | solution.py:48
  92.1 8.3 %collective-permute-done.18.away = bf16[768,256]{1,0:T(8,128)(2,1)S(1)} collective-permute-done((bf16[768,256]{1,0:T(8,128)(2,1)S(1)}, bf16[768,256]{1,0:T(8,128)(2,1)S(1)}, u32[]{:S(2)}, u32[]{:S(2)}) %collective-permute-start.18) | collective-permute-done | bytes 393248 | tf_op jit(solution)/shard_map/ppermute | solution.py:48
  100.4 2.5 %turn.1 = (bf16[192,256]{1,0:T(8,128)(2,1)S(1)}, bf16[192,256]{1,0:T(8,128)(2,1)S(1)}, f32[768,256]{1,0:T(8,128)S(1)}, bf16[768,256]{1,0:T(8,128)(2,1)S(1)}, f32[8,768]{1,0:T(8,128)S(1)}) custom-call(s32[6]{0:T(128)S(1)} %copy-done.8, f32[768,256]{1,0:T(8,128)S(1)} %get-tuple-element.119.scaled_one.scaled, bf16[768,256]{1,0:T(8,128)(2,1)S(1)} %add_convert_fusion.1.own, ...), custom_call_target="tpu_custom_call" | custom-call | tf_op jit(solution)/shard_map/turn/pallas_call | solution.py:27
  104.7 2.5 %back_grads.1 = (bf16[4,96,768]{2,1,0:T(8,128)(2,1)S(1)}, bf16[4,96,768]{2,1,0:T(8,128)(2,1)S(1)}) custom-call(s32[6]{0:T(128)S(1)} %copy-done.8, bf16[768,256]{1,0:T(8,128)(2,1)S(1)} %get-tuple-element.129.own.r_own, bf16[768,256]{1,0:T(8,128)(2,1)S(1)} %collective-permute-done.20.away.r_away, bf16[768,512]{1,0:T(8,128)(2,1)S(1)} %get-tuple-element.131.right), custom_call_target="tpu_custom_call" | custom-call | tf_op jit(solution)/shard_map/back_grads/pallas_call | solution.py:27
  113.7 2.5 %into_grads.1 = (bf16[4,96,768]{2,1,0:T(8,128)(2,1)S(1)}, bf16[4,96,768]{2,1,0:T(8,128)(2,1)S(1)}) custom-call(s32[6]{0:T(128)S(1)} %copy-done.8, bf16[768,256]{1,0:T(8,128)(2,1)S(1)} %get-tuple-element.136.n_own.own, bf16[768,256]{1,0:T(8,128)(2,1)S(1)} %collective-permute-done.14.n_away.away, bf16[768,512]{1,0:T(8,128)(2,1)S(1)} %get-tuple-element.137.right), custom_call_target="tpu_custom_call" | custom-call | tf_op jit(solution)/shard_map/into_grads/pallas_call | solution.py:27
  116.3 5.7 %collective-permute-done.22.away = bf16[768,256]{1,0:T(8,128)(2,1)S(1)} collective-permute-done((bf16[768,256]{1,0:T(8,128)(2,1)S(1)}, bf16[768,256]{1,0:T(8,128)(2,1)S(1)}, u32[]{:S(2)}, u32[]{:S(2)}) %collective-permute-start.22) | collective-permute-done | bytes 393248 | tf_op jit(solution)/shard_map/ppermute | solution.py:48
  124.7 3.6 %collective-permute-done.32.got = bf16[4,96,768]{2,1,0:T(8,128)(2,1)S(1)} collective-permute-done((bf16[4,96,768]{2,1,0:T(8,128)(2,1)S(1)}, bf16[4,96,768]{2,1,0:T(8,128)(2,1)S(1)}, u32[]{:S(2)}, u32[]{:S(2)}) %collective-permute-start.32) | collective-permute-done | bytes 589856 | tf_op jit(solution)/shard_map/ppermute | solution.py:48
  128.5 2.7 %collective-permute-start.33 = (bf16[96,768]{1,0:T(8,128)(2,1)S(1)}, bf16[96,768]{1,0:T(8,128)(2,1)S(1)}, u32[]{:S(2)}, u32[]{:S(2)}) collective-permute-start(bf16[96,768]{1,0:T(8,128)(2,1)S(1)} %get-tuple-element.166), channel_id=1, source_target_pairs={{8,0},{12,4},{0,8},{4,12},{9,1},{13,5},{1,9},{5,13},{10,2},{14,6},... | collective-permute-start | bytes 442376 | tf_op jit(solution)/shard_map/ppermute | solution.py:74
  133.3 5.4 %attend_back.1 = (bf16[576,512]{1,0:T(8,128)(2,1)S(1)}, f32[384,512]{1,0:T(8,128)S(1)}, bf16[384,512]{1,0:T(8,128)(2,1)}) custom-call(s32[6]{0:T(128)S(1)} %copy-done.8, bf16[768,256]{1,0:T(8,128)(2,1)S(1)} %get-tuple-element.143.a_own, bf16[768,256]{1,0:T(8,128)(2,1)S(1)} %collective-permute-done.23.a_away, bf16[4,2,192,384]{3,2,1,0:T(8,128)(2,1)S(1)} %copy-done.2, ...), custom_call_target="tpu_custom_call" | custom-call | tf_op jit(solution)/shard_map/attend_back/pallas_call | solution.py:27
  138.7 2.9 %pack_grads.1 = (bf16[4,208,384]{2,1,0:T(8,128)(2,1)S(1)}, bf16[4,208,384]{2,1,0:T(8,128)(2,1)S(1)}) custom-call(s32[6]{0:T(128)S(1)} %copy-done.8, bf16[768,512]{1,0:T(8,128)(2,1)S(1)} %copy-done, bf16[576,512]{1,0:T(8,128)(2,1)S(1)} %get-tuple-element.149.grad_qkv, bf16[768,256]{1,0:T(8,128)(2,1)S(1)} %get-tuple-element.143.a_own, ...), custom_call_target="tpu_custom_call" | custom-call | tf_op jit(solution)/shard_map/pack_grads/pallas_call | solution.py:27
  149.5 6.5 %collective-permute-done.36 = bf16[96,768]{1,0:T(8,128)(2,1)} collective-permute-done((bf16[96,768]{1,0:T(8,128)(2,1)}, bf16[96,768]{1,0:T(8,128)(2,1)}, u32[]{:S(2)}, u32[]{:S(2)}) %collective-permute-start.36) | collective-permute-done | bytes 147488 | tf_op jit(solution)/shard_map/ppermute | solution.py:74
  156.0 4.9 %collective-permute-done.37 = bf16[96,768]{1,0:T(8,128)(2,1)} collective-permute-done((bf16[96,768]{1,0:T(8,128)(2,1)}, bf16[96,768]{1,0:T(8,128)(2,1)}, u32[]{:S(2)}, u32[]{:S(2)}) %collective-permute-start.37) | collective-permute-done | bytes 147488 | tf_op jit(solution)/shard_map/ppermute | solution.py:74
  165.9 3.3 %collective-permute-done.28.got = bf16[192,512]{1,0:T(8,128)(2,1)S(1)} collective-permute-done((bf16[192,512]{1,0:T(8,128)(2,1)S(1)}, bf16[192,512]{1,0:T(8,128)(2,1)S(1)}, u32[]{:S(2)}, u32[]{:S(2)}) %collective-permute-start.28) | collective-permute-done | bytes 196640 | tf_op jit(solution)/shard_map/ppermute | solution.py:48
  169.2 2.1 %collective-permute-start.27 = (bf16[192,512]{1,0:T(8,128)(2,1)S(1)}, bf16[192,512]{1,0:T(8,128)(2,1)S(1)}, u32[]{:S(2)}, u32[]{:S(2)}) collective-permute-start(bf16[192,512]{1,0:T(8,128)(2,1)S(1)} %pad_maximum_fusion), channel_id=1, source_target_pairs={{0,0},{10,1},{7,2},{13,3},{1,4},{11,5},{4,6},{14,7},{2,8},{8,9},{5... | collective-permute-start | bytes 589832 | tf_op jit(solution)/shard_map/ppermute | solution.py:69
  171.9 3.0 %collective-permute-done.40 = bf16[208,384]{1,0:T(8,128)(2,1)S(1)} collective-permute-done((bf16[208,384]{1,0:T(8,128)(2,1)S(1)}, bf16[208,384]{1,0:T(8,128)(2,1)S(1)}, u32[]{:S(2)}, u32[]{:S(2)}) %collective-permute-start.40) | collective-permute-done | bytes 159776 | tf_op jit(solution)/shard_map/ppermute | solution.py:74
  174.9 2.4 %collective-permute-start.29 = (bf16[192,512]{1,0:T(8,128)(2,1)S(1)}, bf16[192,512]{1,0:T(8,128)(2,1)S(1)}, u32[]{:S(2)}, u32[]{:S(2)}) collective-permute-start(bf16[192,512]{1,0:T(8,128)(2,1)S(1)} %finish.1), channel_id=1, source_target_pairs={{0,0},{10,1},{7,2},{13,3},{1,4},{11,5},{4,6},{14,7},{2,8},{8,9},{5... | collective-permute-start | bytes 589832 | tf_op jit(solution)/shard_map/ppermute | solution.py:69
  177.3 9.8 %collective-permute-done.41 = bf16[208,384]{1,0:T(8,128)(2,1)S(1)} collective-permute-done((bf16[208,384]{1,0:T(8,128)(2,1)S(1)}, bf16[208,384]{1,0:T(8,128)(2,1)S(1)}, u32[]{:S(2)}, u32[]{:S(2)}) %collective-permute-start.41) | collective-permute-done | bytes 159776 | tf_op jit(solution)/shard_map/ppermute | solution.py:74
  (137 shorter events, 67.8 us)
Async XLA Ops:
  0.7 26.8 %collective-permute-start = (bf16[192,512]{1,0:T(8,128)(2,1)}, bf16[192,512]{1,0:T(8,128)(2,1)S(1)}, u32[]{:S(2)}, u32[]{:S(2)}) collective-permute-start(bf16[192,512]{1,0:T(8,128)(2,1)} %param.16), channel_id=1, source_target_pairs={{0,0},{1,10},{2,7},{3,13},{4,1},{5,11},{6,4},{7,14},{8,2},{9,8},{1... | collective-permute-start | bytes 589832 | tf_op jit(solution)/shard_map/ppermute | solution.py:65
  22.9 16.5 %collective-permute-start.7 = (bf16[208,768]{1,0:T(8,128)(2,1)}, bf16[208,768]{1,0:T(8,128)(2,1)S(1)}, u32[]{:S(2)}, u32[]{:S(2)}) collective-permute-start(bf16[208,768]{1,0:T(8,128)(2,1)} %get-tuple-element.108), channel_id=1, source_target_pairs={{12,0},{0,4},{4,8},{8,12},{13,1},{1,5},{5,9},{9,13},{14,2},{2,6},{... | collective-permute-start | bytes 958472 | tf_op jit(solution)/shard_map/ppermute | solution.py:74
  24.1 29.3 %collective-permute-start.3 = (bf16[4,192,384]{2,1,0:T(8,128)(2,1)S(1)}, bf16[4,192,384]{2,1,0:T(8,128)(2,1)S(1)}, u32[]{:S(2)}, u32[]{:S(2)}) collective-permute-start(bf16[4,192,384]{2,1,0:T(8,128)(2,1)S(1)} %bitcast.12), channel_id=1, source_target_pairs={{0,16},{16,0},{1,17},{17,1},{2,18},{18,2},{3,19},{19,3},{4,20},{20... | collective-permute-start | bytes 1769480 | tf_op jit(solution)/shard_map/ppermute | solution.py:48
  27.4 11.9 %collective-permute-start.2 = (bf16[192,512]{1,0:T(8,128)(2,1)S(1)}, bf16[192,512]{1,0:T(8,128)(2,1)S(1)}, u32[]{:S(2)}, u32[]{:S(2)}) collective-permute-start(bf16[192,512]{1,0:T(8,128)(2,1)S(1)} %collective-permute-done.x0), channel_id=1, source_target_pairs={{0,2},{1,3},{2,0},{3,1},{4,6},{5,7},{6,4},{7,5},{8,10},{9,11},{10,... | collective-permute-start | bytes 589832 | tf_op jit(solution)/shard_map/ppermute | solution.py:48
  32.6 20.8 %collective-permute-start.6 = (bf16[208,768]{1,0:T(8,128)(2,1)S(1)}, bf16[208,768]{1,0:T(8,128)(2,1)S(1)}, u32[]{:S(2)}, u32[]{:S(2)}) collective-permute-start(bf16[208,768]{1,0:T(8,128)(2,1)S(1)} %collective-permute-done.4.f1), channel_id=1, source_target_pairs={{4,0},{8,4},{12,8},{0,12},{5,1},{9,5},{13,9},{1,13},{6,2},{10,6},{... | collective-permute-start | bytes 958472 | tf_op jit(solution)/shard_map/ppermute | solution.py:74
  39.4 14.0 %collective-permute-start.8 = (bf16[208,768]{1,0:T(8,128)(2,1)S(1)}, bf16[208,768]{1,0:T(8,128)(2,1)S(1)}, u32[]{:S(2)}, u32[]{:S(2)}) collective-permute-start(bf16[208,768]{1,0:T(8,128)(2,1)S(1)} %collective-permute-done.7.f3), channel_id=1, source_target_pairs={{0,16},{16,0},{1,17},{17,1},{2,18},{18,2},{3,19},{19,3},{4,20},{20... | collective-permute-start | bytes 958472 | tf_op jit(solution)/shard_map/ppermute | solution.py:48
  40.9 13.9 %collective-permute-start.5 = (bf16[208,768]{1,0:T(8,128)(2,1)S(1)}, bf16[208,768]{1,0:T(8,128)(2,1)S(1)}, u32[]{:S(2)}, u32[]{:S(2)}) collective-permute-start(bf16[208,768]{1,0:T(8,128)(2,1)S(1)} %collective-permute-done.4.f1), channel_id=1, source_target_pairs={{0,16},{16,0},{1,17},{17,1},{2,18},{18,2},{3,19},{19,3},{4,20},{20... | collective-permute-start | bytes 958472 | tf_op jit(solution)/shard_map/ppermute | solution.py:48
  68.1 11.6 %collective-permute-start.12 = (bf16[768,256]{1,0:T(8,128)(2,1)S(1)}, bf16[768,256]{1,0:T(8,128)(2,1)S(1)}, u32[]{:S(2)}, u32[]{:S(2)}) collective-permute-start(bf16[768,256]{1,0:T(8,128)(2,1)S(1)} %add_convert_fusion.2.own), channel_id=1, source_target_pairs={{0,2},{1,3},{2,0},{3,1},{4,6},{5,7},{6,4},{7,5},{8,10},{9,11},{10,... | collective-permute-start | bytes 1179656 | tf_op jit(solution)/shard_map/ppermute | solution.py:48
  89.2 11.2 %collective-permute-start.18 = (bf16[768,256]{1,0:T(8,128)(2,1)S(1)}, bf16[768,256]{1,0:T(8,128)(2,1)S(1)}, u32[]{:S(2)}, u32[]{:S(2)}) collective-permute-start(bf16[768,256]{1,0:T(8,128)(2,1)S(1)} %add_convert_fusion.1.own), channel_id=1, source_target_pairs={{0,2},{1,3},{2,0},{3,1},{4,6},{5,7},{6,4},{7,5},{8,10},{9,11},{10,... | collective-permute-start | bytes 1179656 | tf_op jit(solution)/shard_map/ppermute | solution.py:48
  112.2 16.1 %collective-permute-start.32 = (bf16[4,96,768]{2,1,0:T(8,128)(2,1)S(1)}, bf16[4,96,768]{2,1,0:T(8,128)(2,1)S(1)}, u32[]{:S(2)}, u32[]{:S(2)}) collective-permute-start(bf16[4,96,768]{2,1,0:T(8,128)(2,1)S(1)} %get-tuple-element.132), channel_id=1, source_target_pairs={{0,16},{16,0},{1,17},{17,1},{2,18},{18,2},{3,19},{19,3},{4,20},{20... | collective-permute-start | bytes 1769480 | tf_op jit(solution)/shard_map/ppermute | solution.py:48
  123.2 20.3 %collective-permute-start.31 = (bf16[4,96,768]{2,1,0:T(8,128)(2,1)S(1)}, bf16[4,96,768]{2,1,0:T(8,128)(2,1)S(1)}, u32[]{:S(2)}, u32[]{:S(2)}) collective-permute-start(bf16[4,96,768]{2,1,0:T(8,128)(2,1)S(1)} %get-tuple-element.138), channel_id=1, source_target_pairs={{0,16},{16,0},{1,17},{17,1},{2,18},{18,2},{3,19},{19,3},{4,20},{20... | collective-permute-start | bytes 1769480 | tf_op jit(solution)/shard_map/ppermute | solution.py:48
  128.5 14.7 %collective-permute-start.33 = (bf16[96,768]{1,0:T(8,128)(2,1)S(1)}, bf16[96,768]{1,0:T(8,128)(2,1)S(1)}, u32[]{:S(2)}, u32[]{:S(2)}) collective-permute-start(bf16[96,768]{1,0:T(8,128)(2,1)S(1)} %get-tuple-element.166), channel_id=1, source_target_pairs={{8,0},{12,4},{0,8},{4,12},{9,1},{13,5},{1,9},{5,13},{10,2},{14,6},... | collective-permute-start | bytes 442376 | tf_op jit(solution)/shard_map/ppermute | solution.py:74
  131.2 12.1 %collective-permute-start.34 = (bf16[96,768]{1,0:T(8,128)(2,1)S(1)}, bf16[96,768]{1,0:T(8,128)(2,1)S(1)}, u32[]{:S(2)}, u32[]{:S(2)}) collective-permute-start(bf16[96,768]{1,0:T(8,128)(2,1)S(1)} %get-tuple-element.167), channel_id=1, source_target_pairs={{12,0},{0,4},{4,8},{8,12},{13,1},{1,5},{5,9},{9,13},{14,2},{2,6},{... | collective-permute-start | bytes 442376 | tf_op jit(solution)/shard_map/ppermute | solution.py:74
  141.6 21.1 %collective-permute-start.30 = (bf16[4,208,384]{2,1,0:T(8,128)(2,1)S(1)}, bf16[4,208,384]{2,1,0:T(8,128)(2,1)S(1)}, u32[]{:S(2)}, u32[]{:S(2)}) collective-permute-start(bf16[4,208,384]{2,1,0:T(8,128)(2,1)S(1)} %get-tuple-element.153), channel_id=1, source_target_pairs={{0,16},{16,0},{1,17},{17,1},{2,18},{18,2},{3,19},{19,3},{4,20},{20... | collective-permute-start | bytes 1916936 | tf_op jit(solution)/shard_map/ppermute | solution.py:48
  144.2 11.8 %collective-permute-start.36 = (bf16[96,768]{1,0:T(8,128)(2,1)}, bf16[96,768]{1,0:T(8,128)(2,1)}, u32[]{:S(2)}, u32[]{:S(2)}) collective-permute-start(bf16[96,768]{1,0:T(8,128)(2,1)} %get-tuple-element.171), channel_id=1, source_target_pairs={{8,0},{12,4},{0,8},{4,12},{9,1},{13,5},{1,9},{5,13},{10,2},{14,6},... | collective-permute-start | bytes 442376 | tf_op jit(solution)/shard_map/ppermute | solution.py:74
  146.3 14.7 %collective-permute-start.37 = (bf16[96,768]{1,0:T(8,128)(2,1)}, bf16[96,768]{1,0:T(8,128)(2,1)}, u32[]{:S(2)}, u32[]{:S(2)}) collective-permute-start(bf16[96,768]{1,0:T(8,128)(2,1)} %get-tuple-element.172), channel_id=1, source_target_pairs={{12,0},{0,4},{4,8},{8,12},{13,1},{1,5},{5,9},{9,13},{14,2},{2,6},{... | collective-permute-start | bytes 442376 | tf_op jit(solution)/shard_map/ppermute | solution.py:74
  146.7 14.3 %collective-permute-start.38 = (bf16[96,768]{1,0:T(8,128)(2,1)}, bf16[96,768]{1,0:T(8,128)(2,1)}, u32[]{:S(2)}, u32[]{:S(2)}) collective-permute-start(bf16[96,768]{1,0:T(8,128)(2,1)} %get-tuple-element.173), channel_id=1, source_target_pairs={{4,0},{8,4},{12,8},{0,12},{5,1},{9,5},{13,9},{1,13},{6,2},{10,6},{... | collective-permute-start | bytes 442376 | tf_op jit(solution)/shard_map/ppermute | solution.py:74
  148.3 14.4 %collective-permute-start.39 = (bf16[96,768]{1,0:T(8,128)(2,1)S(1)}, bf16[96,768]{1,0:T(8,128)(2,1)S(1)}, u32[]{:S(2)}, u32[]{:S(2)}) collective-permute-start(bf16[96,768]{1,0:T(8,128)(2,1)S(1)} %add_convert_fusion.5.b_own), channel_id=1, source_target_pairs={{0,16},{16,0},{1,17},{17,1},{2,18},{18,2},{3,19},{19,3},{4,20},{20... | collective-permute-start | bytes 442376 | tf_op jit(solution)/shard_map/ppermute | solution.py:48
  162.1 25.1 %collective-permute-start.43 = (bf16[96,768]{1,0:T(8,128)(2,1)S(1)}, bf16[96,768]{1,0:T(8,128)(2,1)S(1)}, u32[]{:S(2)}, u32[]{:S(2)}) collective-permute-start(bf16[96,768]{1,0:T(8,128)(2,1)S(1)} %add_convert_fusion.4.i_own), channel_id=1, source_target_pairs={{0,16},{16,0},{1,17},{17,1},{2,18},{18,2},{3,19},{19,3},{4,20},{20... | collective-permute-start | bytes 442376 | tf_op jit(solution)/shard_map/ppermute | solution.py:48
  162.9 12.0 %collective-permute-start.40 = (bf16[208,384]{1,0:T(8,128)(2,1)S(1)}, bf16[208,384]{1,0:T(8,128)(2,1)S(1)}, u32[]{:S(2)}, u32[]{:S(2)}) collective-permute-start(bf16[208,384]{1,0:T(8,128)(2,1)S(1)} %get-tuple-element.176), channel_id=1, source_target_pairs={{8,0},{12,4},{0,8},{4,12},{9,1},{13,5},{1,9},{5,13},{10,2},{14,6},... | collective-permute-start | bytes 479240 | tf_op jit(solution)/shard_map/ppermute | solution.py:74
  163.8 23.2 %collective-permute-start.41 = (bf16[208,384]{1,0:T(8,128)(2,1)S(1)}, bf16[208,384]{1,0:T(8,128)(2,1)S(1)}, u32[]{:S(2)}, u32[]{:S(2)}) collective-permute-start(bf16[208,384]{1,0:T(8,128)(2,1)S(1)} %get-tuple-element.177), channel_id=1, source_target_pairs={{12,0},{0,4},{4,8},{8,12},{13,1},{1,5},{5,9},{9,13},{14,2},{2,6},{... | collective-permute-start | bytes 479240 | tf_op jit(solution)/shard_map/ppermute | solution.py:74
  165.4 21.7 %collective-permute-start.42 = (bf16[208,384]{1,0:T(8,128)(2,1)S(1)}, bf16[208,384]{1,0:T(8,128)(2,1)S(1)}, u32[]{:S(2)}, u32[]{:S(2)}) collective-permute-start(bf16[208,384]{1,0:T(8,128)(2,1)S(1)} %get-tuple-element.178), channel_id=1, source_target_pairs={{4,0},{8,4},{12,8},{0,12},{5,1},{9,5},{13,9},{1,13},{6,2},{10,6},{... | collective-permute-start | bytes 479240 | tf_op jit(solution)/shard_map/ppermute | solution.py:74
  169.2 21.1 %collective-permute-start.27 = (bf16[192,512]{1,0:T(8,128)(2,1)S(1)}, bf16[192,512]{1,0:T(8,128)(2,1)S(1)}, u32[]{:S(2)}, u32[]{:S(2)}) collective-permute-start(bf16[192,512]{1,0:T(8,128)(2,1)S(1)} %pad_maximum_fusion), channel_id=1, source_target_pairs={{0,0},{10,1},{7,2},{13,3},{1,4},{11,5},{4,6},{14,7},{2,8},{8,9},{5... | collective-permute-start | bytes 589832 | tf_op jit(solution)/shard_map/ppermute | solution.py:69
  174.9 15.4 %collective-permute-start.29 = (bf16[192,512]{1,0:T(8,128)(2,1)S(1)}, bf16[192,512]{1,0:T(8,128)(2,1)S(1)}, u32[]{:S(2)}, u32[]{:S(2)}) collective-permute-start(bf16[192,512]{1,0:T(8,128)(2,1)S(1)} %finish.1), channel_id=1, source_target_pairs={{0,0},{10,1},{7,2},{13,3},{1,4},{11,5},{4,6},{14,7},{2,8},{8,9},{5... | collective-permute-start | bytes 589832 | tf_op jit(solution)/shard_map/ppermute | solution.py:69
  (40 other events, 389.2 us)

commit v7 on v6

--- a/solution.py
+++ b/solution.py
@@ -596,7 +596,8 @@
     x1 = swap_bit(x0, "col", 1)
     wide_swapped = [swap_bit(after(part, x2), "dp", 1) for part in wide_fetched]
     g_own = to_slot(after(out_grad.astype(BF16), fetched))
-    ready = (wide_swapped[0], wide_fetched[1], wide_swapped[2], g_own)
+    g_high = swap_bit(g_own, "col", 2)
+    ready = (wide_swapped[0], wide_fetched[1], wide_swapped[2], g_high)
     x3 = swap_bit(after(x2, swapped, *ready), "col", 1)
 
     in_all, back_all, vecs, in_bias = call(
@@ -623,7 +624,7 @@
         [flags, x0, x1, x2, x3, fetched, swapped, vectors],
         specs={k: pl.BlockSpec(memory_space=pl.ANY) for k in range(1, 7)},
         scratch=[pltpu.VMEM((model, slot), BF16), pltpu.SemaphoreType.DMA((12,))],
-        vmem_mib=56,
+        vmem_mib=40,
         weight=0,
     )
 
@@ -638,7 +639,6 @@
         windowed=True,
         weight=0,
     )
-    g_high = swap_bit(after(g_own, scaled_one), "col", 2)
 
     n_away = swap_bit(n_own, "col", 1)
     hidden, slope, mine, other = call(
@@ -650,7 +650,7 @@
     )
     g_pair = swap_bit(g_own, "col", 1)
     g_last = swap_bit(g_high, "col", 1)
-    own = sum_cores(after(mine, g_last), other)
+    own = sum_cores(mine, other)
     away = swap_bit(own, "col", 2)
     out_own, out_give, grad_second, r_own, sums = call(
         turn_kernel,
@@ -748,7 +748,7 @@
         )
         totals += [add_replicas(add_rows(parts), 2)]
     b_back, i_back = (swap_bit(total, "dp", 1) for total in totals)
-    pack_got = after(swap_bit(pack_give, "dp", 1), totals[1], b_back)
+    pack_got = after(swap_bit(pack_give, "dp", 1), b_back)
     w_back_grad, w_in_grad = call(
         wide_unpack_kernel,
         "wide_unpack",

time: 198 us -> 193 us (0.975)
  waiting for transfers between devices: 87.2 us -> 75.2 us
  starting transfers between devices: 44.9 us -> 54.3 us
    ppermute x2, waiting for transfers between devices: 6.86 us -> 0.01 us  [to_slot(): return lax.ppermute(value, ('row', 'col'), grid_pairs())]
    ppermute x2, starting transfers between devices: 4.48 us -> 9.17 us  [from_slot(): lax.ppermute(value, ('row', 'col'), [(b, a) for a, b in grid_pairs()])]
    ppermute x29, starting transfers between devices: 21.9 us -> 26 us  [swap_bit(): return lax.ppermute(value, axis, [(at, at ^ bit) for at in range(size)])]
    ppermute x12, waiting for transfers between devices: 35.7 us -> 32 us  [from_row(): lax.ppermute(value, 'row', [((a + away) % size, a) for a in range(size)])]
  transfers between devices with their start and end apart: 45 -> 45, of which waited for: 22 -> 23; matrix products, arithmetic and copies ran while one was open for 2% -> 2% of each run, Pallas kernels for 10% -> 9%
where the time goes in v7:
time: 193 us; the launch traced here: 189 us
  waiting for transfers between devices  75.2 us (39%)
  starting transfers between devices  54.3 us (28%)
  Pallas kernels  37.6 us (19%)
  blocking collectives  16.9 us (9%)
  other arithmetic  2.45 us (1%)
  local copies, waits for them, and re-layouts  2.02 us (1%)
    ppermute x29, waiting for transfers between devices, swap_bit(): return lax.ppermute(value, axis, [(at, at ^ bit) for at in range(size)])  43.2 us
    pallas_call x19, Pallas kernels, call(): pl.pallas_call(kernel, name=name, out_shape=outs, grid=(1,) if windowed e...  37.6 us
    ppermute x12, waiting for transfers between devices, from_row(): lax.ppermute(value, 'row', [((a + away) % size, a) for a in range(size)])  32 us
    ppermute x29, starting transfers between devices, swap_bit(): return lax.ppermute(value, axis, [(at, at ^ bit) for at in range(size)])  26 us
    all_gather x1, blocking collectives, shards(): fetched = lax.all_gather(after(pack_half, wide), 'row')  16.9 us
    ppermute x12, starting transfers between devices, from_row(): lax.ppermute(value, 'row', [((a + away) % size, a) for a in range(size)])  14.5 us
    ppermute x2, starting transfers between devices, from_slot(): lax.ppermute(value, ('row', 'col'), [(b, a) for a, b in grid_pairs()])  9.17 us
    ppermute x2, starting transfers between devices, to_slot(): return lax.ppermute(value, ('row', 'col'), grid_pairs())  4.66 us
  transfers between devices with their start and end apart: 45, of which 23 were waited for; matrix products, arithmetic and copies ran while one was open for 2% of the time, Pallas kernels for 9%

profile of v7, /device:TPU:20, one launch (start us, length us, event | category | flops | bytes accessed | tf_op | source)
XLA Modules:
  0.0 189.5 jit_solution(1444604072153097498)
XLA Ops:
  0.7 2.1 %collective-permute-start = (bf16[192,512]{1,0:T(8,128)(2,1)}, bf16[192,512]{1,0:T(8,128)(2,1)S(1)}, u32[]{:S(2)}, u32[]{:S(2)}) collective-permute-start(bf16[192,512]{1,0:T(8,128)(2,1)} %param.16), channel_id=1, source_target_pairs={{0,0},{1,10},{2,7},{3,13},{4,1},{5,11},{6,4},{7,14},{8,2},{9,8},{1... | collective-permute-start | bytes 589832 | tf_op jit(solution)/shard_map/ppermute | solution.py:65
  4.7 16.9 %all-gather = bf16[768,384]{1,0:T(8,128)(2,1)S(1)} all-gather(bf16[192,384]{1,0:T(8,128)(2,1)} %get-tuple-element.104), channel_id=2, replica_groups=mesh['dp'=2,'row'=4,'col'=4] {'row'}, dimensions={0}, use_global_device_ids=true | all-gather | bytes 737280 | tf_op jit(solution)/shard_map/all_gather | solution.py:589
  27.3 2.6 %collective-permute-start.9 = (bf16[192,512]{1,0:T(8,128)(2,1)S(1)}, bf16[192,512]{1,0:T(8,128)(2,1)S(1)}, u32[]{:S(2)}, u32[]{:S(2)}) collective-permute-start(bf16[192,512]{1,0:T(8,128)(2,1)S(1)} %convert_element_type.69), channel_id=1, source_target_pairs={{0,0},{1,10},{2,7},{3,13},{4,1},{5,11},{6,4},{7,14},{8,2},{9,8},{1... | collective-permute-start | bytes 589832 | tf_op jit(solution)/shard_map/ppermute | solution.py:65
  29.9 2.6 %collective-permute-done.4.f1 = bf16[208,768]{1,0:T(8,128)(2,1)S(1)} collective-permute-done((bf16[208,768]{1,0:T(8,128)(2,1)}, bf16[208,768]{1,0:T(8,128)(2,1)S(1)}, u32[]{:S(2)}, u32[]{:S(2)}) %collective-permute-start.4) | collective-permute-done | bytes 319520 | tf_op jit(solution)/shard_map/ppermute | solution.py:74
  32.8 9.6 %collective-permute-done.7.f3 = bf16[208,768]{1,0:T(8,128)(2,1)S(1)} collective-permute-done((bf16[208,768]{1,0:T(8,128)(2,1)}, bf16[208,768]{1,0:T(8,128)(2,1)S(1)}, u32[]{:S(2)}, u32[]{:S(2)}) %collective-permute-start.7) | collective-permute-done | bytes 319520 | tf_op jit(solution)/shard_map/ppermute | solution.py:74
  44.4 5.1 %collective-permute-start.10 = (bf16[192,512]{1,0:T(8,128)(2,1)S(1)}, bf16[192,512]{1,0:T(8,128)(2,1)S(1)}, u32[]{:S(2)}, u32[]{:S(2)}) collective-permute-start(bf16[192,512]{1,0:T(8,128)(2,1)S(1)} %collective-permute-done.9.g_own), channel_id=1, source_target_pairs={{0,2},{1,3},{2,0},{3,1},{4,6},{5,7},{6,4},{7,5},{8,10},{9,11},{10,... | collective-permute-start | bytes 589832 | tf_op jit(solution)/shard_map/ppermute | solution.py:48
  49.6 3.9 %collective-permute-done.10.g_high = bf16[192,512]{1,0:T(8,128)(2,1)S(1)} collective-permute-done((bf16[192,512]{1,0:T(8,128)(2,1)S(1)}, bf16[192,512]{1,0:T(8,128)(2,1)S(1)}, u32[]{:S(2)}, u32[]{:S(2)}) %collective-permute-start.10) | collective-permute-done | bytes 196640 | tf_op jit(solution)/shard_map/ppermute | solution.py:48
  53.5 2.6 %collective-permute-start.1 = (bf16[192,512]{1,0:T(8,128)(2,1)S(1)}, bf16[192,512]{1,0:T(8,128)(2,1)S(1)}, u32[]{:S(2)}, u32[]{:S(2)}) collective-permute-start(bf16[192,512]{1,0:T(8,128)(2,1)S(1)} %collective-permute-done.x0), channel_id=1, source_target_pairs={{0,1},{1,0},{2,3},{3,2},{4,5},{5,4},{6,7},{7,6},{8,9},{9,8},{10,11... | collective-permute-start | bytes 589832 | tf_op jit(solution)/shard_map/ppermute | solution.py:48
  57.6 7.6 %attend.1 = (bf16[768,512]{1,0:T(8,128)(2,1)S(1)}, bf16[4,2,192,384]{3,2,1,0:T(8,128)(2,1)S(1)}, bf16[576,512]{1,0:T(8,128)(2,1)S(1)}, bf16[3,512,512]{2,1,0:T(8...) custom-call(s32[6]{0:T(128)S(1)} %stack.24.flags, ...), custom_call_target="tpu_custom_call" | custom-call | tf_op jit(solution)/shard_map/attend/pallas_call | solution.py:27
  70.5 7.8 %collective-permute-done.14.s2 = bf16[208,768]{1,0:T(8,128)(2,1)S(1)} collective-permute-done((bf16[208,768]{1,0:T(8,128)(2,1)S(1)}, bf16[208,768]{1,0:T(8,128)(2,1)S(1)}, u32[]{:S(2)}, u32[]{:S(2)}) %collective-permute-start.14) | collective-permute-done | bytes 319520 | tf_op jit(solution)/shard_map/ppermute | solution.py:48
  88.1 9.1 %collective-permute-done.17.away = bf16[768,256]{1,0:T(8,128)(2,1)S(1)} collective-permute-done((bf16[768,256]{1,0:T(8,128)(2,1)S(1)}, bf16[768,256]{1,0:T(8,128)(2,1)S(1)}, u32[]{:S(2)}, u32[]{:S(2)}) %collective-permute-start.17) | collective-permute-done | bytes 393248 | tf_op jit(solution)/shard_map/ppermute | solution.py:48
  97.2 2.6 %turn.1 = (bf16[192,256]{1,0:T(8,128)(2,1)S(1)}, bf16[192,256]{1,0:T(8,128)(2,1)S(1)}, f32[768,256]{1,0:T(8,128)S(1)}, bf16[768,256]{1,0:T(8,128)(2,1)S(1)}, f32[8,768]{1,0:T(8,128)S(1)}) custom-call(s32[6]{0:T(128)S(1)} %stack.24.flags, f32[768,256]{1,0:T(8,128)S(1)} %get-tuple-element.117.scaled_one.scaled, bf16[768,256]{1,0:T(8,128)(2,1)S(1)} %add_convert_fusion.1.own, ...), custom_call_target="tpu_custom_call" | custom-call | tf_op jit(solution)/shard_map/turn/pallas_call | solution.py:27
  101.5 2.5 %back_grads.1 = (bf16[4,96,768]{2,1,0:T(8,128)(2,1)S(1)}, bf16[4,96,768]{2,1,0:T(8,128)(2,1)S(1)}) custom-call(s32[6]{0:T(128)S(1)} %stack.24.flags, bf16[768,256]{1,0:T(8,128)(2,1)S(1)} %get-tuple-element.125.own.r_own, bf16[768,256]{1,0:T(8,128)(2,1)S(1)} %collective-permute-done.20.away.r_away, bf16[768,512]{1,0:T(8,128)(2,1)S(1)} %get-tuple-element.127.right), custom_call_target="tpu_custom_call" | custom-call | tf_op jit(solution)/shard_map/back_grads/pallas_call | solution.py:27
  109.6 2.5 %into_grads.1 = (bf16[4,96,768]{2,1,0:T(8,128)(2,1)S(1)}, bf16[4,96,768]{2,1,0:T(8,128)(2,1)S(1)}) custom-call(s32[6]{0:T(128)S(1)} %stack.24.flags, bf16[768,256]{1,0:T(8,128)(2,1)S(1)} %get-tuple-element.132.n_own.own, bf16[768,256]{1,0:T(8,128)(2,1)S(1)} %collective-permute-done.15.n_away.away, bf16[768,512]{1,0:T(8,128)(2,1)S(1)} %get-tuple-element.133.right), custom_call_target="tpu_custom_call" | custom-call | tf_op jit(solution)/shard_map/into_grads/pallas_call | solution.py:27
  112.1 6.7 %collective-permute-done.22.away = bf16[768,256]{1,0:T(8,128)(2,1)S(1)} collective-permute-done((bf16[768,256]{1,0:T(8,128)(2,1)S(1)}, bf16[768,256]{1,0:T(8,128)(2,1)S(1)}, u32[]{:S(2)}, u32[]{:S(2)}) %collective-permute-start.22) | collective-permute-done | bytes 393248 | tf_op jit(solution)/shard_map/ppermute | solution.py:48
  123.3 2.4 %collective-permute-start.32 = (bf16[96,768]{1,0:T(8,128)(2,1)S(1)}, bf16[96,768]{1,0:T(8,128)(2,1)S(1)}, u32[]{:S(2)}, u32[]{:S(2)}) collective-permute-start(bf16[96,768]{1,0:T(8,128)(2,1)S(1)} %get-tuple-element.160), channel_id=1, source_target_pairs={{8,0},{12,4},{0,8},{4,12},{9,1},{13,5},{1,9},{5,13},{10,2},{14,6},... | collective-permute-start | bytes 442376 | tf_op jit(solution)/shard_map/ppermute | solution.py:74
  128.4 5.4 %attend_back.1 = (bf16[576,512]{1,0:T(8,128)(2,1)S(1)}, f32[384,512]{1,0:T(8,128)S(1)}, bf16[384,512]{1,0:T(8,128)(2,1)}) custom-call(s32[6]{0:T(128)S(1)} %stack.24.flags, bf16[768,256]{1,0:T(8,128)(2,1)S(1)} %get-tuple-element.139.a_own, bf16[768,256]{1,0:T(8,128)(2,1)S(1)} %collective-permute-done.23.a_away, ...), custom_call_target="tpu_custom_call" | custom-call | tf_op jit(solution)/shard_map/attend_back/pallas_call | solution.py:27
  133.8 2.9 %pack_grads.1 = (bf16[4,208,384]{2,1,0:T(8,128)(2,1)S(1)}, bf16[4,208,384]{2,1,0:T(8,128)(2,1)S(1)}) custom-call(s32[6]{0:T(128)S(1)} %stack.24.flags, bf16[768,512]{1,0:T(8,128)(2,1)S(1)} %get-tuple-element.112.x.xs, bf16[576,512]{1,0:T(8,128)(2,1)S(1)} %get-tuple-element.145.grad_qkv, bf16[768,256]{1,0:T(8,128)(2,1)S(1)} %get-tuple-element.139.a_own, ...), custom_call_target="tpu_custom_call" | custom-call | tf_op jit(solution)/shard_map/pack_grads/pallas_call | solution.py:27
  144.3 7.6 %collective-permute-done.40 = bf16[96,768]{1,0:T(8,128)(2,1)} collective-permute-done((bf16[96,768]{1,0:T(8,128)(2,1)}, bf16[96,768]{1,0:T(8,128)(2,1)}, u32[]{:S(2)}, u32[]{:S(2)}) %collective-permute-start.40) | collective-permute-done | bytes 147488 | tf_op jit(solution)/shard_map/ppermute | solution.py:74
  151.9 3.6 %collective-permute-done.41 = bf16[96,768]{1,0:T(8,128)(2,1)} collective-permute-done((bf16[96,768]{1,0:T(8,128)(2,1)}, bf16[96,768]{1,0:T(8,128)(2,1)}, u32[]{:S(2)}, u32[]{:S(2)}) %collective-permute-start.41) | collective-permute-done | bytes 147488 | tf_op jit(solution)/shard_map/ppermute | solution.py:74
  163.5 2.1 %collective-permute-start.27 = (bf16[192,512]{1,0:T(8,128)(2,1)S(1)}, bf16[192,512]{1,0:T(8,128)(2,1)S(1)}, u32[]{:S(2)}, u32[]{:S(2)}) collective-permute-start(bf16[192,512]{1,0:T(8,128)(2,1)S(1)} %pad_maximum_fusion), channel_id=1, source_target_pairs={{0,0},{10,1},{7,2},{13,3},{1,4},{11,5},{4,6},{14,7},{2,8},{8,9},{5... | collective-permute-start | bytes 589832 | tf_op jit(solution)/shard_map/ppermute | solution.py:69
  166.3 4.0 %collective-permute-done.36 = bf16[208,384]{1,0:T(8,128)(2,1)S(1)} collective-permute-done((bf16[208,384]{1,0:T(8,128)(2,1)S(1)}, bf16[208,384]{1,0:T(8,128)(2,1)S(1)}, u32[]{:S(2)}, u32[]{:S(2)}) %collective-permute-start.36) | collective-permute-done | bytes 159776 | tf_op jit(solution)/shard_map/ppermute | solution.py:74
  170.3 7.1 %collective-permute-start.29 = (bf16[192,512]{1,0:T(8,128)(2,1)S(1)}, bf16[192,512]{1,0:T(8,128)(2,1)S(1)}, u32[]{:S(2)}, u32[]{:S(2)}) collective-permute-start(bf16[192,512]{1,0:T(8,128)(2,1)S(1)} %finish.1), channel_id=1, source_target_pairs={{0,0},{10,1},{7,2},{13,3},{1,4},{11,5},{4,6},{14,7},{2,8},{8,9},{5... | collective-permute-start | bytes 589832 | tf_op jit(solution)/shard_map/ppermute | solution.py:69
  177.4 4.4 %collective-permute-done.37 = bf16[208,384]{1,0:T(8,128)(2,1)S(1)} collective-permute-done((bf16[208,384]{1,0:T(8,128)(2,1)S(1)}, bf16[208,384]{1,0:T(8,128)(2,1)S(1)}, u32[]{:S(2)}, u32[]{:S(2)}) %collective-permute-start.37) | collective-permute-done | bytes 159776 | tf_op jit(solution)/shard_map/ppermute | solution.py:74
  (113 shorter events, 64.7 us)
Async XLA Ops:
  0.7 26.2 %collective-permute-start = (bf16[192,512]{1,0:T(8,128)(2,1)}, bf16[192,512]{1,0:T(8,128)(2,1)S(1)}, u32[]{:S(2)}, u32[]{:S(2)}) collective-permute-start(bf16[192,512]{1,0:T(8,128)(2,1)} %param.16), channel_id=1, source_target_pairs={{0,0},{1,10},{2,7},{3,13},{4,1},{5,11},{6,4},{7,14},{8,2},{9,8},{1... | collective-permute-start | bytes 589832 | tf_op jit(solution)/shard_map/ppermute | solution.py:65
  22.9 19.5 %collective-permute-start.7 = (bf16[208,768]{1,0:T(8,128)(2,1)}, bf16[208,768]{1,0:T(8,128)(2,1)S(1)}, u32[]{:S(2)}, u32[]{:S(2)}) collective-permute-start(bf16[208,768]{1,0:T(8,128)(2,1)} %get-tuple-element.106), channel_id=1, source_target_pairs={{12,0},{0,4},{4,8},{8,12},{13,1},{1,5},{5,9},{9,13},{14,2},{2,6},{... | collective-permute-start | bytes 958472 | tf_op jit(solution)/shard_map/ppermute | solution.py:74
  24.0 32.0 %collective-permute-start.3 = (bf16[4,192,384]{2,1,0:T(8,128)(2,1)S(1)}, bf16[4,192,384]{2,1,0:T(8,128)(2,1)S(1)}, u32[]{:S(2)}, u32[]{:S(2)}) collective-permute-start(bf16[4,192,384]{2,1,0:T(8,128)(2,1)S(1)} %bitcast.12), channel_id=1, source_target_pairs={{0,16},{16,0},{1,17},{17,1},{2,18},{18,2},{3,19},{19,3},{4,20},{20... | collective-permute-start | bytes 1769480 | tf_op jit(solution)/shard_map/ppermute | solution.py:48
  26.8 15.5 %collective-permute-start.2 = (bf16[192,512]{1,0:T(8,128)(2,1)S(1)}, bf16[192,512]{1,0:T(8,128)(2,1)S(1)}, u32[]{:S(2)}, u32[]{:S(2)}) collective-permute-start(bf16[192,512]{1,0:T(8,128)(2,1)S(1)} %collective-permute-done.x0), channel_id=1, source_target_pairs={{0,2},{1,3},{2,0},{3,1},{4,6},{5,7},{6,4},{7,5},{8,10},{9,11},{10,... | collective-permute-start | bytes 589832 | tf_op jit(solution)/shard_map/ppermute | solution.py:48
  27.3 17.1 %collective-permute-start.9 = (bf16[192,512]{1,0:T(8,128)(2,1)S(1)}, bf16[192,512]{1,0:T(8,128)(2,1)S(1)}, u32[]{:S(2)}, u32[]{:S(2)}) collective-permute-start(bf16[192,512]{1,0:T(8,128)(2,1)S(1)} %convert_element_type.69), channel_id=1, source_target_pairs={{0,0},{1,10},{2,7},{3,13},{4,1},{5,11},{6,4},{7,14},{8,2},{9,8},{1... | collective-permute-start | bytes 589832 | tf_op jit(solution)/shard_map/ppermute | solution.py:65
  32.6 23.5 %collective-permute-start.6 = (bf16[208,768]{1,0:T(8,128)(2,1)S(1)}, bf16[208,768]{1,0:T(8,128)(2,1)S(1)}, u32[]{:S(2)}, u32[]{:S(2)}) collective-permute-start(bf16[208,768]{1,0:T(8,128)(2,1)S(1)} %collective-permute-done.4.f1), channel_id=1, source_target_pairs={{4,0},{8,4},{12,8},{0,12},{5,1},{9,5},{13,9},{1,13},{6,2},{10,6},{... | collective-permute-start | bytes 958472 | tf_op jit(solution)/shard_map/ppermute | solution.py:74
  42.4 13.7 %collective-permute-start.8 = (bf16[208,768]{1,0:T(8,128)(2,1)S(1)}, bf16[208,768]{1,0:T(8,128)(2,1)S(1)}, u32[]{:S(2)}, u32[]{:S(2)}) collective-permute-start(bf16[208,768]{1,0:T(8,128)(2,1)S(1)} %collective-permute-done.7.f3), channel_id=1, source_target_pairs={{0,16},{16,0},{1,17},{17,1},{2,18},{18,2},{3,19},{19,3},{4,20},{20... | collective-permute-start | bytes 958472 | tf_op jit(solution)/shard_map/ppermute | solution.py:48
  43.9 12.2 %collective-permute-start.5 = (bf16[208,768]{1,0:T(8,128)(2,1)S(1)}, bf16[208,768]{1,0:T(8,128)(2,1)S(1)}, u32[]{:S(2)}, u32[]{:S(2)}) collective-permute-start(bf16[208,768]{1,0:T(8,128)(2,1)S(1)} %collective-permute-done.4.f1), channel_id=1, source_target_pairs={{0,16},{16,0},{1,17},{17,1},{2,18},{18,2},{3,19},{19,3},{4,20},{20... | collective-permute-start | bytes 958472 | tf_op jit(solution)/shard_map/ppermute | solution.py:48
  67.1 12.8 %collective-permute-start.13 = (bf16[768,256]{1,0:T(8,128)(2,1)S(1)}, bf16[768,256]{1,0:T(8,128)(2,1)S(1)}, u32[]{:S(2)}, u32[]{:S(2)}) collective-permute-start(bf16[768,256]{1,0:T(8,128)(2,1)S(1)} %add_convert_fusion.2.own), channel_id=1, source_target_pairs={{0,2},{1,3},{2,0},{3,1},{4,6},{5,7},{6,4},{7,5},{8,10},{9,11},{10,... | collective-permute-start | bytes 1179656 | tf_op jit(solution)/shard_map/ppermute | solution.py:48
  108.1 15.1 %collective-permute-start.31 = (bf16[4,96,768]{2,1,0:T(8,128)(2,1)S(1)}, bf16[4,96,768]{2,1,0:T(8,128)(2,1)S(1)}, u32[]{:S(2)}, u32[]{:S(2)}) collective-permute-start(bf16[4,96,768]{2,1,0:T(8,128)(2,1)S(1)} %get-tuple-element.128), channel_id=1, source_target_pairs={{0,16},{16,0},{1,17},{17,1},{2,18},{18,2},{3,19},{19,3},{4,20},{20... | collective-permute-start | bytes 1769480 | tf_op jit(solution)/shard_map/ppermute | solution.py:48
  120.0 18.6 %collective-permute-start.39 = (bf16[4,96,768]{2,1,0:T(8,128)(2,1)S(1)}, bf16[4,96,768]{2,1,0:T(8,128)(2,1)S(1)}, u32[]{:S(2)}, u32[]{:S(2)}) collective-permute-start(bf16[4,96,768]{2,1,0:T(8,128)(2,1)S(1)} %get-tuple-element.134), channel_id=1, source_target_pairs={{0,16},{16,0},{1,17},{17,1},{2,18},{18,2},{3,19},{19,3},{4,20},{20... | collective-permute-start | bytes 1769480 | tf_op jit(solution)/shard_map/ppermute | solution.py:48
  123.3 14.9 %collective-permute-start.32 = (bf16[96,768]{1,0:T(8,128)(2,1)S(1)}, bf16[96,768]{1,0:T(8,128)(2,1)S(1)}, u32[]{:S(2)}, u32[]{:S(2)}) collective-permute-start(bf16[96,768]{1,0:T(8,128)(2,1)S(1)} %get-tuple-element.160), channel_id=1, source_target_pairs={{8,0},{12,4},{0,8},{4,12},{9,1},{13,5},{1,9},{5,13},{10,2},{14,6},... | collective-permute-start | bytes 442376 | tf_op jit(solution)/shard_map/ppermute | solution.py:74
  125.7 12.8 %collective-permute-start.33 = (bf16[96,768]{1,0:T(8,128)(2,1)S(1)}, bf16[96,768]{1,0:T(8,128)(2,1)S(1)}, u32[]{:S(2)}, u32[]{:S(2)}) collective-permute-start(bf16[96,768]{1,0:T(8,128)(2,1)S(1)} %get-tuple-element.161), channel_id=1, source_target_pairs={{12,0},{0,4},{4,8},{8,12},{13,1},{1,5},{5,9},{9,13},{14,2},{2,6},{... | collective-permute-start | bytes 442376 | tf_op jit(solution)/shard_map/ppermute | solution.py:74
  136.6 21.9 %collective-permute-start.30 = (bf16[4,208,384]{2,1,0:T(8,128)(2,1)S(1)}, bf16[4,208,384]{2,1,0:T(8,128)(2,1)S(1)}, u32[]{:S(2)}, u32[]{:S(2)}) collective-permute-start(bf16[4,208,384]{2,1,0:T(8,128)(2,1)S(1)} %get-tuple-element.149), channel_id=1, source_target_pairs={{0,16},{16,0},{1,17},{17,1},{2,18},{18,2},{3,19},{19,3},{4,20},{20... | collective-permute-start | bytes 1916936 | tf_op jit(solution)/shard_map/ppermute | solution.py:48
  139.4 12.5 %collective-permute-start.40 = (bf16[96,768]{1,0:T(8,128)(2,1)}, bf16[96,768]{1,0:T(8,128)(2,1)}, u32[]{:S(2)}, u32[]{:S(2)}) collective-permute-start(bf16[96,768]{1,0:T(8,128)(2,1)} %get-tuple-element.172), channel_id=1, source_target_pairs={{8,0},{12,4},{0,8},{4,12},{9,1},{13,5},{1,9},{5,13},{10,2},{14,6},... | collective-permute-start | bytes 442376 | tf_op jit(solution)/shard_map/ppermute | solution.py:74
  141.1 14.4 %collective-permute-start.41 = (bf16[96,768]{1,0:T(8,128)(2,1)}, bf16[96,768]{1,0:T(8,128)(2,1)}, u32[]{:S(2)}, u32[]{:S(2)}) collective-permute-start(bf16[96,768]{1,0:T(8,128)(2,1)} %get-tuple-element.173), channel_id=1, source_target_pairs={{12,0},{0,4},{4,8},{8,12},{13,1},{1,5},{5,9},{9,13},{14,2},{2,6},{... | collective-permute-start | bytes 442376 | tf_op jit(solution)/shard_map/ppermute | solution.py:74
  142.8 12.7 %collective-permute-start.42 = (bf16[96,768]{1,0:T(8,128)(2,1)}, bf16[96,768]{1,0:T(8,128)(2,1)}, u32[]{:S(2)}, u32[]{:S(2)}) collective-permute-start(bf16[96,768]{1,0:T(8,128)(2,1)} %get-tuple-element.174), channel_id=1, source_target_pairs={{4,0},{8,4},{12,8},{0,12},{5,1},{9,5},{13,9},{1,13},{6,2},{10,6},{... | collective-permute-start | bytes 442376 | tf_op jit(solution)/shard_map/ppermute | solution.py:74
  143.1 15.4 %collective-permute-start.35 = (bf16[96,768]{1,0:T(8,128)(2,1)S(1)}, bf16[96,768]{1,0:T(8,128)(2,1)S(1)}, u32[]{:S(2)}, u32[]{:S(2)}) collective-permute-start(bf16[96,768]{1,0:T(8,128)(2,1)S(1)} %add_convert_fusion.5.b_own), channel_id=1, source_target_pairs={{0,16},{16,0},{1,17},{17,1},{2,18},{18,2},{3,19},{19,3},{4,20},{20... | collective-permute-start | bytes 442376 | tf_op jit(solution)/shard_map/ppermute | solution.py:48
  156.6 25.3 %collective-permute-start.43 = (bf16[96,768]{1,0:T(8,128)(2,1)S(1)}, bf16[96,768]{1,0:T(8,128)(2,1)S(1)}, u32[]{:S(2)}, u32[]{:S(2)}) collective-permute-start(bf16[96,768]{1,0:T(8,128)(2,1)S(1)} %add_convert_fusion.4.i_own), channel_id=1, source_target_pairs={{0,16},{16,0},{1,17},{17,1},{2,18},{18,2},{3,19},{19,3},{4,20},{20... | collective-permute-start | bytes 442376 | tf_op jit(solution)/shard_map/ppermute | solution.py:48
  158.7 11.6 %collective-permute-start.36 = (bf16[208,384]{1,0:T(8,128)(2,1)S(1)}, bf16[208,384]{1,0:T(8,128)(2,1)S(1)}, u32[]{:S(2)}, u32[]{:S(2)}) collective-permute-start(bf16[208,384]{1,0:T(8,128)(2,1)S(1)} %get-tuple-element.165), channel_id=1, source_target_pairs={{8,0},{12,4},{0,8},{4,12},{9,1},{13,5},{1,9},{5,13},{10,2},{14,6},... | collective-permute-start | bytes 479240 | tf_op jit(solution)/shard_map/ppermute | solution.py:74
  159.6 22.1 %collective-permute-start.37 = (bf16[208,384]{1,0:T(8,128)(2,1)S(1)}, bf16[208,384]{1,0:T(8,128)(2,1)S(1)}, u32[]{:S(2)}, u32[]{:S(2)}) collective-permute-start(bf16[208,384]{1,0:T(8,128)(2,1)S(1)} %get-tuple-element.166), channel_id=1, source_target_pairs={{12,0},{0,4},{4,8},{8,12},{13,1},{1,5},{5,9},{9,13},{14,2},{2,6},{... | collective-permute-start | bytes 479240 | tf_op jit(solution)/shard_map/ppermute | solution.py:74
  160.8 21.0 %collective-permute-start.38 = (bf16[208,384]{1,0:T(8,128)(2,1)S(1)}, bf16[208,384]{1,0:T(8,128)(2,1)S(1)}, u32[]{:S(2)}, u32[]{:S(2)}) collective-permute-start(bf16[208,384]{1,0:T(8,128)(2,1)S(1)} %get-tuple-element.167), channel_id=1, source_target_pairs={{4,0},{8,4},{12,8},{0,12},{5,1},{9,5},{13,9},{1,13},{6,2},{10,6},{... | collective-permute-start | bytes 479240 | tf_op jit(solution)/shard_map/ppermute | solution.py:74
  163.5 21.5 %collective-permute-start.27 = (bf16[192,512]{1,0:T(8,128)(2,1)S(1)}, bf16[192,512]{1,0:T(8,128)(2,1)S(1)}, u32[]{:S(2)}, u32[]{:S(2)}) collective-permute-start(bf16[192,512]{1,0:T(8,128)(2,1)S(1)} %pad_maximum_fusion), channel_id=1, source_target_pairs={{0,0},{10,1},{7,2},{13,3},{1,4},{11,5},{4,6},{14,7},{2,8},{8,9},{5... | collective-permute-start | bytes 589832 | tf_op jit(solution)/shard_map/ppermute | solution.py:69
  170.3 14.8 %collective-permute-start.29 = (bf16[192,512]{1,0:T(8,128)(2,1)S(1)}, bf16[192,512]{1,0:T(8,128)(2,1)S(1)}, u32[]{:S(2)}, u32[]{:S(2)}) collective-permute-start(bf16[192,512]{1,0:T(8,128)(2,1)S(1)} %finish.1), channel_id=1, source_target_pairs={{0,0},{10,1},{7,2},{13,3},{1,4},{11,5},{4,6},{14,7},{2,8},{8,9},{5... | collective-permute-start | bytes 589832 | tf_op jit(solution)/shard_map/ppermute | solution.py:69
  (28 other events, 264.9 us)

commit v8 on v7

--- a/solution.py
+++ b/solution.py
@@ -122,12 +122,14 @@
 
     for copy in copies:
         copy.start()
-    vectors[...] = jnp.zeros_like(vectors)
     for copy in copies:
         copy.wait()
-    for at in range(8):
-        vectors[at : at + 1, :feats] = lines[at][...].reshape(1, feats)
-    vectors[8:9, :] = long_line[...].reshape(1, long_line.shape[0])
+    units = long_line.shape[0]
+    short = jnp.concatenate([line[...].astype(F32).reshape(1, feats) for line in lines], axis=0)
+    short = jnp.concatenate((short, jnp.zeros((8, units - feats), F32)), axis=1)
+    long = long_line[...].astype(F32).reshape(1, units)
+    long = jnp.concatenate((long, jnp.zeros((7, units), F32)), axis=0)
+    vectors[...] = jnp.concatenate((short, long), axis=0).astype(BF16)
     wide[feats:] = vectors[...]
     pltpu.make_async_copy(w_in, into, sems.at[9]).wait()
     for at in range(2):

time: 193 us -> 193 us (level)
  no operation moved by 1% of the time
where the time goes in v8:
time: 193 us; the launch traced here: 189 us
  waiting for transfers between devices  75.2 us (39%)
  starting transfers between devices  54.3 us (28%)
  Pallas kernels  37.6 us (19%)
  blocking collectives  16.9 us (9%)
  other arithmetic  2.45 us (1%)
  local copies, waits for them, and re-layouts  2.02 us (1%)
    ppermute x29, waiting for transfers between devices, swap_bit(): return lax.ppermute(value, axis, [(at, at ^ bit) for at in range(size)])  43.2 us
    pallas_call x19, Pallas kernels, call(): pl.pallas_call(kernel, name=name, out_shape=outs, grid=(1,) if windowed e...  37.6 us
    ppermute x12, waiting for transfers between devices, from_row(): lax.ppermute(value, 'row', [((a + away) % size, a) for a in range(size)])  32 us
    ppermute x29, starting transfers between devices, swap_bit(): return lax.ppermute(value, axis, [(at, at ^ bit) for at in range(size)])  26 us
    all_gather x1, blocking collectives, shards(): fetched = lax.all_gather(after(pack_half, wide), 'row')  16.9 us
    ppermute x12, starting transfers between devices, from_row(): lax.ppermute(value, 'row', [((a + away) % size, a) for a in range(size)])  14.5 us
    ppermute x2, starting transfers between devices, from_slot(): lax.ppermute(value, ('row', 'col'), [(b, a) for a, b in grid_pairs()])  9.17 us
    ppermute x2, starting transfers between devices, to_slot(): return lax.ppermute(value, ('row', 'col'), grid_pairs())  4.66 us
  transfers between devices with their start and end apart: 45, of which 23 were waited for; matrix products, arithmetic and copies ran while one was open for 2% of the time, Pallas kernels for 9%

profile of v8, /device:TPU:20, one launch (start us, length us, event | category | flops | bytes accessed | tf_op | source)
XLA Modules:
  0.0 189.5 jit_solution(5564122597739558481)
XLA Ops:
  0.7 2.1 %collective-permute-start = (bf16[192,512]{1,0:T(8,128)(2,1)}, bf16[192,512]{1,0:T(8,128)(2,1)S(1)}, u32[]{:S(2)}, u32[]{:S(2)}) collective-permute-start(bf16[192,512]{1,0:T(8,128)(2,1)} %param.16), channel_id=1, source_target_pairs={{0,0},{1,10},{2,7},{3,13},{4,1},{5,11},{6,4},{7,14},{8,2},{9,8},{1... | collective-permute-start | bytes 589832 | tf_op jit(solution)/shard_map/ppermute | solution.py:65
  4.7 16.9 %all-gather = bf16[768,384]{1,0:T(8,128)(2,1)S(1)} all-gather(bf16[192,384]{1,0:T(8,128)(2,1)} %get-tuple-element.104), channel_id=2, replica_groups=mesh['dp'=2,'row'=4,'col'=4] {'row'}, dimensions={0}, use_global_device_ids=true | all-gather | bytes 737280 | tf_op jit(solution)/shard_map/all_gather | solution.py:591
  27.3 2.6 %collective-permute-start.9 = (bf16[192,512]{1,0:T(8,128)(2,1)S(1)}, bf16[192,512]{1,0:T(8,128)(2,1)S(1)}, u32[]{:S(2)}, u32[]{:S(2)}) collective-permute-start(bf16[192,512]{1,0:T(8,128)(2,1)S(1)} %convert_element_type.69), channel_id=1, source_target_pairs={{0,0},{1,10},{2,7},{3,13},{4,1},{5,11},{6,4},{7,14},{8,2},{9,8},{1... | collective-permute-start | bytes 589832 | tf_op jit(solution)/shard_map/ppermute | solution.py:65
  29.9 2.6 %collective-permute-done.4.f1 = bf16[208,768]{1,0:T(8,128)(2,1)S(1)} collective-permute-done((bf16[208,768]{1,0:T(8,128)(2,1)}, bf16[208,768]{1,0:T(8,128)(2,1)S(1)}, u32[]{:S(2)}, u32[]{:S(2)}) %collective-permute-start.4) | collective-permute-done | bytes 319520 | tf_op jit(solution)/shard_map/ppermute | solution.py:74
  32.8 9.6 %collective-permute-done.7.f3 = bf16[208,768]{1,0:T(8,128)(2,1)S(1)} collective-permute-done((bf16[208,768]{1,0:T(8,128)(2,1)}, bf16[208,768]{1,0:T(8,128)(2,1)S(1)}, u32[]{:S(2)}, u32[]{:S(2)}) %collective-permute-start.7) | collective-permute-done | bytes 319520 | tf_op jit(solution)/shard_map/ppermute | solution.py:74
  44.4 5.1 %collective-permute-start.10 = (bf16[192,512]{1,0:T(8,128)(2,1)S(1)}, bf16[192,512]{1,0:T(8,128)(2,1)S(1)}, u32[]{:S(2)}, u32[]{:S(2)}) collective-permute-start(bf16[192,512]{1,0:T(8,128)(2,1)S(1)} %collective-permute-done.9.g_own), channel_id=1, source_target_pairs={{0,2},{1,3},{2,0},{3,1},{4,6},{5,7},{6,4},{7,5},{8,10},{9,11},{10,... | collective-permute-start | bytes 589832 | tf_op jit(solution)/shard_map/ppermute | solution.py:48
  49.6 3.9 %collective-permute-done.10.g_high = bf16[192,512]{1,0:T(8,128)(2,1)S(1)} collective-permute-done((bf16[192,512]{1,0:T(8,128)(2,1)S(1)}, bf16[192,512]{1,0:T(8,128)(2,1)S(1)}, u32[]{:S(2)}, u32[]{:S(2)}) %collective-permute-start.10) | collective-permute-done | bytes 196640 | tf_op jit(solution)/shard_map/ppermute | solution.py:48
  53.5 2.6 %collective-permute-start.1 = (bf16[192,512]{1,0:T(8,128)(2,1)S(1)}, bf16[192,512]{1,0:T(8,128)(2,1)S(1)}, u32[]{:S(2)}, u32[]{:S(2)}) collective-permute-start(bf16[192,512]{1,0:T(8,128)(2,1)S(1)} %collective-permute-done.x0), channel_id=1, source_target_pairs={{0,1},{1,0},{2,3},{3,2},{4,5},{5,4},{6,7},{7,6},{8,9},{9,8},{10,11... | collective-permute-start | bytes 589832 | tf_op jit(solution)/shard_map/ppermute | solution.py:48
  57.6 7.6 %attend.1 = (bf16[768,512]{1,0:T(8,128)(2,1)S(1)}, bf16[4,2,192,384]{3,2,1,0:T(8,128)(2,1)S(1)}, bf16[576,512]{1,0:T(8,128)(2,1)S(1)}, bf16[3,512,512]{2,1,0:T(8...) custom-call(s32[6]{0:T(128)S(1)} %stack.24.flags, ...), custom_call_target="tpu_custom_call" | custom-call | tf_op jit(solution)/shard_map/attend/pallas_call | solution.py:27
  70.5 7.8 %collective-permute-done.14.s2 = bf16[208,768]{1,0:T(8,128)(2,1)S(1)} collective-permute-done((bf16[208,768]{1,0:T(8,128)(2,1)S(1)}, bf16[208,768]{1,0:T(8,128)(2,1)S(1)}, u32[]{:S(2)}, u32[]{:S(2)}) %collective-permute-start.14) | collective-permute-done | bytes 319520 | tf_op jit(solution)/shard_map/ppermute | solution.py:48
  88.1 9.1 %collective-permute-done.17.away = bf16[768,256]{1,0:T(8,128)(2,1)S(1)} collective-permute-done((bf16[768,256]{1,0:T(8,128)(2,1)S(1)}, bf16[768,256]{1,0:T(8,128)(2,1)S(1)}, u32[]{:S(2)}, u32[]{:S(2)}) %collective-permute-start.17) | collective-permute-done | bytes 393248 | tf_op jit(solution)/shard_map/ppermute | solution.py:48
  97.2 2.6 %turn.1 = (bf16[192,256]{1,0:T(8,128)(2,1)S(1)}, bf16[192,256]{1,0:T(8,128)(2,1)S(1)}, f32[768,256]{1,0:T(8,128)S(1)}, bf16[768,256]{1,0:T(8,128)(2,1)S(1)}, f32[8,768]{1,0:T(8,128)S(1)}) custom-call(s32[6]{0:T(128)S(1)} %stack.24.flags, f32[768,256]{1,0:T(8,128)S(1)} %get-tuple-element.117.scaled_one.scaled, bf16[768,256]{1,0:T(8,128)(2,1)S(1)} %add_convert_fusion.1.own, ...), custom_call_target="tpu_custom_call" | custom-call | tf_op jit(solution)/shard_map/turn/pallas_call | solution.py:27
  101.5 2.5 %back_grads.1 = (bf16[4,96,768]{2,1,0:T(8,128)(2,1)S(1)}, bf16[4,96,768]{2,1,0:T(8,128)(2,1)S(1)}) custom-call(s32[6]{0:T(128)S(1)} %stack.24.flags, bf16[768,256]{1,0:T(8,128)(2,1)S(1)} %get-tuple-element.125.own.r_own, bf16[768,256]{1,0:T(8,128)(2,1)S(1)} %collective-permute-done.20.away.r_away, bf16[768,512]{1,0:T(8,128)(2,1)S(1)} %get-tuple-element.127.right), custom_call_target="tpu_custom_call" | custom-call | tf_op jit(solution)/shard_map/back_grads/pallas_call | solution.py:27
  109.6 2.5 %into_grads.1 = (bf16[4,96,768]{2,1,0:T(8,128)(2,1)S(1)}, bf16[4,96,768]{2,1,0:T(8,128)(2,1)S(1)}) custom-call(s32[6]{0:T(128)S(1)} %stack.24.flags, bf16[768,256]{1,0:T(8,128)(2,1)S(1)} %get-tuple-element.132.n_own.own, bf16[768,256]{1,0:T(8,128)(2,1)S(1)} %collective-permute-done.15.n_away.away, bf16[768,512]{1,0:T(8,128)(2,1)S(1)} %get-tuple-element.133.right), custom_call_target="tpu_custom_call" | custom-call | tf_op jit(solution)/shard_map/into_grads/pallas_call | solution.py:27
  112.1 6.7 %collective-permute-done.22.away = bf16[768,256]{1,0:T(8,128)(2,1)S(1)} collective-permute-done((bf16[768,256]{1,0:T(8,128)(2,1)S(1)}, bf16[768,256]{1,0:T(8,128)(2,1)S(1)}, u32[]{:S(2)}, u32[]{:S(2)}) %collective-permute-start.22) | collective-permute-done | bytes 393248 | tf_op jit(solution)/shard_map/ppermute | solution.py:48
  123.3 2.4 %collective-permute-start.32 = (bf16[96,768]{1,0:T(8,128)(2,1)S(1)}, bf16[96,768]{1,0:T(8,128)(2,1)S(1)}, u32[]{:S(2)}, u32[]{:S(2)}) collective-permute-start(bf16[96,768]{1,0:T(8,128)(2,1)S(1)} %get-tuple-element.160), channel_id=1, source_target_pairs={{8,0},{12,4},{0,8},{4,12},{9,1},{13,5},{1,9},{5,13},{10,2},{14,6},... | collective-permute-start | bytes 442376 | tf_op jit(solution)/shard_map/ppermute | solution.py:74
  128.4 5.4 %attend_back.1 = (bf16[576,512]{1,0:T(8,128)(2,1)S(1)}, f32[384,512]{1,0:T(8,128)S(1)}, bf16[384,512]{1,0:T(8,128)(2,1)}) custom-call(s32[6]{0:T(128)S(1)} %stack.24.flags, bf16[768,256]{1,0:T(8,128)(2,1)S(1)} %get-tuple-element.139.a_own, bf16[768,256]{1,0:T(8,128)(2,1)S(1)} %collective-permute-done.23.a_away, ...), custom_call_target="tpu_custom_call" | custom-call | tf_op jit(solution)/shard_map/attend_back/pallas_call | solution.py:27
  133.8 2.9 %pack_grads.1 = (bf16[4,208,384]{2,1,0:T(8,128)(2,1)S(1)}, bf16[4,208,384]{2,1,0:T(8,128)(2,1)S(1)}) custom-call(s32[6]{0:T(128)S(1)} %stack.24.flags, bf16[768,512]{1,0:T(8,128)(2,1)S(1)} %get-tuple-element.112.x.xs, bf16[576,512]{1,0:T(8,128)(2,1)S(1)} %get-tuple-element.145.grad_qkv, bf16[768,256]{1,0:T(8,128)(2,1)S(1)} %get-tuple-element.139.a_own, ...), custom_call_target="tpu_custom_call" | custom-call | tf_op jit(solution)/shard_map/pack_grads/pallas_call | solution.py:27
  144.3 7.6 %collective-permute-done.40 = bf16[96,768]{1,0:T(8,128)(2,1)} collective-permute-done((bf16[96,768]{1,0:T(8,128)(2,1)}, bf16[96,768]{1,0:T(8,128)(2,1)}, u32[]{:S(2)}, u32[]{:S(2)}) %collective-permute-start.40) | collective-permute-done | bytes 147488 | tf_op jit(solution)/shard_map/ppermute | solution.py:74
  151.9 3.6 %collective-permute-done.41 = bf16[96,768]{1,0:T(8,128)(2,1)} collective-permute-done((bf16[96,768]{1,0:T(8,128)(2,1)}, bf16[96,768]{1,0:T(8,128)(2,1)}, u32[]{:S(2)}, u32[]{:S(2)}) %collective-permute-start.41) | collective-permute-done | bytes 147488 | tf_op jit(solution)/shard_map/ppermute | solution.py:74
  163.5 2.1 %collective-permute-start.27 = (bf16[192,512]{1,0:T(8,128)(2,1)S(1)}, bf16[192,512]{1,0:T(8,128)(2,1)S(1)}, u32[]{:S(2)}, u32[]{:S(2)}) collective-permute-start(bf16[192,512]{1,0:T(8,128)(2,1)S(1)} %pad_maximum_fusion), channel_id=1, source_target_pairs={{0,0},{10,1},{7,2},{13,3},{1,4},{11,5},{4,6},{14,7},{2,8},{8,9},{5... | collective-permute-start | bytes 589832 | tf_op jit(solution)/shard_map/ppermute | solution.py:69
  166.3 4.0 %collective-permute-done.36 = bf16[208,384]{1,0:T(8,128)(2,1)S(1)} collective-permute-done((bf16[208,384]{1,0:T(8,128)(2,1)S(1)}, bf16[208,384]{1,0:T(8,128)(2,1)S(1)}, u32[]{:S(2)}, u32[]{:S(2)}) %collective-permute-start.36) | collective-permute-done | bytes 159776 | tf_op jit(solution)/shard_map/ppermute | solution.py:74
  170.3 7.1 %collective-permute-start.29 = (bf16[192,512]{1,0:T(8,128)(2,1)S(1)}, bf16[192,512]{1,0:T(8,128)(2,1)S(1)}, u32[]{:S(2)}, u32[]{:S(2)}) collective-permute-start(bf16[192,512]{1,0:T(8,128)(2,1)S(1)} %finish.1), channel_id=1, source_target_pairs={{0,0},{10,1},{7,2},{13,3},{1,4},{11,5},{4,6},{14,7},{2,8},{8,9},{5... | collective-permute-start | bytes 589832 | tf_op jit(solution)/shard_map/ppermute | solution.py:69
  177.4 4.4 %collective-permute-done.37 = bf16[208,384]{1,0:T(8,128)(2,1)S(1)} collective-permute-done((bf16[208,384]{1,0:T(8,128)(2,1)S(1)}, bf16[208,384]{1,0:T(8,128)(2,1)S(1)}, u32[]{:S(2)}, u32[]{:S(2)}) %collective-permute-start.37) | collective-permute-done | bytes 159776 | tf_op jit(solution)/shard_map/ppermute | solution.py:74
  (113 shorter events, 64.7 us)
Async XLA Ops:
  0.7 26.2 %collective-permute-start = (bf16[192,512]{1,0:T(8,128)(2,1)}, bf16[192,512]{1,0:T(8,128)(2,1)S(1)}, u32[]{:S(2)}, u32[]{:S(2)}) collective-permute-start(bf16[192,512]{1,0:T(8,128)(2,1)} %param.16), channel_id=1, source_target_pairs={{0,0},{1,10},{2,7},{3,13},{4,1},{5,11},{6,4},{7,14},{8,2},{9,8},{1... | collective-permute-start | bytes 589832 | tf_op jit(solution)/shard_map/ppermute | solution.py:65
  22.9 19.5 %collective-permute-start.7 = (bf16[208,768]{1,0:T(8,128)(2,1)}, bf16[208,768]{1,0:T(8,128)(2,1)S(1)}, u32[]{:S(2)}, u32[]{:S(2)}) collective-permute-start(bf16[208,768]{1,0:T(8,128)(2,1)} %get-tuple-element.106), channel_id=1, source_target_pairs={{12,0},{0,4},{4,8},{8,12},{13,1},{1,5},{5,9},{9,13},{14,2},{2,6},{... | collective-permute-start | bytes 958472 | tf_op jit(solution)/shard_map/ppermute | solution.py:74
  24.0 32.0 %collective-permute-start.3 = (bf16[4,192,384]{2,1,0:T(8,128)(2,1)S(1)}, bf16[4,192,384]{2,1,0:T(8,128)(2,1)S(1)}, u32[]{:S(2)}, u32[]{:S(2)}) collective-permute-start(bf16[4,192,384]{2,1,0:T(8,128)(2,1)S(1)} %bitcast.12), channel_id=1, source_target_pairs={{0,16},{16,0},{1,17},{17,1},{2,18},{18,2},{3,19},{19,3},{4,20},{20... | collective-permute-start | bytes 1769480 | tf_op jit(solution)/shard_map/ppermute | solution.py:48
  26.8 15.5 %collective-permute-start.2 = (bf16[192,512]{1,0:T(8,128)(2,1)S(1)}, bf16[192,512]{1,0:T(8,128)(2,1)S(1)}, u32[]{:S(2)}, u32[]{:S(2)}) collective-permute-start(bf16[192,512]{1,0:T(8,128)(2,1)S(1)} %collective-permute-done.x0), channel_id=1, source_target_pairs={{0,2},{1,3},{2,0},{3,1},{4,6},{5,7},{6,4},{7,5},{8,10},{9,11},{10,... | collective-permute-start | bytes 589832 | tf_op jit(solution)/shard_map/ppermute | solution.py:48
  27.3 17.1 %collective-permute-start.9 = (bf16[192,512]{1,0:T(8,128)(2,1)S(1)}, bf16[192,512]{1,0:T(8,128)(2,1)S(1)}, u32[]{:S(2)}, u32[]{:S(2)}) collective-permute-start(bf16[192,512]{1,0:T(8,128)(2,1)S(1)} %convert_element_type.69), channel_id=1, source_target_pairs={{0,0},{1,10},{2,7},{3,13},{4,1},{5,11},{6,4},{7,14},{8,2},{9,8},{1... | collective-permute-start | bytes 589832 | tf_op jit(solution)/shard_map/ppermute | solution.py:65
  32.6 23.5 %collective-permute-start.6 = (bf16[208,768]{1,0:T(8,128)(2,1)S(1)}, bf16[208,768]{1,0:T(8,128)(2,1)S(1)}, u32[]{:S(2)}, u32[]{:S(2)}) collective-permute-start(bf16[208,768]{1,0:T(8,128)(2,1)S(1)} %collective-permute-done.4.f1), channel_id=1, source_target_pairs={{4,0},{8,4},{12,8},{0,12},{5,1},{9,5},{13,9},{1,13},{6,2},{10,6},{... | collective-permute-start | bytes 958472 | tf_op jit(solution)/shard_map/ppermute | solution.py:74
  42.4 13.7 %collective-permute-start.8 = (bf16[208,768]{1,0:T(8,128)(2,1)S(1)}, bf16[208,768]{1,0:T(8,128)(2,1)S(1)}, u32[]{:S(2)}, u32[]{:S(2)}) collective-permute-start(bf16[208,768]{1,0:T(8,128)(2,1)S(1)} %collective-permute-done.7.f3), channel_id=1, source_target_pairs={{0,16},{16,0},{1,17},{17,1},{2,18},{18,2},{3,19},{19,3},{4,20},{20... | collective-permute-start | bytes 958472 | tf_op jit(solution)/shard_map/ppermute | solution.py:48
  43.9 12.2 %collective-permute-start.5 = (bf16[208,768]{1,0:T(8,128)(2,1)S(1)}, bf16[208,768]{1,0:T(8,128)(2,1)S(1)}, u32[]{:S(2)}, u32[]{:S(2)}) collective-permute-start(bf16[208,768]{1,0:T(8,128)(2,1)S(1)} %collective-permute-done.4.f1), channel_id=1, source_target_pairs={{0,16},{16,0},{1,17},{17,1},{2,18},{18,2},{3,19},{19,3},{4,20},{20... | collective-permute-start | bytes 958472 | tf_op jit(solution)/shard_map/ppermute | solution.py:48
  67.1 12.8 %collective-permute-start.13 = (bf16[768,256]{1,0:T(8,128)(2,1)S(1)}, bf16[768,256]{1,0:T(8,128)(2,1)S(1)}, u32[]{:S(2)}, u32[]{:S(2)}) collective-permute-start(bf16[768,256]{1,0:T(8,128)(2,1)S(1)} %add_convert_fusion.2.own), channel_id=1, source_target_pairs={{0,2},{1,3},{2,0},{3,1},{4,6},{5,7},{6,4},{7,5},{8,10},{9,11},{10,... | collective-permute-start | bytes 1179656 | tf_op jit(solution)/shard_map/ppermute | solution.py:48
  108.1 15.1 %collective-permute-start.31 = (bf16[4,96,768]{2,1,0:T(8,128)(2,1)S(1)}, bf16[4,96,768]{2,1,0:T(8,128)(2,1)S(1)}, u32[]{:S(2)}, u32[]{:S(2)}) collective-permute-start(bf16[4,96,768]{2,1,0:T(8,128)(2,1)S(1)} %get-tuple-element.128), channel_id=1, source_target_pairs={{0,16},{16,0},{1,17},{17,1},{2,18},{18,2},{3,19},{19,3},{4,20},{20... | collective-permute-start | bytes 1769480 | tf_op jit(solution)/shard_map/ppermute | solution.py:48
  120.0 18.6 %collective-permute-start.39 = (bf16[4,96,768]{2,1,0:T(8,128)(2,1)S(1)}, bf16[4,96,768]{2,1,0:T(8,128)(2,1)S(1)}, u32[]{:S(2)}, u32[]{:S(2)}) collective-permute-start(bf16[4,96,768]{2,1,0:T(8,128)(2,1)S(1)} %get-tuple-element.134), channel_id=1, source_target_pairs={{0,16},{16,0},{1,17},{17,1},{2,18},{18,2},{3,19},{19,3},{4,20},{20... | collective-permute-start | bytes 1769480 | tf_op jit(solution)/shard_map/ppermute | solution.py:48
  123.3 14.9 %collective-permute-start.32 = (bf16[96,768]{1,0:T(8,128)(2,1)S(1)}, bf16[96,768]{1,0:T(8,128)(2,1)S(1)}, u32[]{:S(2)}, u32[]{:S(2)}) collective-permute-start(bf16[96,768]{1,0:T(8,128)(2,1)S(1)} %get-tuple-element.160), channel_id=1, source_target_pairs={{8,0},{12,4},{0,8},{4,12},{9,1},{13,5},{1,9},{5,13},{10,2},{14,6},... | collective-permute-start | bytes 442376 | tf_op jit(solution)/shard_map/ppermute | solution.py:74
  125.7 12.8 %collective-permute-start.33 = (bf16[96,768]{1,0:T(8,128)(2,1)S(1)}, bf16[96,768]{1,0:T(8,128)(2,1)S(1)}, u32[]{:S(2)}, u32[]{:S(2)}) collective-permute-start(bf16[96,768]{1,0:T(8,128)(2,1)S(1)} %get-tuple-element.161), channel_id=1, source_target_pairs={{12,0},{0,4},{4,8},{8,12},{13,1},{1,5},{5,9},{9,13},{14,2},{2,6},{... | collective-permute-start | bytes 442376 | tf_op jit(solution)/shard_map/ppermute | solution.py:74
  136.6 21.9 %collective-permute-start.30 = (bf16[4,208,384]{2,1,0:T(8,128)(2,1)S(1)}, bf16[4,208,384]{2,1,0:T(8,128)(2,1)S(1)}, u32[]{:S(2)}, u32[]{:S(2)}) collective-permute-start(bf16[4,208,384]{2,1,0:T(8,128)(2,1)S(1)} %get-tuple-element.149), channel_id=1, source_target_pairs={{0,16},{16,0},{1,17},{17,1},{2,18},{18,2},{3,19},{19,3},{4,20},{20... | collective-permute-start | bytes 1916936 | tf_op jit(solution)/shard_map/ppermute | solution.py:48
  139.4 12.5 %collective-permute-start.40 = (bf16[96,768]{1,0:T(8,128)(2,1)}, bf16[96,768]{1,0:T(8,128)(2,1)}, u32[]{:S(2)}, u32[]{:S(2)}) collective-permute-start(bf16[96,768]{1,0:T(8,128)(2,1)} %get-tuple-element.172), channel_id=1, source_target_pairs={{8,0},{12,4},{0,8},{4,12},{9,1},{13,5},{1,9},{5,13},{10,2},{14,6},... | collective-permute-start | bytes 442376 | tf_op jit(solution)/shard_map/ppermute | solution.py:74
  141.1 14.4 %collective-permute-start.41 = (bf16[96,768]{1,0:T(8,128)(2,1)}, bf16[96,768]{1,0:T(8,128)(2,1)}, u32[]{:S(2)}, u32[]{:S(2)}) collective-permute-start(bf16[96,768]{1,0:T(8,128)(2,1)} %get-tuple-element.173), channel_id=1, source_target_pairs={{12,0},{0,4},{4,8},{8,12},{13,1},{1,5},{5,9},{9,13},{14,2},{2,6},{... | collective-permute-start | bytes 442376 | tf_op jit(solution)/shard_map/ppermute | solution.py:74
  142.8 12.7 %collective-permute-start.42 = (bf16[96,768]{1,0:T(8,128)(2,1)}, bf16[96,768]{1,0:T(8,128)(2,1)}, u32[]{:S(2)}, u32[]{:S(2)}) collective-permute-start(bf16[96,768]{1,0:T(8,128)(2,1)} %get-tuple-element.174), channel_id=1, source_target_pairs={{4,0},{8,4},{12,8},{0,12},{5,1},{9,5},{13,9},{1,13},{6,2},{10,6},{... | collective-permute-start | bytes 442376 | tf_op jit(solution)/shard_map/ppermute | solution.py:74
  143.1 15.4 %collective-permute-start.35 = (bf16[96,768]{1,0:T(8,128)(2,1)S(1)}, bf16[96,768]{1,0:T(8,128)(2,1)S(1)}, u32[]{:S(2)}, u32[]{:S(2)}) collective-permute-start(bf16[96,768]{1,0:T(8,128)(2,1)S(1)} %add_convert_fusion.5.b_own), channel_id=1, source_target_pairs={{0,16},{16,0},{1,17},{17,1},{2,18},{18,2},{3,19},{19,3},{4,20},{20... | collective-permute-start | bytes 442376 | tf_op jit(solution)/shard_map/ppermute | solution.py:48
  156.6 25.3 %collective-permute-start.43 = (bf16[96,768]{1,0:T(8,128)(2,1)S(1)}, bf16[96,768]{1,0:T(8,128)(2,1)S(1)}, u32[]{:S(2)}, u32[]{:S(2)}) collective-permute-start(bf16[96,768]{1,0:T(8,128)(2,1)S(1)} %add_convert_fusion.4.i_own), channel_id=1, source_target_pairs={{0,16},{16,0},{1,17},{17,1},{2,18},{18,2},{3,19},{19,3},{4,20},{20... | collective-permute-start | bytes 442376 | tf_op jit(solution)/shard_map/ppermute | solution.py:48
  158.7 11.6 %collective-permute-start.36 = (bf16[208,384]{1,0:T(8,128)(2,1)S(1)}, bf16[208,384]{1,0:T(8,128)(2,1)S(1)}, u32[]{:S(2)}, u32[]{:S(2)}) collective-permute-start(bf16[208,384]{1,0:T(8,128)(2,1)S(1)} %get-tuple-element.165), channel_id=1, source_target_pairs={{8,0},{12,4},{0,8},{4,12},{9,1},{13,5},{1,9},{5,13},{10,2},{14,6},... | collective-permute-start | bytes 479240 | tf_op jit(solution)/shard_map/ppermute | solution.py:74
  159.6 22.1 %collective-permute-start.37 = (bf16[208,384]{1,0:T(8,128)(2,1)S(1)}, bf16[208,384]{1,0:T(8,128)(2,1)S(1)}, u32[]{:S(2)}, u32[]{:S(2)}) collective-permute-start(bf16[208,384]{1,0:T(8,128)(2,1)S(1)} %get-tuple-element.166), channel_id=1, source_target_pairs={{12,0},{0,4},{4,8},{8,12},{13,1},{1,5},{5,9},{9,13},{14,2},{2,6},{... | collective-permute-start | bytes 479240 | tf_op jit(solution)/shard_map/ppermute | solution.py:74
  160.8 21.0 %collective-permute-start.38 = (bf16[208,384]{1,0:T(8,128)(2,1)S(1)}, bf16[208,384]{1,0:T(8,128)(2,1)S(1)}, u32[]{:S(2)}, u32[]{:S(2)}) collective-permute-start(bf16[208,384]{1,0:T(8,128)(2,1)S(1)} %get-tuple-element.167), channel_id=1, source_target_pairs={{4,0},{8,4},{12,8},{0,12},{5,1},{9,5},{13,9},{1,13},{6,2},{10,6},{... | collective-permute-start | bytes 479240 | tf_op jit(solution)/shard_map/ppermute | solution.py:74
  163.5 21.5 %collective-permute-start.27 = (bf16[192,512]{1,0:T(8,128)(2,1)S(1)}, bf16[192,512]{1,0:T(8,128)(2,1)S(1)}, u32[]{:S(2)}, u32[]{:S(2)}) collective-permute-start(bf16[192,512]{1,0:T(8,128)(2,1)S(1)} %pad_maximum_fusion), channel_id=1, source_target_pairs={{0,0},{10,1},{7,2},{13,3},{1,4},{11,5},{4,6},{14,7},{2,8},{8,9},{5... | collective-permute-start | bytes 589832 | tf_op jit(solution)/shard_map/ppermute | solution.py:69
  170.3 14.8 %collective-permute-start.29 = (bf16[192,512]{1,0:T(8,128)(2,1)S(1)}, bf16[192,512]{1,0:T(8,128)(2,1)S(1)}, u32[]{:S(2)}, u32[]{:S(2)}) collective-permute-start(bf16[192,512]{1,0:T(8,128)(2,1)S(1)} %finish.1), channel_id=1, source_target_pairs={{0,0},{10,1},{7,2},{13,3},{1,4},{11,5},{4,6},{14,7},{2,8},{8,9},{5... | collective-permute-start | bytes 589832 | tf_op jit(solution)/shard_map/ppermute | solution.py:69
  (28 other events, 264.9 us)
